TPU v7x, 256 devices: a whole 4x4x8 slice. The times are simulated.
256 devices in a mesh: gas: 16 (over z_hi, y), space: 16 (over x, z_lo, core).
Axes of the slice: x: 4, y: 4, z: 8 (z_hi: 4, z_lo: 2; z = z_hi * 2 + z_lo), core: 2. Of those that a mesh axis runs over, the one named last changes fastest.
Arguments:
- starting_kelvin_blocks: float32 [16, 2, 128, 128], P('space'), may hold values from 0.8 to 1.6
- volume_thermal_inertia: float32 [16, 2, 128, 128], P('space'), may hold values from 0.5 to 5
- volume_combustion_source: float32 [16, 2, 128, 128], P('space'), may hold values from 0.3 to 5
- extinction_coefficients: float32 [32, 16, 2, 128, 128], P('gas', 'space'), may hold values from 0.01 to 10, as said below
- blackbody_fractions: float32 [32, 16, 2, 128, 128], P('gas', 'space'), may hold values from 0.005 to 0.1
- earlier_irradiance: float32 [32, 16, 2, 128, 128], P('gas', 'space'), may hold values from 0.02 to 1
Outputs:
- final_temperature: float32 [16, 2, 128, 128], P('space')
- radiation: float32 [32, 16, 2, 128, 128], P('gas', 'space')
Inputs may be any that keep to these rules, and one draw needn't show every extreme that they name: `extinction_coefficients`: gas g has a base rate 0.02 * 250^(g / 31), times a factor between 0.5 and 2 in each cell.
All inputs are finite; a program needn't handle non-finite values.
Results may differ from a plain program's by a relative error of at most 0.0001.
Values sent between devices are 32-bit elements; how exact they have to be, the bound alone decides.
No kernel may reach another device: no remote copies, remote signals or barrier semaphores. Data moves between devices by JAX's collectives and lax.ppermute only.
A program may use at most 64 MiB of HBM per device.

v0:
```python
import jax
import jax.numpy as jnp
from jax import lax
from jax.sharding import PartitionSpec as P

SWEEPS = 8
OUTER = 3


LOW_BOUND = 0.05
HIGH_BOUND = 2.0


def from_behind(array, axis, by):
    devices = lax.axis_size(axis)
    pairs = [(i, i + by) for i in range(devices) if 0 <= i + by < devices]
    return lax.ppermute(array, axis, pairs)


def sweep_factors(count):
    theta_mid = (HIGH_BOUND + LOW_BOUND) / 2.0
    delta_half = (HIGH_BOUND - LOW_BOUND) / 2.0
    sigma_ratio = theta_mid / delta_half
    rho_now = 1.0 / sigma_ratio
    factors = []
    for sweep_num in range(count):
        rho_next = 1.0 / (2.0 * sigma_ratio - rho_now)
        factors.append((rho_next * rho_now, 2.0 * rho_next / delta_half))
        rho_now = rho_next
    return (theta_mid, factors)


def tile_layout():
    tiles_y = min(lax.axis_size("space"), 4)
    tiles_x = lax.axis_size("space") // tiles_y
    place = lax.axis_index("space")
    return (tiles_x, tiles_y, place // tiles_y, place % tiles_y)


def shared_neighbours(field):
    tiles_x, tiles_y, tile_row, column = tile_layout()
    zero_layer = jnp.zeros_like(field[:, :1])
    below_z = jnp.concatenate([zero_layer, field[:, :-1]], 1)
    above_z = jnp.concatenate([field[:, 1:], zero_layer], 1)
    lower_part = from_behind(field[:, :, -1:, :], "space", tiles_y)
    upper_part = from_behind(field[:, :, :1, :], "space", -tiles_y)
    below_x = jnp.concatenate([lower_part, field[:, :, :-1, :]], 2)
    above_x = jnp.concatenate([field[:, :, 1:, :], upper_part], 2)
    left_part = from_behind(field[..., -1:], "space", 1)
    right_part = from_behind(field[..., :1], "space", -1)
    left_col = jnp.where(column == 0, 0.0, left_part)
    right_col = jnp.where(column == tiles_y - 1, 0.0, right_part)
    below_y = jnp.concatenate([left_col, field[..., :-1]], 3)
    above_y = jnp.concatenate([field[..., 1:], right_col], 3)
    return [below_z, above_z, below_x, above_x, below_y, above_y]


def coefficients(absorb, own_absorb, near):
    couplings = [2.0 / (3.0 * (own_absorb + other)) for other in near(absorb)]
    diagonal = own_absorb
    for coupling in couplings:
        diagonal = diagonal + coupling
    return (couplings, diagonal)


def operate(field, couplings, diagonal, near):
    total = diagonal * field
    for coupling, other in zip(couplings, near(field)):
        total = total - coupling * other
    return total


def solve_gases(source, start, couplings, diagonal, near, keep):
    theta_mid, factors = sweep_factors(SWEEPS - 1)
    iterate = start
    scaled_res = keep * ((source - operate(iterate, couplings, diagonal, near)) / diagonal)
    direction = scaled_res / theta_mid
    for sweep_num in range(SWEEPS):
        iterate = iterate + direction
        if sweep_num < SWEEPS - 1:
            scaled_res = keep * (
                scaled_res - operate(direction, couplings, diagonal, near) / diagonal
            )
            keep_part, push_part = factors[sweep_num]
            direction = keep_part * direction + push_part * scaled_res
    return iterate


def linearized_correction(
    current_kelvin, earlier_kelvin, thermal_inertia, combustion_source, emitted_power, taken_energy
):
    balance_mismatch = (
        thermal_inertia * (current_kelvin - earlier_kelvin)
        + 4.0 * emitted_power * current_kelvin**4
        - taken_energy
        - combustion_source
    )
    return current_kelvin - balance_mismatch / (
        thermal_inertia + 16.0 * emitted_power * current_kelvin**3
    )


def on_device(
    starting_kelvin_blocks,
    volume_thermal_inertia,
    volume_combustion_source,
    extinction_coefficients,
    blackbody_fractions,
    earlier_irradiance,
):
    absorb = extinction_coefficients[:, 0]
    weight = blackbody_fractions[:, 0]
    iterate = earlier_irradiance[:, 0]
    earlier_kelvin = starting_kelvin_blocks[0]
    thermal_inertia = volume_thermal_inertia[0]
    combustion_source = volume_combustion_source[0]
    couplings, diagonal = coefficients(absorb, absorb, shared_neighbours)
    emission_part = jnp.sum(absorb * weight, axis=0)
    emitted_power = lax.psum(emission_part, "gas")
    current_kelvin = earlier_kelvin
    for outer_step in range(OUTER):
        source = 4.0 * absorb * weight * (current_kelvin**4)[None]
        iterate = solve_gases(source, iterate, couplings, diagonal, shared_neighbours, 1.0)
        absorbed_part = jnp.sum(absorb * iterate, axis=0)
        taken_energy = lax.psum(absorbed_part, "gas")
        current_kelvin = linearized_correction(
            current_kelvin,
            earlier_kelvin,
            thermal_inertia,
            combustion_source,
            emitted_power,
            taken_energy,
        )
    return (current_kelvin[None], iterate[:, None])


def solution(mesh):
    placed = (
        P("space", None, None, None),
        P("space", None, None, None),
        P("space", None, None, None),
        P("gas", "space", None, None, None),
        P("gas", "space", None, None, None),
        P("gas", "space", None, None, None),
    )
    return jax.shard_map(
        on_device,
        mesh=mesh,
        in_specs=placed,
        out_specs=(P("space", None, None, None), P("gas", "space", None, None, None)),
        check_vma=False,
    )
```

profile of v0, /device:TPU:38, one launch (start us, length us, event | category | flops | bytes accessed | tf_op | source)
XLA Modules:
  0.0 933.4 jit_solution(12820303591901426632)
XLA Ops:
  9.8 4.5 collective-permute-start.1
  17.0 4.7 collective-permute-start.5
  32.5 5.7 collective-permute-done.2
  56.1 7.1 collective-permute-start.9
  65.2 3.8 collective-permute-done.11
  73.1 6.8 collective-permute-start.13
  81.9 3.8 collective-permute-done.15
  89.8 6.8 collective-permute-start.17
  98.6 3.8 collective-permute-done.19
  106.5 6.8 collective-permute-start.21
  115.3 3.8 collective-permute-done.23
  123.2 6.8 collective-permute-start.25
  132.0 3.8 collective-permute-done.27
  139.9 6.8 collective-permute-start.29
  148.7 3.8 collective-permute-done.31
  156.6 6.8 collective-permute-start.33
  165.4 3.8 collective-permute-done.35
  175.6 6.8 collective-permute-start.37
  189.1 164.2 %all-reduce.59.cloned.1.call-done = (f32[2,128,128]{2,1,0:T(8,128)}, f32[2,128,128]{2,1,0:T(8,128)}) async-done(((f32[2,128,128]{2,1,0:T(8,128)}, f32[2,128,128]{2,1,0:T(8,128)}), (f32[2,128,128]{2,1,0:T(8,128)}, f32[2,128,128]{2,1,0:T(8,128)})) %all-reduce.59.cloned.1.call-update) | async-done | bytes 262160 | tf_op jit(solution)/shard_map/psum | solution.py:119
  358.7 4.5 collective-permute-start.41
  374.3 6.5 collective-permute-start.45
  382.8 3.8 collective-permute-done.47
  390.7 6.8 collective-permute-start.49
  399.5 3.8 collective-permute-done.51
  407.4 6.8 collective-permute-start.53
  416.2 3.8 collective-permute-done.55
  424.1 6.8 collective-permute-start.57
  432.9 3.8 collective-permute-done.59
  440.8 6.8 collective-permute-start.61
  449.6 3.8 collective-permute-done.63
  457.5 6.8 collective-permute-start.65
  466.3 3.8 collective-permute-done.67
  477.2 6.8 collective-permute-start.69
  486.0 3.9 collective-permute-done.71
  489.9 150.9 %all-reduce.55.cloned.1.call-done = f32[2,128,128]{2,1,0:T(8,128)} async-done(((f32[2,128,128]{2,1,0:T(8,128)}), f32[2,128,128]{2,1,0:T(8,128)}) %all-reduce.55.cloned.1.call-update) | async-done | bytes 131088 | tf_op jit(solution)/shard_map/psum | solution.py:125
  647.0 4.5 collective-permute-start.73
  654.7 3.8 collective-permute-done.75
  662.6 6.5 collective-permute-start.77
  671.1 3.8 collective-permute-done.79
  679.1 6.8 collective-permute-start.81
  687.8 3.8 collective-permute-done.83
  696.0 6.8 collective-permute-start.85
  704.8 3.8 collective-permute-done.87
  712.7 6.8 collective-permute-start.89
  721.5 3.8 collective-permute-done.91
  729.4 6.8 collective-permute-start.93
  746.1 6.8 collective-permute-start.97
  760.8 164.4 %all-reduce.57.cloned.1.call-done = f32[2,128,128]{2,1,0:T(8,128)} async-done(((f32[2,128,128]{2,1,0:T(8,128)}), f32[2,128,128]{2,1,0:T(8,128)}) %all-reduce.57.cloned.1.call-update) | async-done | bytes 131088 | tf_op jit(solution)/shard_map/psum | solution.py:125
  (403 shorter events, 198.3 us)
Async XLA Ops:
  7.2 346.2 %all-reduce.59.cloned.1.call-start = ((), (), s32[]{:S(2)}) async-start(), calls=%async_computation.2 | async-start | bytes 524288 | tf_op jit(solution)/shard_map/psum | solution.py:119
  8.5 43.2 %collective-permute-start = (f32[2,2,1,128]{3,2,1,0:T(1,128)}, f32[2,2,1,128]{3,2,1,0:T(1,128)S(1)}, u32[]{:S(2)}, u32[]{:S(2)}) collective-permute-start(f32[2,2,1,128]{3,2,1,0:T(1,128)} %get-tuple-element.287), channel_id=1, source_target_pairs={{0,4},{1,5},{2,6},{3,7},{4,8},{5,9},{6,10},{7,11},{8,12},{9,13},{1... | collective-permute-start | bytes 6152 | tf_op jit(solution)/shard_map/ppermute | solution.py:17
  9.8 41.9 %collective-permute-start.1 = (f32[2,2,1,128]{3,2,1,0:T(1,128)}, f32[2,2,1,128]{3,2,1,0:T(1,128)S(1)}, u32[]{:S(2)}, u32[]{:S(2)}) collective-permute-start(f32[2,2,1,128]{3,2,1,0:T(1,128)} %get-tuple-element.288), channel_id=1, source_target_pairs={{4,0},{5,1},{6,2},{7,3},{8,4},{9,5},{10,6},{11,7},{12,8},{13,9},{1... | collective-permute-start | bytes 6152 | tf_op jit(solution)/shard_map/ppermute | solution.py:17
  15.7 36.0 %collective-permute-start.4 = (f32[2,2,1,128]{3,2,1,0:T(1,128)}, f32[2,2,1,128]{3,2,1,0:T(1,128)S(1)}, u32[]{:S(2)}, u32[]{:S(2)}) collective-permute-start(f32[2,2,1,128]{3,2,1,0:T(1,128)} %get-tuple-element.299), channel_id=1, source_target_pairs={{0,4},{1,5},{2,6},{3,7},{4,8},{5,9},{6,10},{7,11},{8,12},{9,13},{1... | collective-permute-start | bytes 6152 | tf_op jit(solution)/shard_map/ppermute | solution.py:17
  17.0 34.7 %collective-permute-start.5 = (f32[2,2,1,128]{3,2,1,0:T(1,128)}, f32[2,2,1,128]{3,2,1,0:T(1,128)S(1)}, u32[]{:S(2)}, u32[]{:S(2)}) collective-permute-start(f32[2,2,1,128]{3,2,1,0:T(1,128)} %get-tuple-element.300), channel_id=1, source_target_pairs={{4,0},{5,1},{6,2},{7,3},{8,4},{9,5},{10,6},{11,7},{12,8},{13,9},{1... | collective-permute-start | bytes 6152 | tf_op jit(solution)/shard_map/ppermute | solution.py:17
  54.8 14.2 %collective-permute-start.8 = (f32[2,2,1,128]{3,2,1,0:T(1,128)S(1)}, f32[2,2,1,128]{3,2,1,0:T(1,128)S(1)}, u32[]{:S(2)}, u32[]{:S(2)}) collective-permute-start(f32[2,2,1,128]{3,2,1,0:T(1,128)S(1)} %get-tuple-element.279), channel_id=1, source_target_pairs={{0,4},{1,5},{2,6},{3,7},{4,8},{5,9},{6,10},{7,11},{8,12},{9,13},{1... | collective-permute-start | bytes 6152 | tf_op jit(solution)/shard_map/ppermute | solution.py:17
  56.1 12.9 %collective-permute-start.9 = (f32[2,2,1,128]{3,2,1,0:T(1,128)S(1)}, f32[2,2,1,128]{3,2,1,0:T(1,128)S(1)}, u32[]{:S(2)}, u32[]{:S(2)}) collective-permute-start(f32[2,2,1,128]{3,2,1,0:T(1,128)S(1)} %get-tuple-element.280), channel_id=1, source_target_pairs={{4,0},{5,1},{6,2},{7,3},{8,4},{9,5},{10,6},{11,7},{12,8},{13,9},{1... | collective-permute-start | bytes 6152 | tf_op jit(solution)/shard_map/ppermute | solution.py:17
  71.8 13.9 %collective-permute-start.12 = (f32[2,2,1,128]{3,2,1,0:T(1,128)S(1)}, f32[2,2,1,128]{3,2,1,0:T(1,128)S(1)}, u32[]{:S(2)}, u32[]{:S(2)}) collective-permute-start(f32[2,2,1,128]{3,2,1,0:T(1,128)S(1)} %get-tuple-element.269), channel_id=1, source_target_pairs={{0,4},{1,5},{2,6},{3,7},{4,8},{5,9},{6,10},{7,11},{8,12},{9,13},{1... | collective-permute-start | bytes 6152 | tf_op jit(solution)/shard_map/ppermute | solution.py:17
  73.1 12.6 %collective-permute-start.13 = (f32[2,2,1,128]{3,2,1,0:T(1,128)S(1)}, f32[2,2,1,128]{3,2,1,0:T(1,128)S(1)}, u32[]{:S(2)}, u32[]{:S(2)}) collective-permute-start(f32[2,2,1,128]{3,2,1,0:T(1,128)S(1)} %get-tuple-element.270), channel_id=1, source_target_pairs={{4,0},{5,1},{6,2},{7,3},{8,4},{9,5},{10,6},{11,7},{12,8},{13,9},{1... | collective-permute-start | bytes 6152 | tf_op jit(solution)/shard_map/ppermute | solution.py:17
  88.5 13.9 %collective-permute-start.16 = (f32[2,2,1,128]{3,2,1,0:T(1,128)S(1)}, f32[2,2,1,128]{3,2,1,0:T(1,128)S(1)}, u32[]{:S(2)}, u32[]{:S(2)}) collective-permute-start(f32[2,2,1,128]{3,2,1,0:T(1,128)S(1)} %get-tuple-element.259), channel_id=1, source_target_pairs={{0,4},{1,5},{2,6},{3,7},{4,8},{5,9},{6,10},{7,11},{8,12},{9,13},{1... | collective-permute-start | bytes 6152 | tf_op jit(solution)/shard_map/ppermute | solution.py:17
  89.8 12.6 %collective-permute-start.17 = (f32[2,2,1,128]{3,2,1,0:T(1,128)S(1)}, f32[2,2,1,128]{3,2,1,0:T(1,128)S(1)}, u32[]{:S(2)}, u32[]{:S(2)}) collective-permute-start(f32[2,2,1,128]{3,2,1,0:T(1,128)S(1)} %get-tuple-element.260), channel_id=1, source_target_pairs={{4,0},{5,1},{6,2},{7,3},{8,4},{9,5},{10,6},{11,7},{12,8},{13,9},{1... | collective-permute-start | bytes 6152 | tf_op jit(solution)/shard_map/ppermute | solution.py:17
  105.2 13.9 %collective-permute-start.20 = (f32[2,2,1,128]{3,2,1,0:T(1,128)S(1)}, f32[2,2,1,128]{3,2,1,0:T(1,128)S(1)}, u32[]{:S(2)}, u32[]{:S(2)}) collective-permute-start(f32[2,2,1,128]{3,2,1,0:T(1,128)S(1)} %get-tuple-element.249), channel_id=1, source_target_pairs={{0,4},{1,5},{2,6},{3,7},{4,8},{5,9},{6,10},{7,11},{8,12},{9,13},{1... | collective-permute-start | bytes 6152 | tf_op jit(solution)/shard_map/ppermute | solution.py:17
  106.5 12.6 %collective-permute-start.21 = (f32[2,2,1,128]{3,2,1,0:T(1,128)S(1)}, f32[2,2,1,128]{3,2,1,0:T(1,128)S(1)}, u32[]{:S(2)}, u32[]{:S(2)}) collective-permute-start(f32[2,2,1,128]{3,2,1,0:T(1,128)S(1)} %get-tuple-element.250), channel_id=1, source_target_pairs={{4,0},{5,1},{6,2},{7,3},{8,4},{9,5},{10,6},{11,7},{12,8},{13,9},{1... | collective-permute-start | bytes 6152 | tf_op jit(solution)/shard_map/ppermute | solution.py:17
  121.9 13.9 %collective-permute-start.24 = (f32[2,2,1,128]{3,2,1,0:T(1,128)S(1)}, f32[2,2,1,128]{3,2,1,0:T(1,128)S(1)}, u32[]{:S(2)}, u32[]{:S(2)}) collective-permute-start(f32[2,2,1,128]{3,2,1,0:T(1,128)S(1)} %get-tuple-element.239), channel_id=1, source_target_pairs={{0,4},{1,5},{2,6},{3,7},{4,8},{5,9},{6,10},{7,11},{8,12},{9,13},{1... | collective-permute-start | bytes 6152 | tf_op jit(solution)/shard_map/ppermute | solution.py:17
  123.2 12.6 %collective-permute-start.25 = (f32[2,2,1,128]{3,2,1,0:T(1,128)S(1)}, f32[2,2,1,128]{3,2,1,0:T(1,128)S(1)}, u32[]{:S(2)}, u32[]{:S(2)}) collective-permute-start(f32[2,2,1,128]{3,2,1,0:T(1,128)S(1)} %get-tuple-element.240), channel_id=1, source_target_pairs={{4,0},{5,1},{6,2},{7,3},{8,4},{9,5},{10,6},{11,7},{12,8},{13,9},{1... | collective-permute-start | bytes 6152 | tf_op jit(solution)/shard_map/ppermute | solution.py:17
  138.6 13.9 %collective-permute-start.28 = (f32[2,2,1,128]{3,2,1,0:T(1,128)S(1)}, f32[2,2,1,128]{3,2,1,0:T(1,128)S(1)}, u32[]{:S(2)}, u32[]{:S(2)}) collective-permute-start(f32[2,2,1,128]{3,2,1,0:T(1,128)S(1)} %get-tuple-element.229), channel_id=1, source_target_pairs={{0,4},{1,5},{2,6},{3,7},{4,8},{5,9},{6,10},{7,11},{8,12},{9,13},{1... | collective-permute-start | bytes 6152 | tf_op jit(solution)/shard_map/ppermute | solution.py:17
  139.9 12.6 %collective-permute-start.29 = (f32[2,2,1,128]{3,2,1,0:T(1,128)S(1)}, f32[2,2,1,128]{3,2,1,0:T(1,128)S(1)}, u32[]{:S(2)}, u32[]{:S(2)}) collective-permute-start(f32[2,2,1,128]{3,2,1,0:T(1,128)S(1)} %get-tuple-element.230), channel_id=1, source_target_pairs={{4,0},{5,1},{6,2},{7,3},{8,4},{9,5},{10,6},{11,7},{12,8},{13,9},{1... | collective-permute-start | bytes 6152 | tf_op jit(solution)/shard_map/ppermute | solution.py:17
  155.3 13.9 %collective-permute-start.32 = (f32[2,2,1,128]{3,2,1,0:T(1,128)S(1)}, f32[2,2,1,128]{3,2,1,0:T(1,128)S(1)}, u32[]{:S(2)}, u32[]{:S(2)}) collective-permute-start(f32[2,2,1,128]{3,2,1,0:T(1,128)S(1)} %get-tuple-element.219), channel_id=1, source_target_pairs={{0,4},{1,5},{2,6},{3,7},{4,8},{5,9},{6,10},{7,11},{8,12},{9,13},{1... | collective-permute-start | bytes 6152 | tf_op jit(solution)/shard_map/ppermute | solution.py:17
  156.6 12.6 %collective-permute-start.33 = (f32[2,2,1,128]{3,2,1,0:T(1,128)S(1)}, f32[2,2,1,128]{3,2,1,0:T(1,128)S(1)}, u32[]{:S(2)}, u32[]{:S(2)}) collective-permute-start(f32[2,2,1,128]{3,2,1,0:T(1,128)S(1)} %get-tuple-element.220), channel_id=1, source_target_pairs={{4,0},{5,1},{6,2},{7,3},{8,4},{9,5},{10,6},{11,7},{12,8},{13,9},{1... | collective-permute-start | bytes 6152 | tf_op jit(solution)/shard_map/ppermute | solution.py:17
  174.3 180.2 %collective-permute-start.36 = (f32[2,2,1,128]{3,2,1,0:T(1,128)S(1)}, f32[2,2,1,128]{3,2,1,0:T(1,128)S(1)}, u32[]{:S(2)}, u32[]{:S(2)}) collective-permute-start(f32[2,2,1,128]{3,2,1,0:T(1,128)S(1)} %get-tuple-element.209), channel_id=1, source_target_pairs={{0,4},{1,5},{2,6},{3,7},{4,8},{5,9},{6,10},{7,11},{8,12},{9,13},{1... | collective-permute-start | bytes 6152 | tf_op jit(solution)/shard_map/ppermute | solution.py:17
  175.6 178.9 %collective-permute-start.37 = (f32[2,2,1,128]{3,2,1,0:T(1,128)S(1)}, f32[2,2,1,128]{3,2,1,0:T(1,128)S(1)}, u32[]{:S(2)}, u32[]{:S(2)}) collective-permute-start(f32[2,2,1,128]{3,2,1,0:T(1,128)S(1)} %get-tuple-element.210), channel_id=1, source_target_pairs={{4,0},{5,1},{6,2},{7,3},{8,4},{9,5},{10,6},{11,7},{12,8},{13,9},{1... | collective-permute-start | bytes 6152 | tf_op jit(solution)/shard_map/ppermute | solution.py:17
  184.3 456.5 %all-reduce.55.cloned.1.call-start = ((), (), s32[]{:S(2)}) async-start(), calls=%async_computation | async-start | bytes 262144 | tf_op jit(solution)/shard_map/psum | solution.py:125
  357.4 12.8 %collective-permute-start.40 = (f32[2,2,1,128]{3,2,1,0:T(1,128)S(1)}, f32[2,2,1,128]{3,2,1,0:T(1,128)S(1)}, u32[]{:S(2)}, u32[]{:S(2)}) collective-permute-start(f32[2,2,1,128]{3,2,1,0:T(1,128)S(1)} %get-tuple-element.199), channel_id=1, source_target_pairs={{0,4},{1,5},{2,6},{3,7},{4,8},{5,9},{6,10},{7,11},{8,12},{9,13},{1... | collective-permute-start | bytes 6152 | tf_op jit(solution)/shard_map/ppermute | solution.py:17
  373.0 13.7 %collective-permute-start.44 = (f32[2,2,1,128]{3,2,1,0:T(1,128)S(1)}, f32[2,2,1,128]{3,2,1,0:T(1,128)S(1)}, u32[]{:S(2)}, u32[]{:S(2)}) collective-permute-start(f32[2,2,1,128]{3,2,1,0:T(1,128)S(1)} %get-tuple-element.189), channel_id=1, source_target_pairs={{0,4},{1,5},{2,6},{3,7},{4,8},{5,9},{6,10},{7,11},{8,12},{9,13},{1... | collective-permute-start | bytes 6152 | tf_op jit(solution)/shard_map/ppermute | solution.py:17
  389.4 13.9 %collective-permute-start.48 = (f32[2,2,1,128]{3,2,1,0:T(1,128)S(1)}, f32[2,2,1,128]{3,2,1,0:T(1,128)S(1)}, u32[]{:S(2)}, u32[]{:S(2)}) collective-permute-start(f32[2,2,1,128]{3,2,1,0:T(1,128)S(1)} %get-tuple-element.179), channel_id=1, source_target_pairs={{0,4},{1,5},{2,6},{3,7},{4,8},{5,9},{6,10},{7,11},{8,12},{9,13},{1... | collective-permute-start | bytes 6152 | tf_op jit(solution)/shard_map/ppermute | solution.py:17
  390.7 12.6 %collective-permute-start.49 = (f32[2,2,1,128]{3,2,1,0:T(1,128)S(1)}, f32[2,2,1,128]{3,2,1,0:T(1,128)S(1)}, u32[]{:S(2)}, u32[]{:S(2)}) collective-permute-start(f32[2,2,1,128]{3,2,1,0:T(1,128)S(1)} %get-tuple-element.180), channel_id=1, source_target_pairs={{4,0},{5,1},{6,2},{7,3},{8,4},{9,5},{10,6},{11,7},{12,8},{13,9},{1... | collective-permute-start | bytes 6152 | tf_op jit(solution)/shard_map/ppermute | solution.py:17
  406.1 13.9 %collective-permute-start.52 = (f32[2,2,1,128]{3,2,1,0:T(1,128)S(1)}, f32[2,2,1,128]{3,2,1,0:T(1,128)S(1)}, u32[]{:S(2)}, u32[]{:S(2)}) collective-permute-start(f32[2,2,1,128]{3,2,1,0:T(1,128)S(1)} %get-tuple-element.169), channel_id=1, source_target_pairs={{0,4},{1,5},{2,6},{3,7},{4,8},{5,9},{6,10},{7,11},{8,12},{9,13},{1... | collective-permute-start | bytes 6152 | tf_op jit(solution)/shard_map/ppermute | solution.py:17
  407.4 12.6 %collective-permute-start.53 = (f32[2,2,1,128]{3,2,1,0:T(1,128)S(1)}, f32[2,2,1,128]{3,2,1,0:T(1,128)S(1)}, u32[]{:S(2)}, u32[]{:S(2)}) collective-permute-start(f32[2,2,1,128]{3,2,1,0:T(1,128)S(1)} %get-tuple-element.170), channel_id=1, source_target_pairs={{4,0},{5,1},{6,2},{7,3},{8,4},{9,5},{10,6},{11,7},{12,8},{13,9},{1... | collective-permute-start | bytes 6152 | tf_op jit(solution)/shard_map/ppermute | solution.py:17
  422.8 13.9 %collective-permute-start.56 = (f32[2,2,1,128]{3,2,1,0:T(1,128)S(1)}, f32[2,2,1,128]{3,2,1,0:T(1,128)S(1)}, u32[]{:S(2)}, u32[]{:S(2)}) collective-permute-start(f32[2,2,1,128]{3,2,1,0:T(1,128)S(1)} %get-tuple-element.159), channel_id=1, source_target_pairs={{0,4},{1,5},{2,6},{3,7},{4,8},{5,9},{6,10},{7,11},{8,12},{9,13},{1... | collective-permute-start | bytes 6152 | tf_op jit(solution)/shard_map/ppermute | solution.py:17
  424.1 12.6 %collective-permute-start.57 = (f32[2,2,1,128]{3,2,1,0:T(1,128)S(1)}, f32[2,2,1,128]{3,2,1,0:T(1,128)S(1)}, u32[]{:S(2)}, u32[]{:S(2)}) collective-permute-start(f32[2,2,1,128]{3,2,1,0:T(1,128)S(1)} %get-tuple-element.160), channel_id=1, source_target_pairs={{4,0},{5,1},{6,2},{7,3},{8,4},{9,5},{10,6},{11,7},{12,8},{13,9},{1... | collective-permute-start | bytes 6152 | tf_op jit(solution)/shard_map/ppermute | solution.py:17
  439.5 13.9 %collective-permute-start.60 = (f32[2,2,1,128]{3,2,1,0:T(1,128)S(1)}, f32[2,2,1,128]{3,2,1,0:T(1,128)S(1)}, u32[]{:S(2)}, u32[]{:S(2)}) collective-permute-start(f32[2,2,1,128]{3,2,1,0:T(1,128)S(1)} %get-tuple-element.149), channel_id=1, source_target_pairs={{0,4},{1,5},{2,6},{3,7},{4,8},{5,9},{6,10},{7,11},{8,12},{9,13},{1... | collective-permute-start | bytes 6152 | tf_op jit(solution)/shard_map/ppermute | solution.py:17
  440.8 12.6 %collective-permute-start.61 = (f32[2,2,1,128]{3,2,1,0:T(1,128)S(1)}, f32[2,2,1,128]{3,2,1,0:T(1,128)S(1)}, u32[]{:S(2)}, u32[]{:S(2)}) collective-permute-start(f32[2,2,1,128]{3,2,1,0:T(1,128)S(1)} %get-tuple-element.150), channel_id=1, source_target_pairs={{4,0},{5,1},{6,2},{7,3},{8,4},{9,5},{10,6},{11,7},{12,8},{13,9},{1... | collective-permute-start | bytes 6152 | tf_op jit(solution)/shard_map/ppermute | solution.py:17
  456.2 13.9 %collective-permute-start.64 = (f32[2,2,1,128]{3,2,1,0:T(1,128)S(1)}, f32[2,2,1,128]{3,2,1,0:T(1,128)S(1)}, u32[]{:S(2)}, u32[]{:S(2)}) collective-permute-start(f32[2,2,1,128]{3,2,1,0:T(1,128)S(1)} %get-tuple-element.139), channel_id=1, source_target_pairs={{0,4},{1,5},{2,6},{3,7},{4,8},{5,9},{6,10},{7,11},{8,12},{9,13},{1... | collective-permute-start | bytes 6152 | tf_op jit(solution)/shard_map/ppermute | solution.py:17
  457.5 12.6 %collective-permute-start.65 = (f32[2,2,1,128]{3,2,1,0:T(1,128)S(1)}, f32[2,2,1,128]{3,2,1,0:T(1,128)S(1)}, u32[]{:S(2)}, u32[]{:S(2)}) collective-permute-start(f32[2,2,1,128]{3,2,1,0:T(1,128)S(1)} %get-tuple-element.140), channel_id=1, source_target_pairs={{4,0},{5,1},{6,2},{7,3},{8,4},{9,5},{10,6},{11,7},{12,8},{13,9},{1... | collective-permute-start | bytes 6152 | tf_op jit(solution)/shard_map/ppermute | solution.py:17
  475.9 449.3 %all-reduce.57.cloned.1.call-start = ((), (), s32[]{:S(2)}) async-start(), calls=%async_computation.1 | async-start | bytes 262144 | tf_op jit(solution)/shard_map/psum | solution.py:125
  475.9 166.1 %collective-permute-start.68 = (f32[2,2,1,128]{3,2,1,0:T(1,128)S(1)}, f32[2,2,1,128]{3,2,1,0:T(1,128)S(1)}, u32[]{:S(2)}, u32[]{:S(2)}) collective-permute-start(f32[2,2,1,128]{3,2,1,0:T(1,128)S(1)} %get-tuple-element.129), channel_id=1, source_target_pairs={{0,4},{1,5},{2,6},{3,7},{4,8},{5,9},{6,10},{7,11},{8,12},{9,13},{1... | collective-permute-start | bytes 6152 | tf_op jit(solution)/shard_map/ppermute | solution.py:17
  477.2 164.8 %collective-permute-start.69 = (f32[2,2,1,128]{3,2,1,0:T(1,128)S(1)}, f32[2,2,1,128]{3,2,1,0:T(1,128)S(1)}, u32[]{:S(2)}, u32[]{:S(2)}) collective-permute-start(f32[2,2,1,128]{3,2,1,0:T(1,128)S(1)} %get-tuple-element.130), channel_id=1, source_target_pairs={{4,0},{5,1},{6,2},{7,3},{8,4},{9,5},{10,6},{11,7},{12,8},{13,9},{1... | collective-permute-start | bytes 6152 | tf_op jit(solution)/shard_map/ppermute | solution.py:17
  645.7 12.8 %collective-permute-start.72 = (f32[2,2,1,128]{3,2,1,0:T(1,128)S(1)}, f32[2,2,1,128]{3,2,1,0:T(1,128)S(1)}, u32[]{:S(2)}, u32[]{:S(2)}) collective-permute-start(f32[2,2,1,128]{3,2,1,0:T(1,128)S(1)} %get-tuple-element.119), channel_id=1, source_target_pairs={{0,4},{1,5},{2,6},{3,7},{4,8},{5,9},{6,10},{7,11},{8,12},{9,13},{1... | collective-permute-start | bytes 6152 | tf_op jit(solution)/shard_map/ppermute | solution.py:17
  661.3 13.7 %collective-permute-start.76 = (f32[2,2,1,128]{3,2,1,0:T(1,128)S(1)}, f32[2,2,1,128]{3,2,1,0:T(1,128)S(1)}, u32[]{:S(2)}, u32[]{:S(2)}) collective-permute-start(f32[2,2,1,128]{3,2,1,0:T(1,128)S(1)} %get-tuple-element.109), channel_id=1, source_target_pairs={{0,4},{1,5},{2,6},{3,7},{4,8},{5,9},{6,10},{7,11},{8,12},{9,13},{1... | collective-permute-start | bytes 6152 | tf_op jit(solution)/shard_map/ppermute | solution.py:17
  677.8 13.9 %collective-permute-start.80 = (f32[2,2,1,128]{3,2,1,0:T(1,128)S(1)}, f32[2,2,1,128]{3,2,1,0:T(1,128)S(1)}, u32[]{:S(2)}, u32[]{:S(2)}) collective-permute-start(f32[2,2,1,128]{3,2,1,0:T(1,128)S(1)} %get-tuple-element.99), channel_id=1, source_target_pairs={{0,4},{1,5},{2,6},{3,7},{4,8},{5,9},{6,10},{7,11},{8,12},{9,13},{1... | collective-permute-start | bytes 6152 | tf_op jit(solution)/shard_map/ppermute | solution.py:17
  679.1 12.6 %collective-permute-start.81 = (f32[2,2,1,128]{3,2,1,0:T(1,128)S(1)}, f32[2,2,1,128]{3,2,1,0:T(1,128)S(1)}, u32[]{:S(2)}, u32[]{:S(2)}) collective-permute-start(f32[2,2,1,128]{3,2,1,0:T(1,128)S(1)} %get-tuple-element.100), channel_id=1, source_target_pairs={{4,0},{5,1},{6,2},{7,3},{8,4},{9,5},{10,6},{11,7},{12,8},{13,9},{1... | collective-permute-start | bytes 6152 | tf_op jit(solution)/shard_map/ppermute | solution.py:17
  694.7 13.9 %collective-permute-start.84 = (f32[2,2,1,128]{3,2,1,0:T(1,128)S(1)}, f32[2,2,1,128]{3,2,1,0:T(1,128)S(1)}, u32[]{:S(2)}, u32[]{:S(2)}) collective-permute-start(f32[2,2,1,128]{3,2,1,0:T(1,128)S(1)} %get-tuple-element.89), channel_id=1, source_target_pairs={{0,4},{1,5},{2,6},{3,7},{4,8},{5,9},{6,10},{7,11},{8,12},{9,13},{1... | collective-permute-start | bytes 6152 | tf_op jit(solution)/shard_map/ppermute | solution.py:17
  696.0 12.6 %collective-permute-start.85 = (f32[2,2,1,128]{3,2,1,0:T(1,128)S(1)}, f32[2,2,1,128]{3,2,1,0:T(1,128)S(1)}, u32[]{:S(2)}, u32[]{:S(2)}) collective-permute-start(f32[2,2,1,128]{3,2,1,0:T(1,128)S(1)} %get-tuple-element.90), channel_id=1, source_target_pairs={{4,0},{5,1},{6,2},{7,3},{8,4},{9,5},{10,6},{11,7},{12,8},{13,9},{1... | collective-permute-start | bytes 6152 | tf_op jit(solution)/shard_map/ppermute | solution.py:17
  711.4 13.9 %collective-permute-start.88 = (f32[2,2,1,128]{3,2,1,0:T(1,128)S(1)}, f32[2,2,1,128]{3,2,1,0:T(1,128)S(1)}, u32[]{:S(2)}, u32[]{:S(2)}) collective-permute-start(f32[2,2,1,128]{3,2,1,0:T(1,128)S(1)} %get-tuple-element.79), channel_id=1, source_target_pairs={{0,4},{1,5},{2,6},{3,7},{4,8},{5,9},{6,10},{7,11},{8,12},{9,13},{1... | collective-permute-start | bytes 6152 | tf_op jit(solution)/shard_map/ppermute | solution.py:17
  712.7 12.6 %collective-permute-start.89 = (f32[2,2,1,128]{3,2,1,0:T(1,128)S(1)}, f32[2,2,1,128]{3,2,1,0:T(1,128)S(1)}, u32[]{:S(2)}, u32[]{:S(2)}) collective-permute-start(f32[2,2,1,128]{3,2,1,0:T(1,128)S(1)} %get-tuple-element.80), channel_id=1, source_target_pairs={{4,0},{5,1},{6,2},{7,3},{8,4},{9,5},{10,6},{11,7},{12,8},{13,9},{1... | collective-permute-start | bytes 6152 | tf_op jit(solution)/shard_map/ppermute | solution.py:17
  728.1 13.9 %collective-permute-start.92 = (f32[2,2,1,128]{3,2,1,0:T(1,128)S(1)}, f32[2,2,1,128]{3,2,1,0:T(1,128)S(1)}, u32[]{:S(2)}, u32[]{:S(2)}) collective-permute-start(f32[2,2,1,128]{3,2,1,0:T(1,128)S(1)} %get-tuple-element.69), channel_id=1, source_target_pairs={{0,4},{1,5},{2,6},{3,7},{4,8},{5,9},{6,10},{7,11},{8,12},{9,13},{1... | collective-permute-start | bytes 6152 | tf_op jit(solution)/shard_map/ppermute | solution.py:17
  729.4 12.6 %collective-permute-start.93 = (f32[2,2,1,128]{3,2,1,0:T(1,128)S(1)}, f32[2,2,1,128]{3,2,1,0:T(1,128)S(1)}, u32[]{:S(2)}, u32[]{:S(2)}) collective-permute-start(f32[2,2,1,128]{3,2,1,0:T(1,128)S(1)} %get-tuple-element.70), channel_id=1, source_target_pairs={{4,0},{5,1},{6,2},{7,3},{8,4},{9,5},{10,6},{11,7},{12,8},{13,9},{1... | collective-permute-start | bytes 6152 | tf_op jit(solution)/shard_map/ppermute | solution.py:17
  744.8 13.9 %collective-permute-start.96 = (f32[2,2,1,128]{3,2,1,0:T(1,128)S(1)}, f32[2,2,1,128]{3,2,1,0:T(1,128)S(1)}, u32[]{:S(2)}, u32[]{:S(2)}) collective-permute-start(f32[2,2,1,128]{3,2,1,0:T(1,128)S(1)} %get-tuple-element.59), channel_id=1, source_target_pairs={{0,4},{1,5},{2,6},{3,7},{4,8},{5,9},{6,10},{7,11},{8,12},{9,13},{1... | collective-permute-start | bytes 6152 | tf_op jit(solution)/shard_map/ppermute | solution.py:17
  (76 other events, 1374.4 us)
Sparse Core Ops, SparseCore 0:
  184.5 168.8 all-reduce.58
  476.0 164.7 all-reduce.54
  760.9 164.2 all-reduce.56
where the time goes:
time: 938 us; the launch traced here: 933 us
  waiting for transfers between devices  585 us (62%)
  starting transfers between devices  294 us (31%)
  other arithmetic  21.7 us (2%)
  local copies, waits for them, and re-layouts  17 us (2%)
  between operations  16.6 us (2%)
    psum x2, waiting for transfers between devices, on_device(): taken_energy = lax.psum(absorbed_part, 'gas')  315 us
    ppermute x100, starting transfers between devices, from_behind(): return lax.ppermute(array, axis, pairs)  293 us
    psum x1, waiting for transfers between devices, on_device(): emitted_power = lax.psum(emission_part, 'gas')  164 us
    ppermute x100, waiting for transfers between devices, from_behind(): return lax.ppermute(array, axis, pairs)  105 us
  transfers between devices with their start and end apart: 103, of which 30 were waited for; matrix products, arithmetic and copies ran while one was open for 1% of the time, Pallas kernels for 0%

commit v1 on v0

v1 whole, which is shorter than its diff:
```python
import functools

import jax
import jax.numpy as jnp
from jax import lax
from jax.experimental import pallas as pl
from jax.experimental.pallas import tpu as pltpu
from jax.sharding import PartitionSpec as P

SWEEPS = 8
OUTER = 3
LOW_BOUND = 0.05
HIGH_BOUND = 2.0

TILE = 128
HALO = SWEEPS * OUTER
ROWS = TILE + 2 * HALO
PAD = 8
STEP = 16
PLANES = 18
PACK = 5
PACKS = 4
CHUNK = 40
GROUP = 16
LAST = ROWS // 8 - 1
EXTRA = (1, 2, LAST - 2, LAST - 1)
VMEM_LIMIT = 40 * 1024 * 1024
F32 = jnp.float32


def sweep_weights():
    theta_mid = (HIGH_BOUND + LOW_BOUND) / 2.0
    delta_half = (HIGH_BOUND - LOW_BOUND) / 2.0
    sigma_ratio = theta_mid / delta_half
    rho_now = 1.0 / sigma_ratio
    weights = [(0.0, 1.0 / theta_mid)]
    for _ in range(SWEEPS - 1):
        rho_next = 1.0 / (2.0 * sigma_ratio - rho_now)
        weights.append((rho_next * rho_now, 2.0 * rho_next / delta_half))
        rho_now = rho_next
    return weights


def own_planes(refs):
    k, w, g, t, i, s = refs
    planes = [(ref, (gas, 0, z)) for ref in (k, w, g) for gas in range(2) for z in range(2)]
    return planes + [(ref, (0, z)) for ref in (t, i, s) for z in range(2)]


def pack_x_kernel(*refs):
    up, down = refs[6:]
    for p, (ref, at) in enumerate(own_planes(refs[:6])):
        up[p] = ref[at + (pl.ds(TILE - HALO, HALO), slice(None))]
        down[p] = ref[at + (pl.ds(0, HALO), slice(None))]


def row_parts():
    parts = [(0, HALO, "top", 0)]
    parts += [(HALO + r, 32, "own", r) for r in range(0, TILE, 32)]
    parts += [(HALO + TILE, HALO, "bottom", 0)]
    return parts


def pack_y_kernel(*refs):
    planes = own_planes(refs[:6])
    top, bottom, right, left = refs[6:]
    for row, count, kind, at_row in row_parts():
        lane = lax.broadcasted_iota(jnp.int32, (count, TILE), 1)
        for t in range(PACKS):
            to_right = jnp.zeros((count, TILE), F32)
            to_left = jnp.zeros((count, TILE), F32)
            for j in range(PACK):
                p = t * PACK + j
                if p >= PLANES:
                    break
                if kind == "own":
                    ref, at = planes[p]
                    value = ref[at + (pl.ds(at_row, count), slice(None))]
                else:
                    value = (top if kind == "top" else bottom)[p]
                here = (lane >= HALO * j) & (lane < HALO * (j + 1))
                to_left = jnp.where(here, pltpu.roll(value, (HALO * j) % TILE, 1), to_left)
                to_right = jnp.where(here, pltpu.roll(value, (HALO * (j + 1)) % TILE, 1), to_right)
            right[t, pl.ds(row, count), :] = to_right
            left[t, pl.ds(row, count), :] = to_left


def chunk_out(out, field, first=0):
    for c in range(GROUP):
        z, i = divmod(c, 8)
        for l in range(2):
            out[c, pl.ds(first + 16 * l, 16), :] = field[z, l, pl.ds(HALO + 16 * i, 16), :]
        e, l, z = c // 4, (c // 2) % 2, c % 2
        out[c, pl.ds(first + 32, 8), :] = field[z, l, pl.ds(8 * EXTRA[e], 8), :]


def chunk_in(field, chunks, change):
    for c in range(GROUP):
        z, i = divmod(c, 8)
        for l in range(2):
            field[z, l, pl.ds(HALO + 16 * i, 16), :] = change(chunks[c, pl.ds(16 * l, 16), :])
        e, l, z = c // 4, (c // 2) % 2, c % 2
        field[z, l, pl.ds(8 * EXTRA[e], 8), :] = change(chunks[c, pl.ds(32, 8), :])


def fourth(value):
    square = value * value
    return square * square


def left_right(own, other, lane):
    left = pltpu.roll(jnp.where(lane == TILE - 1, other, own), 1, 1)
    right = pltpu.roll(jnp.where(lane == 0, other, own), TILE - 1, 1)
    return left, right


def each_step(first, last, body):
    def run(i, carry):
        body(pl.multiple_of(first + STEP * i, 8))
        return carry

    lax.fori_loop(0, (last - first) // STEP, run, 0)


def solve(step, a, q, t4, sp, now, old):
    first, last = 8 * step, ROWS - 8 * step

    def source(r):
        for gz in range(4):
            for l in range(2):
                weight = q[gz, l, pl.ds(r, STEP), :]
                value = weight * t4[gz % 2, l, pl.ds(r, STEP), :]
                sp[gz, l, pl.ds(r, STEP), :] = jnp.where(weight > 0.0, value, 0.0)

    each_step(first, last, source)
    for sweep, (keep, push) in enumerate(sweep_weights()):
        src, dst = (now, old) if sweep % 2 == 0 else (old, now)

        def body(r, src=src, dst=dst, keep=keep, push=push, sweep=sweep):
            lane = lax.broadcasted_iota(jnp.int32, (STEP, TILE), 1)
            rows = pl.ds(r, STEP)
            for g in range(2):
                own = [[src[2 * g + z, l, pl.ds(r + PAD, STEP), :] for l in range(2)] for z in range(2)]
                for z in range(2):
                    for l in range(2):
                        gz = 2 * g + z
                        here = own[z][l]
                        left, right = left_right(here, own[z][1 - l], lane)
                        total = sp[gz, l, rows, :] + a[0, gz, l, rows, :] * own[1 - z][l]
                        total += a[1, gz, l, rows, :] * src[gz, l, pl.ds(r + PAD - 1, STEP), :]
                        total += a[2, gz, l, rows, :] * src[gz, l, pl.ds(r + PAD + 1, STEP), :]
                        total += a[3, gz, l, rows, :] * left + a[4, gz, l, rows, :] * right
                        value = (1.0 + keep - push) * here + push * total
                        if sweep:
                            value -= keep * dst[gz, l, pl.ds(r + PAD, STEP), :]
                        dst[gz, l, pl.ds(r + PAD, STEP), :] = value

        each_step(first, last, body)


def absorb(kap, now, out):
    def body(r):
        for z in range(2):
            for l in range(2):
                rows = pl.ds(r + PAD, STEP)
                out[z, l, pl.ds(r, STEP), :] = (
                    kap[z, l, rows, :] * now[z, l, rows, :] + kap[2 + z, l, rows, :] * now[2 + z, l, rows, :]
                )

    each_step(8, ROWS - 8, body)


def first_kernel(*refs):
    planes = own_planes(refs[:6])
    top, bottom, from_left, from_right = refs[6:10]
    a, q, kap, now, sums, held = refs[10:16]
    tis, sp, t4, old = refs[16:]
    planck = sp

    def place(p):
        if p < 4:
            return kap, p, PAD
        if p < 8:
            return q, p - 4, 0
        if p < 12:
            return now, p - 8, PAD
        return tis, p - 12, 0

    for p in range(PLANES):
        dst, at, pad = place(p)
        ref, own = planes[p]
        dst[at, 0, pl.ds(pad, HALO), :] = top[p]
        dst[at, 0, pl.ds(pad + HALO, TILE), :] = ref[own]
        dst[at, 0, pl.ds(pad + HALO + TILE, HALO), :] = bottom[p]
    for buffer in (kap, now, old):
        for gz in range(4):
            for l in range(2):
                buffer[gz, l, pl.ds(0, PAD), :] = jnp.zeros((PAD, TILE), F32)
                buffer[gz, l, pl.ds(PAD + ROWS, PAD), :] = jnp.zeros((PAD, TILE), F32)

    def sides(r):
        lane = lax.broadcasted_iota(jnp.int32, (STEP, TILE), 1)
        for t in range(PACKS):
            lefts = from_left[t, pl.ds(r, STEP), :]
            rights = from_right[t, pl.ds(r, STEP), :]
            for j in range(PACK):
                p = t * PACK + j
                if p >= PLANES:
                    break
                dst, at, pad = place(p)
                right = jnp.where(lane < HALO, pltpu.roll(rights, (TILE - HALO * j) % TILE, 1), 0.0)
                left = pltpu.roll(lefts, (TILE - HALO * (j + 1)) % TILE, 1)
                dst[at, 1, pl.ds(r + pad, STEP), :] = jnp.where(lane >= TILE - HALO, left, right)

    each_step(0, ROWS, sides)
    for f in range(3):
        chunk_out(held.at[f], tis.at[pl.ds(2 * f, 2)])

    def coefficients(r):
        lane = lax.broadcasted_iota(jnp.int32, (STEP, TILE), 1)
        rows = pl.ds(r, STEP)
        two_thirds = 2.0 / 3.0
        for z in range(2):
            for l in range(2):
                t4[z, l, rows, :] = fourth(tis[z, l, rows, :])
                planck[z, l, rows, :] = (
                    kap[z, l, pl.ds(r + PAD, STEP), :] * q[z, l, rows, :]
                    + kap[2 + z, l, pl.ds(r + PAD, STEP), :] * q[2 + z, l, rows, :]
                )
        for g in range(2):
            own = [[kap[2 * g + z, l, pl.ds(r + PAD, STEP), :] for l in range(2)] for z in range(2)]
            between = [two_thirds / (own[0][l] + own[1][l]) for l in range(2)]
            for z in range(2):
                for l in range(2):
                    gz = 2 * g + z
                    here = own[z][l]
                    left, right = left_right(here, own[z][1 - l], lane)
                    couplings = [
                        between[l],
                        two_thirds / (here + kap[gz, l, pl.ds(r + PAD - 1, STEP), :]),
                        two_thirds / (here + kap[gz, l, pl.ds(r + PAD + 1, STEP), :]),
                        two_thirds / (here + left),
                        two_thirds / (here + right),
                    ]
                    diagonal = here + two_thirds / here
                    for coupling in couplings:
                        diagonal += coupling
                    inside = here > 0.0
                    inverse = 1.0 / diagonal
                    for f, coupling in enumerate(couplings):
                        a[f, gz, l, rows, :] = jnp.where(inside, coupling * inverse, 0.0)
                    weight = 4.0 * here * q[gz, l, rows, :] * inverse
                    q[gz, l, rows, :] = jnp.where(inside, weight, 0.0)

    each_step(0, ROWS, coefficients)
    chunk_out(sums, planck, CHUNK)
    solve(0, a, q, t4, sp, now, old)
    absorb(kap, now, t4)
    chunk_out(sums, t4)


def next_kernel(a, q, kap, now_in, chunks, now, sums, sp, t4, old):
    now[...] = now_in[...]
    chunk_in(t4, chunks, fourth)
    solve(1, a, q, t4, sp, now, old)
    absorb(kap, now, t4)
    chunk_out(sums, t4)


def last_kernel(a, q, kap, now_in, chunks, radiation, sums, sp, t4, old, now):
    now[...] = now_in[...]
    chunk_in(t4, chunks, fourth)
    solve(2, a, q, t4, sp, now, old)
    rows = pl.ds(PAD + HALO, TILE)
    for gz in range(4):
        radiation[gz // 2, 0, gz % 2, :, :] = now[gz, 0, rows, :]
    for c in range(GROUP):
        z, i = divmod(c, 8)
        part = pl.ds(PAD + HALO + 16 * i, 16)
        sums[c] = kap[z, 0, part, :] * now[z, 0, part, :] + kap[2 + z, 0, part, :] * now[2 + z, 0, part, :]


def corrected(current, earlier, inertia, source, emitted, taken):
    mismatch = inertia * (current - earlier) + 4.0 * emitted * fourth(current) - taken - source
    slope = inertia + 16.0 * emitted * (current * current * current)
    return jnp.where(inertia > 0.0, current - mismatch / slope, 0.0)


def first_update(me, parts, held, everyone, state):
    total = parts[0]
    for c in range(1, GROUP):
        total += parts[c]
    taken, emitted = total[:CHUNK], total[CHUNK:]
    earlier, inertia, source = held[0, me[0]], held[1, me[0]], held[2, me[0]]
    current = corrected(earlier, earlier, inertia, source, emitted, taken)
    for f, value in enumerate((current, earlier, inertia, source, emitted)):
        state[f] = value
    for c in range(GROUP):
        everyone[c] = current


def next_update(parts, state_in, everyone, state):
    count = everyone.shape[1]
    total = parts[0]
    for c in range(1, GROUP):
        total += parts[c]
    current, earlier, inertia, source, emitted = (state_in[f, pl.ds(0, count), :] for f in range(5))
    current = corrected(current, earlier, inertia, source, emitted, total)
    if state is not None:
        for f, value in enumerate((current, earlier, inertia, source, emitted)):
            state[f] = value
    for c in range(GROUP):
        everyone[c] = current


def last_update(parts, state_in, everyone):
    next_update(parts, state_in, everyone, None)


def call(kernel, outs, scratch=(), smem=0):
    def shape(*dims):
        return jax.ShapeDtypeStruct(dims, F32)

    def run(*args):
        specs = [pl.BlockSpec(memory_space=pltpu.SMEM)] * smem
        specs += [pl.BlockSpec(memory_space=pltpu.VMEM)] * (len(args) - smem)
        return pl.pallas_call(
            kernel,
            out_shape=[shape(*dims) for dims in outs],
            in_specs=specs,
            out_specs=[pl.BlockSpec(memory_space=pltpu.VMEM)] * len(outs),
            scratch_shapes=[pltpu.VMEM(dims, F32) for dims in scratch],
            compiler_params=pltpu.CompilerParams(vmem_limit_bytes=VMEM_LIMIT),
        )(*args)

    return run


FIELD = (4, 2, ROWS, TILE)
PADDED = (4, 2, ROWS + 2 * PAD, TILE)
SHARED = (2, 2, ROWS, TILE)


def swap(array):
    return lax.all_to_all(array, "gas", 0, 0)


def on_device(*inputs):
    kelvin, inertia, source, extinction, fractions, irradiance = inputs
    own = (extinction, fractions, irradiance, kelvin, inertia, source)
    devices = lax.axis_size("space")
    across = 4
    up, down = call(pack_x_kernel, [(PLANES, HALO, TILE)] * 2)(*own)
    top = lax.ppermute(up, "space", [(i, i + across) for i in range(devices - across)])
    bottom = lax.ppermute(down, "space", [(i + across, i) for i in range(devices - across)])
    right, left = call(pack_y_kernel, [(PACKS, ROWS, TILE)] * 2)(*own, top, bottom)
    pairs = [(i, i + 1) for i in range(devices) if i % across != across - 1]
    from_left = lax.ppermute(right, "space", pairs)
    from_right = lax.ppermute(left, "space", [(j, i) for i, j in pairs])
    a, q, kap, now, sums, held = call(
        first_kernel,
        [(5,) + FIELD, FIELD, PADDED, PADDED, (GROUP, 2 * CHUNK, TILE), (3, GROUP, CHUNK, TILE)],
        [(6, 2, ROWS, TILE), FIELD, SHARED, PADDED],
    )(*own, top, bottom, from_left, from_right)
    me = lax.axis_index("gas").reshape(1)
    chunks, state = call(first_update, [(GROUP, CHUNK, TILE), (5, CHUNK, TILE)], smem=1)(me, swap(sums), held)
    now, sums = call(next_kernel, [PADDED, (GROUP, CHUNK, TILE)], [FIELD, SHARED, PADDED])(
        a, q, kap, now, swap(chunks)
    )
    chunks, state = call(next_update, [(GROUP, CHUNK, TILE), (5, CHUNK, TILE)])(swap(sums), state)
    radiation, sums = call(
        last_kernel, [(2, 1, 2, TILE, TILE), (GROUP, 16, TILE)], [FIELD, SHARED, PADDED, PADDED]
    )(a, q, kap, now, swap(chunks))
    (chunks,) = call(last_update, [(GROUP, 16, TILE)])(swap(sums), state)
    final = swap(chunks).reshape(1, 2, TILE, TILE)
    return final, radiation


def solution(mesh):
    placed = (
        P("space", None, None, None),
        P("space", None, None, None),
        P("space", None, None, None),
        P("gas", "space", None, None, None),
        P("gas", "space", None, None, None),
        P("gas", "space", None, None, None),
    )
    return jax.shard_map(
        on_device,
        mesh=mesh,
        in_specs=placed,
        out_specs=(P("space", None, None, None), P("gas", "space", None, None, None)),
        check_vma=False,
    )
```

time: 938 us -> 174 us (0.19)
  the two profiles are of different devices: /device:TPU:38 before, /device:TPU:2 now
where the time goes in v1:
time: 174 us; the launch traced here: 173 us
  blocking collectives  81.3 us (47%)
  Pallas kernels  31.9 us (18%)
  waiting for transfers between devices  27.5 us (16%)
  starting transfers between devices  18.8 us (11%)
  local copies, waits for them, and re-layouts  12.9 us (7%)
    all_to_all x5, blocking collectives, swap(): return lax.all_to_all(array, 'gas', 0, 0)  81.3 us
    pallas_call x8, Pallas kernels, run(): pl.pallas_call(kernel, out_shape=[shape(*dims) for dims in outs], in_spec...  31.9 us
    all_to_all x1, waiting for transfers between devices, swap(): return lax.all_to_all(array, 'gas', 0, 0)  16.7 us
    unnamed x25, local copies, waits for them, and re-layouts  12.9 us
    all_to_all x1, starting transfers between devices, swap(): return lax.all_to_all(array, 'gas', 0, 0)  10.3 us
    ppermute x1, waiting for transfers between devices, on_device(): from_right = lax.ppermute(left, 'space', [(j, i) for i, j in pairs])  4.39 us
  transfers between devices with their start and end apart: 5, of which 4 were waited for; matrix products, arithmetic and copies ran while one was open for 0% of the time, Pallas kernels for 0%

profile of v1, /device:TPU:2, one launch (start us, length us, event | category | flops | bytes accessed | tf_op | source)
XLA Modules:
  0.0 173.0 jit_solution(1274839154500573117)
XLA Ops:
  0.6 0.0 copy-start.3
  0.6 0.9 copy-done.3
  1.6 0.0 copy-start.4
  1.6 0.9 copy-done.4
  2.5 0.0 copy-start.5
  2.5 0.9 copy-done.5
  3.5 0.0 copy-start.6
  3.5 0.9 copy-done.6
  4.4 0.0 copy-start.7
  4.4 0.9 copy-done.7
  5.3 0.0 copy-start.8
  5.3 0.9 copy-done.8
  6.2 3.4 %collective-permute-start = (f32[18,24,128]{2,1,0:T(8,128)S(1)}, f32[18,24,128]{2,1,0:T(8,128)S(1)}, u32[]{:S(2)}, u32[]{:S(2)}) collective-permute-start(f32[18,24,128]{2,1,0:T(8,128)S(1)} %get-tuple-element.20), channel_id=1, source_target_pairs={{0,4},{1,5},{2,6},{3,7},{4,8},{5,9},{6,10},{7,11},{8,12},{9,13},{1... | collective-permute-start | bytes 663560 | tf_op jit(solution)/shard_map/ppermute | solution.py:354
  9.6 2.5 %collective-permute-start.1 = (f32[18,24,128]{2,1,0:T(8,128)S(1)}, f32[18,24,128]{2,1,0:T(8,128)S(1)}, u32[]{:S(2)}, u32[]{:S(2)}) collective-permute-start(f32[18,24,128]{2,1,0:T(8,128)S(1)} %get-tuple-element.21), channel_id=1, source_target_pairs={{4,0},{5,1},{6,2},{7,3},{8,4},{9,5},{10,6},{11,7},{12,8},{13,9},{1... | collective-permute-start | bytes 663560 | tf_op jit(solution)/shard_map/ppermute | solution.py:355
  12.1 3.2 %collective-permute-done.refs_6_ = f32[18,24,128]{2,1,0:T(8,128)S(1)} collective-permute-done((f32[18,24,128]{2,1,0:T(8,128)S(1)}, f32[18,24,128]{2,1,0:T(8,128)S(1)}, u32[]{:S(2)}, u32[]{:S(2)}) %collective-permute-start) | collective-permute-done | bytes 221216 | tf_op jit(solution)/shard_map/ppermute | solution.py:354
  15.3 3.1 %collective-permute-done.1.refs_7_ = f32[18,24,128]{2,1,0:T(8,128)S(1)} collective-permute-done((f32[18,24,128]{2,1,0:T(8,128)S(1)}, f32[18,24,128]{2,1,0:T(8,128)S(1)}, u32[]{:S(2)}, u32[]{:S(2)}) %collective-permute-start.1) | collective-permute-done | bytes 221216 | tf_op jit(solution)/shard_map/ppermute | solution.py:355
  18.4 0.8 shard_map.78
  19.2 1.3 collective-permute-start.2
  20.5 1.3 collective-permute-start.3
  21.8 0.0 collective-permute-done.2.refs_8_
  21.9 4.4 %collective-permute-done.3.refs_9_ = f32[4,176,128]{2,1,0:T(8,128)S(1)} collective-permute-done((f32[4,176,128]{2,1,0:T(8,128)S(1)}, f32[4,176,128]{2,1,0:T(8,128)S(1)}, u32[]{:S(2)}, u32[]{:S(2)}) %collective-permute-start.3) | collective-permute-done | bytes 360480 | tf_op jit(solution)/shard_map/ppermute | solution.py:359
  26.3 13.2 %shard_map.79 = (f32[5,4,2,176,128]{4,3,2,1,0:T(8,128)S(1)}, f32[4,2,176,128]{3,2,1,0:T(8,128)S(1)}, f32[4,2,192,128]{3,2,1,0:T(8,128)S(1)}, f32[4,2,192,128]{3,...) custom-call(f32[2,1,2,128,128]{4,3,2,1,0:T(8,128)S(1)} %copy-done.3, ...), custom_call_target="tpu_custom_call" | custom-call | tf_op jit(solution)/shard_map/pallas_call | solution.py:327
  39.4 0.0 copy-start
  39.4 1.7 %copy-done = f32[5,4,2,176,128]{4,3,2,1,0:T(8,128)} copy-done((f32[5,4,2,176,128]{4,3,2,1,0:T(8,128)}, f32[5,4,2,176,128]{4,3,2,1,0:T(8,128)S(1)}, u32[]{:S(2)}) %copy-start) | copy-done | bytes 3604504
  41.2 0.0 copy-start.9
  41.2 0.9 copy-done.9
  42.1 0.0 copy-start.11
  42.1 0.8 copy-done.11
  42.9 10.3 %all-to-all-start = ((f32[16,80,128]{2,1,0:T(8,128)}), f32[16,80,128]{2,1,0:T(8,128)S(1)}, u32[]{:S(2)}, u32[]{:S(2)}) async-start(f32[16,80,128]{2,1,0:T(8,128)} %copy-done.11), calls=%async_computation | async-start | bytes 1310720 | tf_op jit(solution)/shard_map/all_to_all | solution.py:345
  53.3 16.7 %all-to-all-done.parts = f32[16,80,128]{2,1,0:T(8,128)S(1)} async-done(((f32[16,80,128]{2,1,0:T(8,128)}), f32[16,80,128]{2,1,0:T(8,128)S(1)}, u32[]{:S(2)}, u32[]{:S(2)}) %all-to-all-start) | async-done | bytes 655392 | tf_op jit(solution)/shard_map/all_to_all | solution.py:345
  70.0 0.1 shard_map.80
  70.1 18.4 %all_to_all.30.chunks = f32[16,40,128]{2,1,0:T(8,128)S(1)} all-to-all(f32[16,40,128]{2,1,0:T(8,128)S(1)} %get-tuple-element.30), channel_id=1, replica_groups=mesh['gas'=16,'space'=16] {'gas'}, dimensions={0} | all-to-all | bytes 655360 | tf_op jit(solution)/shard_map/all_to_all | solution.py:345
  88.4 0.0 copy-start.1
  88.4 2.0 %copy-done.1 = f32[5,4,2,176,128]{4,3,2,1,0:T(8,128)S(1)} copy-done((f32[5,4,2,176,128]{4,3,2,1,0:T(8,128)S(1)}, f32[5,4,2,176,128]{4,3,2,1,0:T(8,128)}, u32[]{:S(2)}) %copy-start.1) | copy-done | bytes 3604504
  90.5 0.0 copy-start.10
  90.5 1.1 copy-done.10
  91.6 0.0 copy-start.2
  91.6 9.0 %shard_map.81 = (f32[4,2,192,128]{3,2,1,0:T(8,128)S(1)}, f32[16,40,128]{2,1,0:T(8,128)S(1)}) custom-call(f32[5,4,2,176,128]{4,3,2,1,0:T(8,128)S(1)} %copy-done.1, f32[4,2,176,128]{3,2,1,0:T(8,128)S(1)} %get-tuple-element.25.q, f32[4,2,192,128]{3,2,1,0:T(8,128)S(1)} %get-tuple-element.26.kap, f32[4,2,192,128]{3,2,1,0:T(8,128)S(1)} %copy-done.10, ...), custom_call_target="tpu_custom_call" | custom-call | tf_op jit(solution)/shard_map/pallas_call | solution.py:327
  100.6 18.4 %all_to_all.31.parts = f32[16,40,128]{2,1,0:T(8,128)S(1)} all-to-all(f32[16,40,128]{2,1,0:T(8,128)S(1)} %get-tuple-element.32), channel_id=1, replica_groups=mesh['gas'=16,'space'=16] {'gas'}, dimensions={0} | all-to-all | bytes 655360 | tf_op jit(solution)/shard_map/all_to_all | solution.py:345
  119.0 17.1 %all_to_all.32.chunks = f32[16,40,128]{2,1,0:T(8,128)S(1)} all-to-all(f32[16,40,128]{2,1,0:T(8,128)S(1)} %get-tuple-element.34), channel_id=1, replica_groups=mesh['gas'=16,'space'=16] {'gas'}, dimensions={0} | all-to-all | bytes 655360 | tf_op jit(solution)/shard_map/all_to_all | solution.py:345
  136.1 0.0 copy-done.2
  136.1 8.7 %shard_map.83 = (f32[2,1,2,128,128]{4,3,2,1,0:T(8,128)}, f32[16,16,128]{2,1,0:T(8,128)S(1)}) custom-call(f32[5,4,2,176,128]{4,3,2,1,0:T(8,128)S(1)} %copy-done.2, f32[4,2,176,128]{3,2,1,0:T(8,128)S(1)} %get-tuple-element.25.q, f32[4,2,192,128]{3,2,1,0:T(8,128)S(1)} %get-tuple-element.26.kap, f32[4,2,192,128]{3,2,1,0:T(8,128)S(1)} %get-tuple-element.31.now_in, ...), custom_call_target="tpu_custom_call" | custom-call | tf_op jit(solution)/shard_map/pallas_call | solution.py:327
  144.8 14.3 %all_to_all.33.parts = f32[16,16,128]{2,1,0:T(8,128)S(1)} all-to-all(f32[16,16,128]{2,1,0:T(8,128)S(1)} %get-tuple-element.35), channel_id=1, replica_groups=mesh['gas'=16,'space'=16] {'gas'}, dimensions={0} | all-to-all | bytes 262144 | tf_op jit(solution)/shard_map/all_to_all | solution.py:345
  159.2 13.1 %all_to_all.34 = f32[16,16,128]{2,1,0:T(8,128)S(1)} all-to-all(f32[16,16,128]{2,1,0:T(8,128)S(1)} %shard_map.84), channel_id=1, replica_groups=mesh['gas'=16,'space'=16] {'gas'}, dimensions={0} | all-to-all | bytes 262144 | tf_op jit(solution)/shard_map/all_to_all | solution.py:345
  172.3 0.7 copy.9
  (3 shorter events, 0.1 us)
Async XLA Ops:
  0.6 1.0 copy-start.3
  1.6 0.9 copy-start.4
  2.5 0.9 copy-start.5
  3.5 0.9 copy-start.6
  4.4 0.9 copy-start.7
  5.3 0.9 copy-start.8
  6.2 9.1 %collective-permute-start = (f32[18,24,128]{2,1,0:T(8,128)S(1)}, f32[18,24,128]{2,1,0:T(8,128)S(1)}, u32[]{:S(2)}, u32[]{:S(2)}) collective-permute-start(f32[18,24,128]{2,1,0:T(8,128)S(1)} %get-tuple-element.20), channel_id=1, source_target_pairs={{0,4},{1,5},{2,6},{3,7},{4,8},{5,9},{6,10},{7,11},{8,12},{9,13},{1... | collective-permute-start | bytes 663560 | tf_op jit(solution)/shard_map/ppermute | solution.py:354
  9.6 8.8 %collective-permute-start.1 = (f32[18,24,128]{2,1,0:T(8,128)S(1)}, f32[18,24,128]{2,1,0:T(8,128)S(1)}, u32[]{:S(2)}, u32[]{:S(2)}) collective-permute-start(f32[18,24,128]{2,1,0:T(8,128)S(1)} %get-tuple-element.21), channel_id=1, source_target_pairs={{4,0},{5,1},{6,2},{7,3},{8,4},{9,5},{10,6},{11,7},{12,8},{13,9},{1... | collective-permute-start | bytes 663560 | tf_op jit(solution)/shard_map/ppermute | solution.py:355
  19.2 2.6 %collective-permute-start.2 = (f32[4,176,128]{2,1,0:T(8,128)S(1)}, f32[4,176,128]{2,1,0:T(8,128)S(1)}, u32[]{:S(2)}, u32[]{:S(2)}) collective-permute-start(f32[4,176,128]{2,1,0:T(8,128)S(1)} %get-tuple-element.22), channel_id=1, source_target_pairs={{0,1},{1,2},{2,3},{4,5},{5,6},{6,7},{8,9},{9,10},{10,11},{12,13},{... | collective-permute-start | bytes 1081352 | tf_op jit(solution)/shard_map/ppermute | solution.py:358
  20.5 5.7 %collective-permute-start.3 = (f32[4,176,128]{2,1,0:T(8,128)S(1)}, f32[4,176,128]{2,1,0:T(8,128)S(1)}, u32[]{:S(2)}, u32[]{:S(2)}) collective-permute-start(f32[4,176,128]{2,1,0:T(8,128)S(1)} %get-tuple-element.23), channel_id=1, source_target_pairs={{1,0},{2,1},{3,2},{5,4},{6,5},{7,6},{9,8},{10,9},{11,10},{13,12},{... | collective-permute-start | bytes 1081352 | tf_op jit(solution)/shard_map/ppermute | solution.py:359
  39.4 1.8 %copy-start = (f32[5,4,2,176,128]{4,3,2,1,0:T(8,128)}, f32[5,4,2,176,128]{4,3,2,1,0:T(8,128)S(1)}, u32[]{:S(2)}) copy-start(f32[5,4,2,176,128]{4,3,2,1,0:T(8,128)S(1)} %get-tuple-element.24.a) | copy-start | bytes 10813444
  41.2 0.9 copy-start.9
  42.1 0.8 copy-start.11
  42.9 27.1 %all-to-all-start = ((f32[16,80,128]{2,1,0:T(8,128)}), f32[16,80,128]{2,1,0:T(8,128)S(1)}, u32[]{:S(2)}, u32[]{:S(2)}) async-start(f32[16,80,128]{2,1,0:T(8,128)} %copy-done.11), calls=%async_computation | async-start | bytes 1310720 | tf_op jit(solution)/shard_map/all_to_all | solution.py:345
  88.4 2.0 %copy-start.1 = (f32[5,4,2,176,128]{4,3,2,1,0:T(8,128)S(1)}, f32[5,4,2,176,128]{4,3,2,1,0:T(8,128)}, u32[]{:S(2)}) copy-start(f32[5,4,2,176,128]{4,3,2,1,0:T(8,128)} %copy-done) | copy-start | bytes 10813444
  90.5 1.1 copy-start.10
  91.6 44.5 %copy-start.2 = (f32[5,4,2,176,128]{4,3,2,1,0:T(8,128)S(1)}, f32[5,4,2,176,128]{4,3,2,1,0:T(8,128)}, u32[]{:S(2)}) copy-start(f32[5,4,2,176,128]{4,3,2,1,0:T(8,128)} %copy-done) | copy-start | bytes 10813444

commit v2 on v1

v2 whole, which is shorter than its diff:
```python
import functools

import jax
import jax.numpy as jnp
from jax import lax
from jax.experimental import pallas as pl
from jax.experimental.pallas import tpu as pltpu
from jax.sharding import PartitionSpec as P

SWEEPS = 8
OUTER = 3
LOW_BOUND = 0.05
HIGH_BOUND = 2.0

TILE = 128
HALO = SWEEPS * OUTER
ROWS = TILE + 2 * HALO
PAD = 8
STEP = 16
PLANES = 18
PACK = 5
PACKS = 4
RING = 4
MAIN = 64
FULL = 80
CHUNK = 104
SIDE = 16
VMEM_LIMIT = 16 * 1024 * 1024
F32 = jnp.float32


def sweep_weights():
    theta_mid = (HIGH_BOUND + LOW_BOUND) / 2.0
    delta_half = (HIGH_BOUND - LOW_BOUND) / 2.0
    sigma_ratio = theta_mid / delta_half
    rho_now = 1.0 / sigma_ratio
    weights = [(0.0, 1.0 / theta_mid)]
    for _ in range(SWEEPS - 1):
        rho_next = 1.0 / (2.0 * sigma_ratio - rho_now)
        weights.append((rho_next * rho_now, 2.0 * rho_next / delta_half))
        rho_now = rho_next
    return weights


def load_kernel(*refs):
    planes, up, down, sems = refs[6:]
    copies = []
    for f, ref in enumerate(refs[:6]):
        for gas in range(2 if f < 3 else 1):
            first = 4 * f + 2 * gas if f < 3 else 12 + 2 * (f - 3)
            source = ref.at[gas, 0] if f < 3 else ref.at[0]
            for row, count, out in ((TILE - HALO, HALO, up), (0, HALO, down), (0, TILE, planes)):
                copies.append(
                    pltpu.make_async_copy(
                        source.at[:, pl.ds(row, count), :], out.at[pl.ds(first, 2)], sems.at[len(copies)]
                    )
                )
    for copy in copies:
        copy.start()
    for copy in copies:
        copy.wait()


def row_parts():
    parts = [(0, HALO, "top", 0)]
    parts += [(HALO + r, 32, "own", r) for r in range(0, TILE, 32)]
    parts += [(HALO + TILE, HALO, "bottom", 0)]
    return parts


def pack_y_kernel(planes, top, bottom, right, left):
    for row, count, kind, at_row in row_parts():
        lane = lax.broadcasted_iota(jnp.int32, (count, TILE), 1)
        for t in range(PACKS):
            to_right = jnp.zeros((count, TILE), F32)
            to_left = jnp.zeros((count, TILE), F32)
            for j in range(PACK):
                p = t * PACK + j
                if p >= PLANES:
                    break
                if kind == "own":
                    value = planes[p, pl.ds(at_row, count), :]
                else:
                    value = (top if kind == "top" else bottom)[p]
                here = (lane >= HALO * j) & (lane < HALO * (j + 1))
                to_left = jnp.where(here, pltpu.roll(value, (HALO * j) % TILE, 1), to_left)
                to_right = jnp.where(here, pltpu.roll(value, (HALO * (j + 1)) % TILE, 1), to_right)
            right[t, pl.ds(row, count), :] = to_right
            left[t, pl.ds(row, count), :] = to_left


def chunk_rows(half):
    return [HALO + MAIN * half + 8 * k for k in range(8)] + ([8, 16], [ROWS - 24, ROWS - 16])[half]


def chunk_out(out, field, first=0):
    lane = lax.broadcasted_iota(jnp.int32, (8, TILE), 1)
    for c in range(RING):
        z, rows = c // 2, chunk_rows(c % 2)
        for k, row in enumerate(rows):
            out[c, pl.ds(first + 8 * k, 8), :] = field[z, 0, pl.ds(row, 8), :]
        for slot in range(3):
            packed = jnp.zeros((8, TILE), F32)
            for j, k in enumerate(range(slot, 10, 3)):
                value = pltpu.roll(field[z, 1, pl.ds(rows[k], 8), :], (SIDE + 32 * j) % TILE, 1)
                packed = jnp.where((lane >= 32 * j) & (lane < 32 * (j + 1)), value, packed)
            out[c, pl.ds(first + FULL + 8 * slot, 8), :] = packed


def chunk_in(field, chunks, change):
    for c in range(RING):
        z, rows = c // 2, chunk_rows(c % 2)
        for k, row in enumerate(rows):
            field[z, 0, pl.ds(row, 8), :] = change(chunks[c, pl.ds(8 * k, 8), :])
            packed = change(chunks[c, pl.ds(FULL + 8 * (k % 3), 8), :])
            field[z, 1, pl.ds(row, 8), :] = pltpu.roll(packed, (TILE - SIDE - 32 * (k // 3)) % TILE, 1)


def turn(me, k):
    return lax.rem(me[0] + k, RING)


def send_chunks(me, chunks, outs):
    for k, out in enumerate(outs):
        out[...] = chunks[turn(me, k)]


def gather_chunks(me, chunks, parts):
    for k, part in enumerate(parts):
        chunks[turn(me, RING - k)] = part[...]


def fourth(value):
    square = value * value
    return square * square


def left_right(own, other, lane):
    left = pltpu.roll(jnp.where(lane == TILE - 1, other, own), 1, 1)
    right = pltpu.roll(jnp.where(lane == 0, other, own), TILE - 1, 1)
    return left, right


def each_step(first, last, body):
    for r in range(first, last, STEP):
        body(r)


def solve(step, a, q, t4, sp, start, now, old):
    first, last = 8 * step, ROWS - 8 * step

    def source(r):
        for gz in range(4):
            for l in range(2):
                weight = q[gz, l, pl.ds(r, STEP), :]
                value = weight * t4[gz % 2, l, pl.ds(r, STEP), :]
                sp[gz, l, pl.ds(r, STEP), :] = jnp.where(weight > 0.0, value, 0.0)

    each_step(first, last, source)
    before, src = None, start
    for sweep, (keep, push) in enumerate(sweep_weights()):
        dst = old if sweep % 2 == 0 else now

        def body(r, src=src, dst=dst, before=before, keep=keep, push=push):
            lane = lax.broadcasted_iota(jnp.int32, (STEP, TILE), 1)
            rows = pl.ds(r, STEP)
            for g in range(2):
                own = [[src[2 * g + z, l, pl.ds(r + PAD, STEP), :] for l in range(2)] for z in range(2)]
                for z in range(2):
                    for l in range(2):
                        gz = 2 * g + z
                        here = own[z][l]
                        left, right = left_right(here, own[z][1 - l], lane)
                        total = sp[gz, l, rows, :] + a[0, gz, l, rows, :] * own[1 - z][l]
                        total += a[1, gz, l, rows, :] * src[gz, l, pl.ds(r + PAD - 1, STEP), :]
                        total += a[2, gz, l, rows, :] * src[gz, l, pl.ds(r + PAD + 1, STEP), :]
                        total += a[3, gz, l, rows, :] * left + a[4, gz, l, rows, :] * right
                        value = (1.0 + keep - push) * here + push * total
                        if before is not None:
                            value -= keep * before[gz, l, pl.ds(r + PAD, STEP), :]
                        dst[gz, l, pl.ds(r + PAD, STEP), :] = value

        each_step(first, last, body)
        before, src = src, dst


def absorb(kap, now, out):
    def body(r):
        for z in range(2):
            for l in range(2):
                rows = pl.ds(r + PAD, STEP)
                out[z, l, pl.ds(r, STEP), :] = (
                    kap[z, l, rows, :] * now[z, l, rows, :] + kap[2 + z, l, rows, :] * now[2 + z, l, rows, :]
                )

    each_step(8, ROWS - 8, body)


def first_kernel(*refs):
    planes, top, bottom, from_left, from_right, me = refs[:6]
    a, q, kap, now, held, *outs = refs[6 : 11 + RING]
    tis, sp, t4, old, begin, sums = refs[11 + RING :]
    planck = sp

    def place(p):
        if p < 4:
            return kap, p, PAD
        if p < 8:
            return q, p - 4, 0
        if p < 12:
            return begin, p - 8, PAD
        return tis, p - 12, 0

    for p in range(PLANES):
        dst, at, pad = place(p)
        dst[at, 0, pl.ds(pad, HALO), :] = top[p]
        dst[at, 0, pl.ds(pad + HALO, TILE), :] = planes[p]
        dst[at, 0, pl.ds(pad + HALO + TILE, HALO), :] = bottom[p]
    def sides(r):
        lane = lax.broadcasted_iota(jnp.int32, (STEP, TILE), 1)
        for t in range(PACKS):
            lefts = from_left[t, pl.ds(r, STEP), :]
            rights = from_right[t, pl.ds(r, STEP), :]
            for j in range(PACK):
                p = t * PACK + j
                if p >= PLANES:
                    break
                dst, at, pad = place(p)
                right = jnp.where(lane < HALO, pltpu.roll(rights, (TILE - HALO * j) % TILE, 1), 0.0)
                left = pltpu.roll(lefts, (TILE - HALO * (j + 1)) % TILE, 1)
                dst[at, 1, pl.ds(r + pad, STEP), :] = jnp.where(lane >= TILE - HALO, left, right)

    each_step(0, ROWS, sides)
    for f in range(3):
        chunk_out(sums, tis.at[pl.ds(2 * f, 2)])
        held[f] = sums[me[0], pl.ds(0, CHUNK), :]

    def coefficients(r):
        lane = lax.broadcasted_iota(jnp.int32, (STEP, TILE), 1)
        rows = pl.ds(r, STEP)
        two_thirds = 2.0 / 3.0
        for z in range(2):
            for l in range(2):
                t4[z, l, rows, :] = fourth(tis[z, l, rows, :])
                planck[z, l, rows, :] = (
                    kap[z, l, pl.ds(r + PAD, STEP), :] * q[z, l, rows, :]
                    + kap[2 + z, l, pl.ds(r + PAD, STEP), :] * q[2 + z, l, rows, :]
                )
        for g in range(2):
            own = [[kap[2 * g + z, l, pl.ds(r + PAD, STEP), :] for l in range(2)] for z in range(2)]
            between = [two_thirds / (own[0][l] + own[1][l]) for l in range(2)]
            for z in range(2):
                for l in range(2):
                    gz = 2 * g + z
                    here = own[z][l]
                    left, right = left_right(here, own[z][1 - l], lane)
                    couplings = [
                        between[l],
                        two_thirds / (here + kap[gz, l, pl.ds(r + PAD - 1, STEP), :]),
                        two_thirds / (here + kap[gz, l, pl.ds(r + PAD + 1, STEP), :]),
                        two_thirds / (here + left),
                        two_thirds / (here + right),
                    ]
                    diagonal = here + two_thirds / here
                    for coupling in couplings:
                        diagonal += coupling
                    inside = here > 0.0
                    inverse = 1.0 / diagonal
                    for f, coupling in enumerate(couplings):
                        a[f, gz, l, rows, :] = jnp.where(inside, coupling * inverse, 0.0)
                    weight = 4.0 * here * q[gz, l, rows, :] * inverse
                    q[gz, l, rows, :] = jnp.where(inside, weight, 0.0)

    each_step(0, ROWS, coefficients)
    chunk_out(sums, planck, CHUNK)
    solve(0, a, q, t4, sp, begin, now, old)
    absorb(kap, now, t4)
    chunk_out(sums, t4)
    send_chunks(me, sums, outs)


def next_kernel(a, q, kap, start, *refs):
    parts, me = refs[:RING], refs[RING]
    now, *outs = refs[RING + 1 : 2 * RING + 2]
    sp, t4, old, sums = refs[2 * RING + 2 :]
    gather_chunks(me, sums, parts)
    chunk_in(t4, sums, fourth)
    solve(1, a, q, t4, sp, start, now, old)
    absorb(kap, now, t4)
    chunk_out(sums, t4)
    send_chunks(me, sums, outs)


def last_kernel(a, q, kap, start, *refs):
    parts, me = refs[:RING], refs[RING]
    radiation, *outs = refs[RING + 1 : 2 * RING + 2]
    sp, t4, old, now, sums = refs[2 * RING + 2 :]
    gather_chunks(me, sums, parts)
    chunk_in(t4, sums, fourth)
    solve(2, a, q, t4, sp, start, now, old)
    rows = pl.ds(PAD + HALO, TILE)
    for gz in range(4):
        radiation[gz // 2, 0, gz % 2, :, :] = now[gz, 0, rows, :]
    for c in range(RING):
        z = c // 2
        part = pl.ds(PAD + HALO + MAIN * (c % 2), MAIN)
        sums[c, pl.ds(0, MAIN), :] = (
            kap[z, 0, part, :] * now[z, 0, part, :] + kap[2 + z, 0, part, :] * now[2 + z, 0, part, :]
        )
    for k, out in enumerate(outs):
        out[...] = sums[turn(me, k), pl.ds(0, MAIN), :]


def final_kernel(*refs):
    parts, me, out = refs[:RING], refs[RING], refs[RING + 1]
    gather_chunks(me, out, parts)


def corrected(current, earlier, inertia, source, emitted, taken):
    mismatch = inertia * (current - earlier) + 4.0 * emitted * fourth(current) - taken - source
    slope = inertia + 16.0 * emitted * (current * current * current)
    return jnp.where(inertia > 0.0, current - mismatch / slope, 0.0)


def call(kernel, outs, scratch=(), space=pltpu.VMEM, smem=()):
    def run(*args):
        specs = [pl.BlockSpec(memory_space=pltpu.SMEM if n in smem else space) for n in range(len(args))]
        return pl.pallas_call(
            kernel,
            out_shape=[jax.ShapeDtypeStruct(dims, F32) for dims in outs],
            in_specs=specs,
            out_specs=[pl.BlockSpec(memory_space=pltpu.VMEM)] * len(outs),
            scratch_shapes=[pltpu.VMEM(s, F32) if isinstance(s, tuple) else s for s in scratch],
            compiler_params=pltpu.CompilerParams(vmem_limit_bytes=VMEM_LIMIT),
        )(*args)

    return run


FIELD = (4, 2, ROWS, TILE)
PADDED = (4, 2, ROWS + 2 * PAD, TILE)
SHARED = (2, 2, ROWS, TILE)
TURNS = (0, 1, 3, 2)


def along_y(array, by):
    pairs = [(4 * z + y, 4 * z + (y + by) % 4) for z in range(4) for y in range(4)]
    return lax.ppermute(array, "gas", pairs)


def sum_over_gas(parts):
    total = parts[0]
    for k in TURNS[1:]:
        total = total + along_y(parts[k], k)
    total = total + lax.ppermute(total, "gas", [(4 * z + y, 4 * (z ^ 1) + y) for z in range(4) for y in range(4)])
    return total + lax.ppermute(total, "gas", [(4 * z + y, 4 * (z ^ 2) + y) for z in range(4) for y in range(4)])


def spread(chunk):
    parts = {k: along_y(chunk, k) for k in TURNS[1:]}
    return [chunk] + [parts[k] for k in range(1, RING)]


def on_device(*inputs):
    kelvin, inertia, source, extinction, fractions, irradiance = inputs
    own = (extinction, fractions, irradiance, kelvin, inertia, source)
    own = [pltpu.with_memory_space_constraint(array, pltpu.HBM) for array in own]
    devices = lax.axis_size("space")
    across = 4
    me = lax.rem(lax.axis_index("gas"), RING).reshape(1)
    planes, up, down = call(
        load_kernel,
        [(PLANES, TILE, TILE)] + [(PLANES, HALO, TILE)] * 2,
        [pltpu.SemaphoreType.DMA((27,))],
        space=pltpu.HBM,
    )(*own)
    top = lax.ppermute(up, "space", [(i, i + across) for i in range(devices - across)])
    bottom = lax.ppermute(down, "space", [(i + across, i) for i in range(devices - across)])
    right, left = call(pack_y_kernel, [(PACKS, ROWS, TILE)] * 2)(planes, top, bottom)
    pairs = [(i, i + 1) for i in range(devices) if i % across != across - 1]
    from_left = lax.ppermute(right, "space", pairs)
    from_right = lax.ppermute(left, "space", [(j, i) for i, j in pairs])
    two = (2 * CHUNK, TILE)
    a, q, kap, now, held, *parts = call(
        first_kernel,
        [(5,) + FIELD, FIELD, PADDED, PADDED, (3, CHUNK, TILE)] + [two] * RING,
        [(6, 2, ROWS, TILE), FIELD, SHARED, PADDED, PADDED, (RING,) + two],
        smem=(5,),
    )(planes, top, bottom, from_left, from_right, me)
    total = sum_over_gas(parts)
    taken, emitted = total[:CHUNK], total[CHUNK:]
    earlier, inertia, source = held[0], held[1], held[2]
    current = corrected(earlier, earlier, inertia, source, emitted, taken)
    one = (CHUNK, TILE)
    now, *parts = call(
        next_kernel, [PADDED] + [one] * RING, [FIELD, SHARED, PADDED, (RING,) + one], smem=(8,)
    )(a, q, kap, now, *spread(current), me)
    current = corrected(current, earlier, inertia, source, emitted, sum_over_gas(parts))
    radiation, *parts = call(
        last_kernel,
        [(2, 1, 2, TILE, TILE)] + [(MAIN, TILE)] * RING,
        [FIELD, SHARED, PADDED, PADDED, (RING,) + one],
        smem=(8,),
    )(a, q, kap, now, *spread(current), me)
    rest = (value[:MAIN] for value in (current, earlier, inertia, source, emitted))
    current = corrected(*rest, sum_over_gas(parts))
    (final,) = call(final_kernel, [(RING, MAIN, TILE)], smem=(RING,))(*spread(current), me)
    return final.reshape(1, 2, TILE, TILE), radiation


def solution(mesh):
    placed = (
        P("space", None, None, None),
        P("space", None, None, None),
        P("space", None, None, None),
        P("gas", "space", None, None, None),
        P("gas", "space", None, None, None),
        P("gas", "space", None, None, None),
    )
    return jax.shard_map(
        on_device,
        mesh=mesh,
        in_specs=placed,
        out_specs=(P("space", None, None, None), P("gas", "space", None, None, None)),
        check_vma=False,
    )
```

time: 174 us -> 133 us (0.76)
  the two profiles are of different devices: /device:TPU:2 before, /device:TPU:38 now
where the time goes in v2:
time: 133 us; the launch traced here: 131 us
  starting transfers between devices  58.8 us (44%)
  waiting for transfers between devices  52.8 us (40%)
  Pallas kernels  18.2 us (14%)
    ppermute x18, waiting for transfers between devices, along_y(): return lax.ppermute(array, 'gas', pairs)  28.6 us
    ppermute x18, starting transfers between devices, along_y(): return lax.ppermute(array, 'gas', pairs)  20.3 us
    ppermute x3, starting transfers between devices, sum_over_gas(): lax.ppermute(total, 'gas', [(4 * z + y, 4 * (z ^ 2) + y) for z in range(4...  19.2 us
    pallas_call x6, Pallas kernels, run(): pl.pallas_call(kernel, out_shape=[jax.ShapeDtypeStruct(dims, F32) for dim...  18.2 us
    ppermute x3, waiting for transfers between devices, sum_over_gas(): lax.ppermute(total, 'gas', [(4 * z + y, 4 * (z ^ 1) + y) for z in range(4...  8.26 us
    ppermute x3, starting transfers between devices, sum_over_gas(): lax.ppermute(total, 'gas', [(4 * z + y, 4 * (z ^ 1) + y) for z in range(4...  7.84 us
    ppermute x3, waiting for transfers between devices, sum_over_gas(): lax.ppermute(total, 'gas', [(4 * z + y, 4 * (z ^ 2) + y) for z in range(4...  6.69 us
    ppermute x1, starting transfers between devices, on_device(): lax.ppermute(down, 'space', [(i + across, i) for i in range(devices - acr...  4.56 us
  transfers between devices with their start and end apart: 28, of which 26 were waited for; matrix products, arithmetic and copies ran while one was open for 0% of the time, Pallas kernels for 0%

profile of v2, /device:TPU:38, one launch (start us, length us, event | category | flops | bytes accessed | tf_op | source)
XLA Modules:
  0.0 130.7 jit_solution(3739340259997451921)
XLA Ops:
  0.6 1.7 %shard_map.77 = (f32[18,128,128]{2,1,0:T(8,128)S(1)}, f32[18,24,128]{2,1,0:T(8,128)S(1)}, f32[18,24,128]{2,1,0:T(8,128)S(1)}) custom-call(f32[2,1,2,128,128]{4,3,2,1,0:T(8,128)} %refs_0_.1, f32[2,1,2,128,128]{4,3,2,1,0:T(8,128)} %refs_1_.1, f32[2,1,2,128,128]{4,3,2,1,0:T(8,128)} %refs_2_.1, f32[1,2,128,128]{3,2,1,0:T(8,128)} %refs_3_.1, ...), custom_call_target="tpu_custom_call" | custom-call | tf_op jit(solution)/shard_map/pallas_call | solution.py:328
  2.4 1.3 collective-permute-start
  3.7 4.6 %collective-permute-start.1 = (f32[18,24,128]{2,1,0:T(8,128)S(1)}, f32[18,24,128]{2,1,0:T(8,128)S(1)}, u32[]{:S(2)}, u32[]{:S(2)}) collective-permute-start(f32[18,24,128]{2,1,0:T(8,128)S(1)} %get-tuple-element.28), channel_id=1, source_target_pairs={{4,0},{5,1},{6,2},{7,3},{8,4},{9,5},{10,6},{11,7},{12,8},{13,9},{1... | collective-permute-start | bytes 663560 | tf_op jit(solution)/shard_map/ppermute | solution.py:378
  8.2 3.2 %collective-permute-done.top.refs_1_ = f32[18,24,128]{2,1,0:T(8,128)S(1)} collective-permute-done((f32[18,24,128]{2,1,0:T(8,128)S(1)}, f32[18,24,128]{2,1,0:T(8,128)S(1)}, u32[]{:S(2)}, u32[]{:S(2)}) %collective-permute-start) | collective-permute-done | bytes 221216 | tf_op jit(solution)/shard_map/ppermute | solution.py:377
  11.4 1.2 collective-permute-done.1.bottom.refs_2_
  12.6 0.8 shard_map.78
  13.4 1.9 %collective-permute-start.2 = (f32[4,176,128]{2,1,0:T(8,128)S(1)}, f32[4,176,128]{2,1,0:T(8,128)S(1)}, u32[]{:S(2)}, u32[]{:S(2)}) collective-permute-start(f32[4,176,128]{2,1,0:T(8,128)S(1)} %get-tuple-element.29), channel_id=1, source_target_pairs={{0,1},{1,2},{2,3},{4,5},{5,6},{6,7},{8,9},{9,10},{10,11},{12,13},{... | collective-permute-start | bytes 1081352 | tf_op jit(solution)/shard_map/ppermute | solution.py:381
  15.3 3.6 %collective-permute-start.3 = (f32[4,176,128]{2,1,0:T(8,128)S(1)}, f32[4,176,128]{2,1,0:T(8,128)S(1)}, u32[]{:S(2)}, u32[]{:S(2)}) collective-permute-start(f32[4,176,128]{2,1,0:T(8,128)S(1)} %get-tuple-element.30), channel_id=1, source_target_pairs={{1,0},{2,1},{3,2},{5,4},{6,5},{7,6},{9,8},{10,9},{11,10},{13,12},{... | collective-permute-start | bytes 1081352 | tf_op jit(solution)/shard_map/ppermute | solution.py:382
  19.0 3.2 %collective-permute-done.2.refs_3_ = f32[4,176,128]{2,1,0:T(8,128)S(1)} collective-permute-done((f32[4,176,128]{2,1,0:T(8,128)S(1)}, f32[4,176,128]{2,1,0:T(8,128)S(1)}, u32[]{:S(2)}, u32[]{:S(2)}) %collective-permute-start.2) | collective-permute-done | bytes 360480 | tf_op jit(solution)/shard_map/ppermute | solution.py:381
  22.2 1.8 %collective-permute-done.3.refs_4_ = f32[4,176,128]{2,1,0:T(8,128)S(1)} collective-permute-done((f32[4,176,128]{2,1,0:T(8,128)S(1)}, f32[4,176,128]{2,1,0:T(8,128)S(1)}, u32[]{:S(2)}, u32[]{:S(2)}) %collective-permute-start.3) | collective-permute-done | bytes 360480 | tf_op jit(solution)/shard_map/ppermute | solution.py:382
  23.9 6.5 %shard_map.79 = (f32[5,4,2,176,128]{4,3,2,1,0:T(8,128)S(1)}, f32[4,2,176,128]{3,2,1,0:T(8,128)S(1)}, f32[4,2,192,128]{3,2,1,0:T(8,128)S(1)}, f32[4,2,192,128]{3,...) custom-call(f32[18,128,128]{2,1,0:T(8,128)S(1)} %get-tuple-element.2, ...), custom_call_target="tpu_custom_call" | custom-call | tf_op jit(solution)/shard_map/pallas_call | solution.py:328
  30.4 1.7 %collective-permute-start.4 = (f32[208,128]{1,0:T(8,128)S(1)}, f32[208,128]{1,0:T(8,128)S(1)}, u32[]{:S(2)}, u32[]{:S(2)}) collective-permute-start(f32[208,128]{1,0:T(8,128)S(1)} %get-tuple-element.33), channel_id=1, source_target_pairs={{0,16},{16,32},{32,48},{48,0},{64,80},{80,96},{96,112},{112,64},{1... | collective-permute-start | bytes 319496 | tf_op jit(solution)/shard_map/ppermute | solution.py:348
  32.0 1.7 %collective-permute-start.5 = (f32[208,128]{1,0:T(8,128)S(1)}, f32[208,128]{1,0:T(8,128)S(1)}, u32[]{:S(2)}, u32[]{:S(2)}) collective-permute-start(f32[208,128]{1,0:T(8,128)S(1)} %get-tuple-element.34), channel_id=1, source_target_pairs={{0,48},{16,0},{32,16},{48,32},{64,112},{80,64},{96,80},{112,96},{1... | collective-permute-start | bytes 319496 | tf_op jit(solution)/shard_map/ppermute | solution.py:348
  33.7 2.0 %collective-permute-start.6 = (f32[208,128]{1,0:T(8,128)S(1)}, f32[208,128]{1,0:T(8,128)S(1)}, u32[]{:S(2)}, u32[]{:S(2)}) collective-permute-start(f32[208,128]{1,0:T(8,128)S(1)} %get-tuple-element.35), channel_id=1, source_target_pairs={{0,32},{16,48},{32,0},{48,16},{64,96},{80,112},{96,64},{112,80},{1... | collective-permute-start | bytes 319496 | tf_op jit(solution)/shard_map/ppermute | solution.py:348
  36.8 3.2 %collective-permute-done.6 = f32[208,128]{1,0:T(8,128)S(1)} collective-permute-done((f32[208,128]{1,0:T(8,128)S(1)}, f32[208,128]{1,0:T(8,128)S(1)}, u32[]{:S(2)}, u32[]{:S(2)}) %collective-permute-start.6) | collective-permute-done | bytes 106528 | tf_op jit(solution)/shard_map/ppermute | solution.py:348
  39.9 3.4 %collective-permute-start.7 = (f32[208,128]{1,0:T(8,128)S(1)}, f32[208,128]{1,0:T(8,128)S(1)}, u32[]{:S(2)}, u32[]{:S(2)}) collective-permute-start(f32[208,128]{1,0:T(8,128)S(1)} %add_add_fusion), channel_id=1, source_target_pairs={{0,64},{16,80},{32,96},{48,112},{64,0},{80,16},{96,32},{112,48},{1... | collective-permute-start | bytes 319496 | tf_op jit(solution)/shard_map/ppermute | solution.py:355
  43.3 2.7 %collective-permute-done.7 = f32[208,128]{1,0:T(8,128)S(1)} collective-permute-done((f32[208,128]{1,0:T(8,128)S(1)}, f32[208,128]{1,0:T(8,128)S(1)}, u32[]{:S(2)}, u32[]{:S(2)}) %collective-permute-start.7) | collective-permute-done | bytes 106528 | tf_op jit(solution)/shard_map/ppermute | solution.py:355
  46.0 7.1 %collective-permute-start.8 = (f32[208,128]{1,0:T(8,128)S(1)}, f32[208,128]{1,0:T(8,128)S(1)}, u32[]{:S(2)}, u32[]{:S(2)}) collective-permute-start(f32[208,128]{1,0:T(8,128)S(1)} %add.66), channel_id=1, source_target_pairs={{0,128},{16,144},{32,160},{48,176},{64,192},{80,208},{96,224},{112... | collective-permute-start | bytes 319496 | tf_op jit(solution)/shard_map/ppermute | solution.py:356
  53.2 2.7 %collective-permute-done.8 = f32[208,128]{1,0:T(8,128)S(1)} collective-permute-done((f32[208,128]{1,0:T(8,128)S(1)}, f32[208,128]{1,0:T(8,128)S(1)}, u32[]{:S(2)}, u32[]{:S(2)}) %collective-permute-start.8) | collective-permute-done | bytes 106528 | tf_op jit(solution)/shard_map/ppermute | solution.py:356
  55.9 1.9 %collective-permute-start.11 = (f32[104,128]{1,0:T(8,128)S(1)}, f32[104,128]{1,0:T(8,128)S(1)}, u32[]{:S(2)}, u32[]{:S(2)}) collective-permute-start(f32[104,128]{1,0:T(8,128)S(1)} %fusion.6.refs_0_), channel_id=1, source_target_pairs={{0,48},{16,0},{32,16},{48,32},{64,112},{80,64},{96,80},{112,96},{1... | collective-permute-start | bytes 159752 | tf_op jit(solution)/shard_map/ppermute | solution.py:348
  58.4 1.0 collective-permute-start.9
  59.4 0.7 collective-permute-done.11.refs_3_
  60.1 3.3 %collective-permute-done.10.refs_2_ = f32[104,128]{1,0:T(8,128)S(1)} collective-permute-done((f32[104,128]{1,0:T(8,128)S(1)}, f32[104,128]{1,0:T(8,128)S(1)}, u32[]{:S(2)}, u32[]{:S(2)}) %collective-permute-start.10) | collective-permute-done | bytes 53280 | tf_op jit(solution)/shard_map/ppermute | solution.py:348
  64.0 4.2 %shard_map.80 = (f32[4,2,192,128]{3,2,1,0:T(8,128)S(1)}, f32[104,128]{1,0:T(8,128)S(1)}, f32[104,128]{1,0:T(8,128)S(1)}, f32[104,128]{1,0:T(8,128)S(1)}, f32[104,128]{1,0:T(8,128)S(1)}) custom-call(f32[5,4,2,176,128]{4,3,2,1,0:T(8,128)S(1)} %get-tuple-element.36.a, f32[4,2,176,128]{3,2,1,0:T(8,128)S(1)} %get-tuple-element.37.q, ...), custom_call_target="tpu_custom_call" | custom-call | tf_op jit(solution)/shard_map/pallas_call | solution.py:328
  68.3 3.2 %collective-permute-start.13 = (f32[104,128]{1,0:T(8,128)S(1)}, f32[104,128]{1,0:T(8,128)S(1)}, u32[]{:S(2)}, u32[]{:S(2)}) collective-permute-start(f32[104,128]{1,0:T(8,128)S(1)} %get-tuple-element.42), channel_id=1, source_target_pairs={{0,48},{16,0},{32,16},{48,32},{64,112},{80,64},{96,80},{112,96},{1... | collective-permute-start | bytes 159752 | tf_op jit(solution)/shard_map/ppermute | solution.py:348
  72.1 1.6 %collective-permute-done.12 = f32[104,128]{1,0:T(8,128)S(1)} collective-permute-done((f32[104,128]{1,0:T(8,128)S(1)}, f32[104,128]{1,0:T(8,128)S(1)}, u32[]{:S(2)}, u32[]{:S(2)}) %collective-permute-start.12) | collective-permute-done | bytes 53280 | tf_op jit(solution)/shard_map/ppermute | solution.py:348
  73.6 3.5 %collective-permute-done.14 = f32[104,128]{1,0:T(8,128)S(1)} collective-permute-done((f32[104,128]{1,0:T(8,128)S(1)}, f32[104,128]{1,0:T(8,128)S(1)}, u32[]{:S(2)}, u32[]{:S(2)}) %collective-permute-start.14) | collective-permute-done | bytes 53280 | tf_op jit(solution)/shard_map/ppermute | solution.py:348
  77.2 2.1 %collective-permute-start.15 = (f32[104,128]{1,0:T(8,128)S(1)}, f32[104,128]{1,0:T(8,128)S(1)}, u32[]{:S(2)}, u32[]{:S(2)}) collective-permute-start(f32[104,128]{1,0:T(8,128)S(1)} %add_add_fusion.1), channel_id=1, source_target_pairs={{0,64},{16,80},{32,96},{48,112},{64,0},{80,16},{96,32},{112,48},{1... | collective-permute-start | bytes 159752 | tf_op jit(solution)/shard_map/ppermute | solution.py:355
  79.2 3.1 %collective-permute-done.15 = f32[104,128]{1,0:T(8,128)S(1)} collective-permute-done((f32[104,128]{1,0:T(8,128)S(1)}, f32[104,128]{1,0:T(8,128)S(1)}, u32[]{:S(2)}, u32[]{:S(2)}) %collective-permute-start.15) | collective-permute-done | bytes 53280 | tf_op jit(solution)/shard_map/ppermute | solution.py:355
  82.3 6.0 %collective-permute-start.16 = (f32[104,128]{1,0:T(8,128)S(1)}, f32[104,128]{1,0:T(8,128)S(1)}, u32[]{:S(2)}, u32[]{:S(2)}) collective-permute-start(f32[104,128]{1,0:T(8,128)S(1)} %add.74), channel_id=1, source_target_pairs={{0,128},{16,144},{32,160},{48,176},{64,192},{80,208},{96,224},{112... | collective-permute-start | bytes 159752 | tf_op jit(solution)/shard_map/ppermute | solution.py:356
  88.3 2.1 %collective-permute-done.16 = f32[104,128]{1,0:T(8,128)S(1)} collective-permute-done((f32[104,128]{1,0:T(8,128)S(1)}, f32[104,128]{1,0:T(8,128)S(1)}, u32[]{:S(2)}, u32[]{:S(2)}) %collective-permute-start.16) | collective-permute-done | bytes 53280 | tf_op jit(solution)/shard_map/ppermute | solution.py:356
  91.6 1.0 collective-permute-start.17
  92.6 2.1 %collective-permute-done.19.refs_3_ = f32[104,128]{1,0:T(8,128)S(1)} collective-permute-done((f32[104,128]{1,0:T(8,128)S(1)}, f32[104,128]{1,0:T(8,128)S(1)}, u32[]{:S(2)}, u32[]{:S(2)}) %collective-permute-start.19) | collective-permute-done | bytes 53280 | tf_op jit(solution)/shard_map/ppermute | solution.py:348
  94.7 1.8 %collective-permute-done.18.refs_2_ = f32[104,128]{1,0:T(8,128)S(1)} collective-permute-done((f32[104,128]{1,0:T(8,128)S(1)}, f32[104,128]{1,0:T(8,128)S(1)}, u32[]{:S(2)}, u32[]{:S(2)}) %collective-permute-start.18) | collective-permute-done | bytes 53280 | tf_op jit(solution)/shard_map/ppermute | solution.py:348
  96.5 0.8 collective-permute-done.17.refs_1_
  97.4 4.3 %shard_map.81 = (f32[2,1,2,128,128]{4,3,2,1,0:T(8,128)}, f32[64,128]{1,0:T(8,128)S(1)}, f32[64,128]{1,0:T(8,128)S(1)}, f32[64,128]{1,0:T(8,128)S(1)}, f32[64,128]{1,0:T(8,128)S(1)}) custom-call(f32[5,4,2,176,128]{4,3,2,1,0:T(8,128)S(1)} %get-tuple-element.36.a, f32[4,2,176,128]{3,2,1,0:T(8,128)S(1)} %get-tuple-element.37.q, ...), custom_call_target="tpu_custom_call" | custom-call | tf_op jit(solution)/shard_map/pallas_call | solution.py:328
  101.7 0.9 collective-permute-start.20
  102.6 2.4 %collective-permute-start.21 = (f32[64,128]{1,0:T(8,128)S(1)}, f32[64,128]{1,0:T(8,128)S(1)}, u32[]{:S(2)}, u32[]{:S(2)}) collective-permute-start(f32[64,128]{1,0:T(8,128)S(1)} %get-tuple-element.47), channel_id=1, source_target_pairs={{0,48},{16,0},{32,16},{48,32},{64,112},{80,64},{96,80},{112,96},{1... | collective-permute-start | bytes 98312 | tf_op jit(solution)/shard_map/ppermute | solution.py:348
  105.2 1.6 %collective-permute-done.20 = f32[64,128]{1,0:T(8,128)S(1)} collective-permute-done((f32[64,128]{1,0:T(8,128)S(1)}, f32[64,128]{1,0:T(8,128)S(1)}, u32[]{:S(2)}, u32[]{:S(2)}) %collective-permute-start.20) | collective-permute-done | bytes 32800 | tf_op jit(solution)/shard_map/ppermute | solution.py:348
  106.8 3.5 %collective-permute-done.22 = f32[64,128]{1,0:T(8,128)S(1)} collective-permute-done((f32[64,128]{1,0:T(8,128)S(1)}, f32[64,128]{1,0:T(8,128)S(1)}, u32[]{:S(2)}, u32[]{:S(2)}) %collective-permute-start.22) | collective-permute-done | bytes 32800 | tf_op jit(solution)/shard_map/ppermute | solution.py:348
  110.4 2.4 %collective-permute-start.23 = (f32[64,128]{1,0:T(8,128)S(1)}, f32[64,128]{1,0:T(8,128)S(1)}, u32[]{:S(2)}, u32[]{:S(2)}) collective-permute-start(f32[64,128]{1,0:T(8,128)S(1)} %add_add_fusion.2), channel_id=1, source_target_pairs={{0,64},{16,80},{32,96},{48,112},{64,0},{80,16},{96,32},{112,48},{1... | collective-permute-start | bytes 98312 | tf_op jit(solution)/shard_map/ppermute | solution.py:355
  112.8 2.5 %collective-permute-done.23 = f32[64,128]{1,0:T(8,128)S(1)} collective-permute-done((f32[64,128]{1,0:T(8,128)S(1)}, f32[64,128]{1,0:T(8,128)S(1)}, u32[]{:S(2)}, u32[]{:S(2)}) %collective-permute-start.23) | collective-permute-done | bytes 32800 | tf_op jit(solution)/shard_map/ppermute | solution.py:355
  115.3 6.0 %collective-permute-start.24 = (f32[64,128]{1,0:T(8,128)S(1)}, f32[64,128]{1,0:T(8,128)S(1)}, u32[]{:S(2)}, u32[]{:S(2)}) collective-permute-start(f32[64,128]{1,0:T(8,128)S(1)} %add.81), channel_id=1, source_target_pairs={{0,128},{16,144},{32,160},{48,176},{64,192},{80,208},{96,224},{112... | collective-permute-start | bytes 98312 | tf_op jit(solution)/shard_map/ppermute | solution.py:356
  121.3 1.9 %collective-permute-done.24 = f32[64,128]{1,0:T(8,128)S(1)} collective-permute-done((f32[64,128]{1,0:T(8,128)S(1)}, f32[64,128]{1,0:T(8,128)S(1)}, u32[]{:S(2)}, u32[]{:S(2)}) %collective-permute-start.24) | collective-permute-done | bytes 32800 | tf_op jit(solution)/shard_map/ppermute | solution.py:356
  123.3 0.8 collective-permute-start.27
  124.1 0.9 collective-permute-start.26
  125.4 1.9 %collective-permute-done.27.refs_3_ = f32[64,128]{1,0:T(8,128)S(1)} collective-permute-done((f32[64,128]{1,0:T(8,128)S(1)}, f32[64,128]{1,0:T(8,128)S(1)}, u32[]{:S(2)}, u32[]{:S(2)}) %collective-permute-start.27) | collective-permute-done | bytes 32800 | tf_op jit(solution)/shard_map/ppermute | solution.py:348
  127.2 2.2 %collective-permute-done.26.refs_2_ = f32[64,128]{1,0:T(8,128)S(1)} collective-permute-done((f32[64,128]{1,0:T(8,128)S(1)}, f32[64,128]{1,0:T(8,128)S(1)}, u32[]{:S(2)}, u32[]{:S(2)}) %collective-permute-start.26) | collective-permute-done | bytes 32800 | tf_op jit(solution)/shard_map/ppermute | solution.py:348
  (24 shorter events, 6.0 us)
Async XLA Ops:
  2.4 9.1 %collective-permute-start = (f32[18,24,128]{2,1,0:T(8,128)S(1)}, f32[18,24,128]{2,1,0:T(8,128)S(1)}, u32[]{:S(2)}, u32[]{:S(2)}) collective-permute-start(f32[18,24,128]{2,1,0:T(8,128)S(1)} %get-tuple-element.27), channel_id=1, source_target_pairs={{0,4},{1,5},{2,6},{3,7},{4,8},{5,9},{6,10},{7,11},{8,12},{9,13},{1... | collective-permute-start | bytes 663560 | tf_op jit(solution)/shard_map/ppermute | solution.py:377
  3.7 8.9 %collective-permute-start.1 = (f32[18,24,128]{2,1,0:T(8,128)S(1)}, f32[18,24,128]{2,1,0:T(8,128)S(1)}, u32[]{:S(2)}, u32[]{:S(2)}) collective-permute-start(f32[18,24,128]{2,1,0:T(8,128)S(1)} %get-tuple-element.28), channel_id=1, source_target_pairs={{4,0},{5,1},{6,2},{7,3},{8,4},{9,5},{10,6},{11,7},{12,8},{13,9},{1... | collective-permute-start | bytes 663560 | tf_op jit(solution)/shard_map/ppermute | solution.py:378
  13.4 8.7 %collective-permute-start.2 = (f32[4,176,128]{2,1,0:T(8,128)S(1)}, f32[4,176,128]{2,1,0:T(8,128)S(1)}, u32[]{:S(2)}, u32[]{:S(2)}) collective-permute-start(f32[4,176,128]{2,1,0:T(8,128)S(1)} %get-tuple-element.29), channel_id=1, source_target_pairs={{0,1},{1,2},{2,3},{4,5},{5,6},{6,7},{8,9},{9,10},{10,11},{12,13},{... | collective-permute-start | bytes 1081352 | tf_op jit(solution)/shard_map/ppermute | solution.py:381
  15.3 8.6 %collective-permute-start.3 = (f32[4,176,128]{2,1,0:T(8,128)S(1)}, f32[4,176,128]{2,1,0:T(8,128)S(1)}, u32[]{:S(2)}, u32[]{:S(2)}) collective-permute-start(f32[4,176,128]{2,1,0:T(8,128)S(1)} %get-tuple-element.30), channel_id=1, source_target_pairs={{1,0},{2,1},{3,2},{5,4},{6,5},{7,6},{9,8},{10,9},{11,10},{13,12},{... | collective-permute-start | bytes 1081352 | tf_op jit(solution)/shard_map/ppermute | solution.py:382
  30.4 6.0 %collective-permute-start.4 = (f32[208,128]{1,0:T(8,128)S(1)}, f32[208,128]{1,0:T(8,128)S(1)}, u32[]{:S(2)}, u32[]{:S(2)}) collective-permute-start(f32[208,128]{1,0:T(8,128)S(1)} %get-tuple-element.33), channel_id=1, source_target_pairs={{0,16},{16,32},{32,48},{48,0},{64,80},{80,96},{96,112},{112,64},{1... | collective-permute-start | bytes 319496 | tf_op jit(solution)/shard_map/ppermute | solution.py:348
  32.0 4.7 %collective-permute-start.5 = (f32[208,128]{1,0:T(8,128)S(1)}, f32[208,128]{1,0:T(8,128)S(1)}, u32[]{:S(2)}, u32[]{:S(2)}) collective-permute-start(f32[208,128]{1,0:T(8,128)S(1)} %get-tuple-element.34), channel_id=1, source_target_pairs={{0,48},{16,0},{32,16},{48,32},{64,112},{80,64},{96,80},{112,96},{1... | collective-permute-start | bytes 319496 | tf_op jit(solution)/shard_map/ppermute | solution.py:348
  33.7 6.2 %collective-permute-start.6 = (f32[208,128]{1,0:T(8,128)S(1)}, f32[208,128]{1,0:T(8,128)S(1)}, u32[]{:S(2)}, u32[]{:S(2)}) collective-permute-start(f32[208,128]{1,0:T(8,128)S(1)} %get-tuple-element.35), channel_id=1, source_target_pairs={{0,32},{16,48},{32,0},{48,16},{64,96},{80,112},{96,64},{112,80},{1... | collective-permute-start | bytes 319496 | tf_op jit(solution)/shard_map/ppermute | solution.py:348
  39.9 6.1 %collective-permute-start.7 = (f32[208,128]{1,0:T(8,128)S(1)}, f32[208,128]{1,0:T(8,128)S(1)}, u32[]{:S(2)}, u32[]{:S(2)}) collective-permute-start(f32[208,128]{1,0:T(8,128)S(1)} %add_add_fusion), channel_id=1, source_target_pairs={{0,64},{16,80},{32,96},{48,112},{64,0},{80,16},{96,32},{112,48},{1... | collective-permute-start | bytes 319496 | tf_op jit(solution)/shard_map/ppermute | solution.py:355
  46.0 9.8 %collective-permute-start.8 = (f32[208,128]{1,0:T(8,128)S(1)}, f32[208,128]{1,0:T(8,128)S(1)}, u32[]{:S(2)}, u32[]{:S(2)}) collective-permute-start(f32[208,128]{1,0:T(8,128)S(1)} %add.66), channel_id=1, source_target_pairs={{0,128},{16,144},{32,160},{48,176},{64,192},{80,208},{96,224},{112... | collective-permute-start | bytes 319496 | tf_op jit(solution)/shard_map/ppermute | solution.py:356
  55.9 4.2 %collective-permute-start.11 = (f32[104,128]{1,0:T(8,128)S(1)}, f32[104,128]{1,0:T(8,128)S(1)}, u32[]{:S(2)}, u32[]{:S(2)}) collective-permute-start(f32[104,128]{1,0:T(8,128)S(1)} %fusion.6.refs_0_), channel_id=1, source_target_pairs={{0,48},{16,0},{32,16},{48,32},{64,112},{80,64},{96,80},{112,96},{1... | collective-permute-start | bytes 159752 | tf_op jit(solution)/shard_map/ppermute | solution.py:348
  57.8 5.7 %collective-permute-start.10 = (f32[104,128]{1,0:T(8,128)S(1)}, f32[104,128]{1,0:T(8,128)S(1)}, u32[]{:S(2)}, u32[]{:S(2)}) collective-permute-start(f32[104,128]{1,0:T(8,128)S(1)} %fusion.6.refs_0_), channel_id=1, source_target_pairs={{0,32},{16,48},{32,0},{48,16},{64,96},{80,112},{96,64},{112,80},{1... | collective-permute-start | bytes 159752 | tf_op jit(solution)/shard_map/ppermute | solution.py:348
  58.4 5.6 %collective-permute-start.9 = (f32[104,128]{1,0:T(8,128)S(1)}, f32[104,128]{1,0:T(8,128)S(1)}, u32[]{:S(2)}, u32[]{:S(2)}) collective-permute-start(f32[104,128]{1,0:T(8,128)S(1)} %fusion.6.refs_0_), channel_id=1, source_target_pairs={{0,16},{16,32},{32,48},{48,0},{64,80},{80,96},{96,112},{112,64},{1... | collective-permute-start | bytes 159752 | tf_op jit(solution)/shard_map/ppermute | solution.py:348
  68.2 5.4 %collective-permute-start.12 = (f32[104,128]{1,0:T(8,128)S(1)}, f32[104,128]{1,0:T(8,128)S(1)}, u32[]{:S(2)}, u32[]{:S(2)}) collective-permute-start(f32[104,128]{1,0:T(8,128)S(1)} %get-tuple-element.41), channel_id=1, source_target_pairs={{0,16},{16,32},{32,48},{48,0},{64,80},{80,96},{96,112},{112,64},{1... | collective-permute-start | bytes 159752 | tf_op jit(solution)/shard_map/ppermute | solution.py:348
  68.3 5.3 %collective-permute-start.13 = (f32[104,128]{1,0:T(8,128)S(1)}, f32[104,128]{1,0:T(8,128)S(1)}, u32[]{:S(2)}, u32[]{:S(2)}) collective-permute-start(f32[104,128]{1,0:T(8,128)S(1)} %get-tuple-element.42), channel_id=1, source_target_pairs={{0,48},{16,0},{32,16},{48,32},{64,112},{80,64},{96,80},{112,96},{1... | collective-permute-start | bytes 159752 | tf_op jit(solution)/shard_map/ppermute | solution.py:348
  71.5 5.6 %collective-permute-start.14 = (f32[104,128]{1,0:T(8,128)S(1)}, f32[104,128]{1,0:T(8,128)S(1)}, u32[]{:S(2)}, u32[]{:S(2)}) collective-permute-start(f32[104,128]{1,0:T(8,128)S(1)} %get-tuple-element.43), channel_id=1, source_target_pairs={{0,32},{16,48},{32,0},{48,16},{64,96},{80,112},{96,64},{112,80},{1... | collective-permute-start | bytes 159752 | tf_op jit(solution)/shard_map/ppermute | solution.py:348
  77.2 5.1 %collective-permute-start.15 = (f32[104,128]{1,0:T(8,128)S(1)}, f32[104,128]{1,0:T(8,128)S(1)}, u32[]{:S(2)}, u32[]{:S(2)}) collective-permute-start(f32[104,128]{1,0:T(8,128)S(1)} %add_add_fusion.1), channel_id=1, source_target_pairs={{0,64},{16,80},{32,96},{48,112},{64,0},{80,16},{96,32},{112,48},{1... | collective-permute-start | bytes 159752 | tf_op jit(solution)/shard_map/ppermute | solution.py:355
  82.3 8.1 %collective-permute-start.16 = (f32[104,128]{1,0:T(8,128)S(1)}, f32[104,128]{1,0:T(8,128)S(1)}, u32[]{:S(2)}, u32[]{:S(2)}) collective-permute-start(f32[104,128]{1,0:T(8,128)S(1)} %add.74), channel_id=1, source_target_pairs={{0,128},{16,144},{32,160},{48,176},{64,192},{80,208},{96,224},{112... | collective-permute-start | bytes 159752 | tf_op jit(solution)/shard_map/ppermute | solution.py:356
  90.5 4.2 %collective-permute-start.19 = (f32[104,128]{1,0:T(8,128)S(1)}, f32[104,128]{1,0:T(8,128)S(1)}, u32[]{:S(2)}, u32[]{:S(2)}) collective-permute-start(f32[104,128]{1,0:T(8,128)S(1)} %fusion.15.refs_0_), channel_id=1, source_target_pairs={{0,48},{16,0},{32,16},{48,32},{64,112},{80,64},{96,80},{112,96},{1... | collective-permute-start | bytes 159752 | tf_op jit(solution)/shard_map/ppermute | solution.py:348
  90.8 5.7 %collective-permute-start.18 = (f32[104,128]{1,0:T(8,128)S(1)}, f32[104,128]{1,0:T(8,128)S(1)}, u32[]{:S(2)}, u32[]{:S(2)}) collective-permute-start(f32[104,128]{1,0:T(8,128)S(1)} %fusion.15.refs_0_), channel_id=1, source_target_pairs={{0,32},{16,48},{32,0},{48,16},{64,96},{80,112},{96,64},{112,80},{1... | collective-permute-start | bytes 159752 | tf_op jit(solution)/shard_map/ppermute | solution.py:348
  91.6 5.8 %collective-permute-start.17 = (f32[104,128]{1,0:T(8,128)S(1)}, f32[104,128]{1,0:T(8,128)S(1)}, u32[]{:S(2)}, u32[]{:S(2)}) collective-permute-start(f32[104,128]{1,0:T(8,128)S(1)} %fusion.15.refs_0_), channel_id=1, source_target_pairs={{0,16},{16,32},{32,48},{48,0},{64,80},{80,96},{96,112},{112,64},{1... | collective-permute-start | bytes 159752 | tf_op jit(solution)/shard_map/ppermute | solution.py:348
  101.7 5.1 %collective-permute-start.20 = (f32[64,128]{1,0:T(8,128)S(1)}, f32[64,128]{1,0:T(8,128)S(1)}, u32[]{:S(2)}, u32[]{:S(2)}) collective-permute-start(f32[64,128]{1,0:T(8,128)S(1)} %get-tuple-element.46), channel_id=1, source_target_pairs={{0,16},{16,32},{32,48},{48,0},{64,80},{80,96},{96,112},{112,64},{1... | collective-permute-start | bytes 98312 | tf_op jit(solution)/shard_map/ppermute | solution.py:348
  102.6 4.3 %collective-permute-start.21 = (f32[64,128]{1,0:T(8,128)S(1)}, f32[64,128]{1,0:T(8,128)S(1)}, u32[]{:S(2)}, u32[]{:S(2)}) collective-permute-start(f32[64,128]{1,0:T(8,128)S(1)} %get-tuple-element.47), channel_id=1, source_target_pairs={{0,48},{16,0},{32,16},{48,32},{64,112},{80,64},{96,80},{112,96},{1... | collective-permute-start | bytes 98312 | tf_op jit(solution)/shard_map/ppermute | solution.py:348
  105.0 5.4 %collective-permute-start.22 = (f32[64,128]{1,0:T(8,128)S(1)}, f32[64,128]{1,0:T(8,128)S(1)}, u32[]{:S(2)}, u32[]{:S(2)}) collective-permute-start(f32[64,128]{1,0:T(8,128)S(1)} %get-tuple-element.48), channel_id=1, source_target_pairs={{0,32},{16,48},{32,0},{48,16},{64,96},{80,112},{96,64},{112,80},{1... | collective-permute-start | bytes 98312 | tf_op jit(solution)/shard_map/ppermute | solution.py:348
  110.4 4.9 %collective-permute-start.23 = (f32[64,128]{1,0:T(8,128)S(1)}, f32[64,128]{1,0:T(8,128)S(1)}, u32[]{:S(2)}, u32[]{:S(2)}) collective-permute-start(f32[64,128]{1,0:T(8,128)S(1)} %add_add_fusion.2), channel_id=1, source_target_pairs={{0,64},{16,80},{32,96},{48,112},{64,0},{80,16},{96,32},{112,48},{1... | collective-permute-start | bytes 98312 | tf_op jit(solution)/shard_map/ppermute | solution.py:355
  115.3 7.9 %collective-permute-start.24 = (f32[64,128]{1,0:T(8,128)S(1)}, f32[64,128]{1,0:T(8,128)S(1)}, u32[]{:S(2)}, u32[]{:S(2)}) collective-permute-start(f32[64,128]{1,0:T(8,128)S(1)} %add.81), channel_id=1, source_target_pairs={{0,128},{16,144},{32,160},{48,176},{64,192},{80,208},{96,224},{112... | collective-permute-start | bytes 98312 | tf_op jit(solution)/shard_map/ppermute | solution.py:356
  123.3 4.0 %collective-permute-start.27 = (f32[64,128]{1,0:T(8,128)S(1)}, f32[64,128]{1,0:T(8,128)S(1)}, u32[]{:S(2)}, u32[]{:S(2)}) collective-permute-start(f32[64,128]{1,0:T(8,128)S(1)} %fusion.26.refs_0_), channel_id=1, source_target_pairs={{0,48},{16,0},{32,16},{48,32},{64,112},{80,64},{96,80},{112,96},{1... | collective-permute-start | bytes 98312 | tf_op jit(solution)/shard_map/ppermute | solution.py:348
  124.1 5.4 %collective-permute-start.26 = (f32[64,128]{1,0:T(8,128)S(1)}, f32[64,128]{1,0:T(8,128)S(1)}, u32[]{:S(2)}, u32[]{:S(2)}) collective-permute-start(f32[64,128]{1,0:T(8,128)S(1)} %fusion.26.refs_0_), channel_id=1, source_target_pairs={{0,32},{16,48},{32,0},{48,16},{64,96},{80,112},{96,64},{112,80},{1... | collective-permute-start | bytes 98312 | tf_op jit(solution)/shard_map/ppermute | solution.py:348
  124.9 5.1 %collective-permute-start.25 = (f32[64,128]{1,0:T(8,128)S(1)}, f32[64,128]{1,0:T(8,128)S(1)}, u32[]{:S(2)}, u32[]{:S(2)}) collective-permute-start(f32[64,128]{1,0:T(8,128)S(1)} %fusion.26.refs_0_), channel_id=1, source_target_pairs={{0,16},{16,32},{32,48},{48,0},{64,80},{80,96},{96,112},{112,64},{1... | collective-permute-start | bytes 98312 | tf_op jit(solution)/shard_map/ppermute | solution.py:348

commit v3 on v2

v3 whole, which is shorter than its diff:
```python
import functools

import jax
import jax.numpy as jnp
from jax import lax
from jax.experimental import pallas as pl
from jax.experimental.pallas import tpu as pltpu
from jax.sharding import PartitionSpec as P

SWEEPS = 8
OUTER = 3
LOW_BOUND = 0.05
HIGH_BOUND = 2.0

TILE = 128
HALO = SWEEPS * OUTER
ROWS = TILE + 2 * HALO
PAD = 8
STEP = 16
PLANES = 16
PACKS = 3
ACROSS = 4
RING = 4
MAIN = 64
FULL = 80
CHUNK = 104
SIDE = 16
VMEM_LIMIT = 16 * 1024 * 1024
F32 = jnp.float32


def sweep_weights():
    theta_mid = (HIGH_BOUND + LOW_BOUND) / 2.0
    delta_half = (HIGH_BOUND - LOW_BOUND) / 2.0
    sigma_ratio = theta_mid / delta_half
    rho_now = 1.0 / sigma_ratio
    weights = [(0.0, 1.0 / theta_mid)]
    for _ in range(SWEEPS - 1):
        rho_next = 1.0 / (2.0 * sigma_ratio - rho_now)
        weights.append((rho_next * rho_now, 2.0 * rho_next / delta_half))
        rho_now = rho_next
    return weights


def place_in_space():
    place = lax.axis_index("space")
    return place >> 2, place & 3


def owner():
    return lax.axis_index("gas") & 3


def load_kernel(*refs):
    planes, up, down, sems = refs[6:]
    copies = []
    sources = [(refs[f].at[gas, 0], 4 * f + 2 * gas, 2) for f in range(3) for gas in range(2)]
    sources.append((refs[3].at[0], 12, 2))
    layer = owner() >> 1
    sources += [(refs[4 + f].at[0, pl.ds(layer, 1)], 14 + f, 1) for f in range(2)]
    for source, first, layers in sources:
        for row, count, out in ((TILE - HALO, HALO, up), (0, HALO, down), (0, TILE, planes)):
            copies.append(
                pltpu.make_async_copy(
                    source.at[:, pl.ds(row, count), :], out.at[pl.ds(first, layers)], sems.at[len(copies)]
                )
            )
    for copy in copies:
        copy.start()
    for copy in copies:
        copy.wait()


def slot(p):
    pack, lane = divmod(HALO * p, TILE)
    return pack, lane, [pack] if lane + HALO <= TILE else [pack, pack + 1]


def pack_y_kernel(planes, top, bottom, first, second):
    tile_row, column = place_in_space()
    odd = (column & 1) == 1
    for row in range(0, ROWS, 8):
        lane = lax.broadcasted_iota(jnp.int32, (8, TILE), 1)
        to_right = [jnp.zeros((8, TILE), F32) for _ in range(PACKS)]
        to_left = [jnp.zeros((8, TILE), F32) for _ in range(PACKS)]
        for p in range(PLANES):
            if row < HALO:
                value = jnp.where(tile_row > 0, top[p, pl.ds(row, 8), :], 0.0)
            elif row < HALO + TILE:
                value = planes[p, pl.ds(row - HALO, 8), :]
            else:
                value = jnp.where(tile_row < ACROSS - 1, bottom[p, pl.ds(row - HALO - TILE, 8), :], 0.0)
            _, start, packs = slot(p)
            left = pltpu.roll(value, start, 1) if start else value
            right = pltpu.roll(value, (start + HALO) % TILE, 1)
            for pack in packs:
                at = lane + TILE * pack
                here = (at >= HALO * p) & (at < HALO * (p + 1))
                to_left[pack] = jnp.where(here, left, to_left[pack])
                to_right[pack] = jnp.where(here, right, to_right[pack])
        for pack in range(PACKS):
            first[pack, pl.ds(row, 8), :] = jnp.where(odd, to_left[pack], to_right[pack])
            second[pack, pl.ds(row, 8), :] = jnp.where(odd, to_right[pack], to_left[pack])


def chunk_rows(half):
    return [HALO + MAIN * half + 8 * k for k in range(8)] + ([8, 16], [ROWS - 24, ROWS - 16])[half]


def chunk_out(out, field, first=0):
    lane = lax.broadcasted_iota(jnp.int32, (8, TILE), 1)
    for c in range(RING):
        z, rows = c // 2, chunk_rows(c % 2)
        for k, row in enumerate(rows):
            out[c, pl.ds(first + 8 * k, 8), :] = field[z, 0, pl.ds(row, 8), :]
        for slot in range(3):
            packed = jnp.zeros((8, TILE), F32)
            for j, k in enumerate(range(slot, 10, 3)):
                value = pltpu.roll(field[z, 1, pl.ds(rows[k], 8), :], (SIDE + 32 * j) % TILE, 1)
                packed = jnp.where((lane >= 32 * j) & (lane < 32 * (j + 1)), value, packed)
            out[c, pl.ds(first + FULL + 8 * slot, 8), :] = packed


def chunk_in(field, chunks, change):
    for c in range(RING):
        z, rows = c // 2, chunk_rows(c % 2)
        for k, row in enumerate(rows):
            field[z, 0, pl.ds(row, 8), :] = change(chunks[c, pl.ds(8 * k, 8), :])
            packed = change(chunks[c, pl.ds(FULL + 8 * (k % 3), 8), :])
            field[z, 1, pl.ds(row, 8), :] = pltpu.roll(packed, (TILE - SIDE - 32 * (k // 3)) % TILE, 1)


def own_chunk(out, layer):
    lane = lax.broadcasted_iota(jnp.int32, (8, TILE), 1)
    half = owner() & 1
    low, high = chunk_rows(0), chunk_rows(1)
    rows = [pl.multiple_of(a + (b - a) * half, 8) for a, b in zip(low, high)]
    for k, row in enumerate(rows):
        out[pl.ds(8 * k, 8), :] = layer[0, pl.ds(row, 8), :]
    for slot_of in range(3):
        packed = jnp.zeros((8, TILE), F32)
        for j, k in enumerate(range(slot_of, 10, 3)):
            value = pltpu.roll(layer[1, pl.ds(rows[k], 8), :], (SIDE + 32 * j) % TILE, 1)
            packed = jnp.where((lane >= 32 * j) & (lane < 32 * (j + 1)), value, packed)
        out[pl.ds(FULL + 8 * slot_of, 8), :] = packed


def turn(k):
    return (owner() + k) & 3


def send_chunks(chunks, outs):
    for k, out in enumerate(outs):
        out[...] = chunks[turn(k)]


def gather_chunks(chunks, parts):
    for k, part in enumerate(parts):
        chunks[turn(RING - k)] = part[...]


def fourth(value):
    square = value * value
    return square * square


def left_right(own, other, lane):
    left = pltpu.roll(jnp.where(lane == TILE - 1, other, own), 1, 1)
    right = pltpu.roll(jnp.where(lane == 0, other, own), TILE - 1, 1)
    return left, right


def each_step(first, last, body):
    for r in range(first, last, STEP):
        body(r)


def solve(step, a, q, t4, sp, start, now, old):
    first, last = 8 * step, ROWS - 8 * step

    def source(r):
        for gz in range(4):
            for l in range(2):
                weight = q[gz, l, pl.ds(r, STEP), :]
                value = weight * t4[gz % 2, l, pl.ds(r, STEP), :]
                sp[gz, l, pl.ds(r, STEP), :] = jnp.where(weight > 0.0, value, 0.0)

    each_step(first, last, source)
    before, src = None, start
    for sweep, (keep, push) in enumerate(sweep_weights()):
        dst = old if sweep % 2 == 0 else now

        def body(r, src=src, dst=dst, before=before, keep=keep, push=push):
            lane = lax.broadcasted_iota(jnp.int32, (STEP, TILE), 1)
            rows = pl.ds(r, STEP)
            for g in range(2):
                own = [[src[2 * g + z, l, pl.ds(r + PAD, STEP), :] for l in range(2)] for z in range(2)]
                for z in range(2):
                    for l in range(2):
                        gz = 2 * g + z
                        here = own[z][l]
                        left, right = left_right(here, own[z][1 - l], lane)
                        total = sp[gz, l, rows, :] + a[0, gz, l, rows, :] * own[1 - z][l]
                        total += a[1, gz, l, rows, :] * src[gz, l, pl.ds(r + PAD - 1, STEP), :]
                        total += a[2, gz, l, rows, :] * src[gz, l, pl.ds(r + PAD + 1, STEP), :]
                        total += a[3, gz, l, rows, :] * left + a[4, gz, l, rows, :] * right
                        value = (1.0 + keep - push) * here + push * total
                        if before is not None:
                            value -= keep * before[gz, l, pl.ds(r + PAD, STEP), :]
                        dst[gz, l, pl.ds(r + PAD, STEP), :] = value

        each_step(first, last, body)
        before, src = src, dst


def absorb(kap, now, out):
    def body(r):
        for z in range(2):
            for l in range(2):
                rows = pl.ds(r + PAD, STEP)
                out[z, l, pl.ds(r, STEP), :] = (
                    kap[z, l, rows, :] * now[z, l, rows, :] + kap[2 + z, l, rows, :] * now[2 + z, l, rows, :]
                )

    each_step(8, ROWS - 8, body)


def first_kernel(planes, top, bottom, first, second, *refs):
    a, q, kap, now, held, *outs = refs[: 5 + RING]
    tis, sp, t4, old, begin, sums = refs[5 + RING :]
    planck = now
    tile_row, column = place_in_space()
    odd = (column & 1) == 1

    def place(p):
        if p < 4:
            return kap, p, PAD
        if p < 8:
            return q, p - 4, 0
        if p < 12:
            return begin, p - 8, PAD
        return tis, p - 12, 0

    for p in range(PLANES):
        dst, at, pad = place(p)
        dst[at, 0, pl.ds(pad, HALO), :] = jnp.where(tile_row > 0, top[p], 0.0)
        dst[at, 0, pl.ds(pad + HALO, TILE), :] = planes[p]
        dst[at, 0, pl.ds(pad + HALO + TILE, HALO), :] = jnp.where(tile_row < ACROSS - 1, bottom[p], 0.0)

    def sides(r):
        lane = lax.broadcasted_iota(jnp.int32, (STEP, TILE), 1)
        got = [(first[pack, pl.ds(r, STEP), :], second[pack, pl.ds(r, STEP), :]) for pack in range(PACKS)]
        lefts = [jnp.where(column > 0, jnp.where(odd, f, s), 0.0) for f, s in got]
        rights = [jnp.where(column < ACROSS - 1, jnp.where(odd, s, f), 0.0) for f, s in got]
        for p in range(PLANES):
            pack, start, packs = slot(p)
            left, right = lefts[pack], rights[pack]
            if len(packs) > 1:
                left = jnp.where(lane >= start, left, lefts[pack + 1])
                right = jnp.where(lane >= start, right, rights[pack + 1])
            left = pltpu.roll(left, (2 * TILE - HALO - start) % TILE, 1)
            right = pltpu.roll(right, TILE - start, 1) if start else right
            dst, at, pad = place(p)
            value = jnp.where(lane < HALO, right, jnp.where(lane >= TILE - HALO, left, 0.0))
            dst[at, 1, pl.ds(r + pad, STEP), :] = value

    each_step(0, ROWS, sides)
    own_chunk(held.at[0], tis.at[owner() >> 1])
    own_chunk(held.at[1], tis.at[2])
    own_chunk(held.at[2], tis.at[3])

    def halves(r):
        lane = lax.broadcasted_iota(jnp.int32, (STEP, TILE), 1)
        rows, padded = pl.ds(r, STEP), pl.ds(r + PAD, STEP)
        for z in range(2):
            for l in range(2):
                t4[z, l, rows, :] = fourth(tis[z, l, rows, :])
                planck[z, l, rows, :] = (
                    kap[z, l, padded, :] * q[z, l, rows, :] + kap[2 + z, l, padded, :] * q[2 + z, l, rows, :]
                )
        for gz in range(4):
            own = [kap[gz, l, padded, :] for l in range(2)]
            for l in range(2):
                old[gz, l, padded, :] = 1.0 / (own[l] + kap[gz, l, pl.ds(r + PAD + 1, STEP), :])
                sp[gz, l, rows, :] = 1.0 / (own[l] + left_right(own[l], own[1 - l], lane)[1])

    each_step(0, ROWS, halves)

    def coefficients(r):
        lane = lax.broadcasted_iota(jnp.int32, (STEP, TILE), 1)
        rows, padded = pl.ds(r, STEP), pl.ds(r + PAD, STEP)
        for g in range(2):
            own = [[kap[2 * g + z, l, padded, :] for l in range(2)] for z in range(2)]
            between = [1.0 / (own[0][l] + own[1][l]) for l in range(2)]
            for z in range(2):
                gz = 2 * g + z
                to_right = [sp[gz, l, rows, :] for l in range(2)]
                for l in range(2):
                    here = own[z][l]
                    to_left = left_right(to_right[l], to_right[1 - l], lane)[0]
                    to_up = old[gz, l, pl.ds(r + PAD - 1, STEP), :]
                    couplings = [between[l], to_up, old[gz, l, padded, :], to_left, to_right[l]]
                    diagonal = 1.5 * here + 1.0 / here
                    for coupling in couplings:
                        diagonal += coupling
                    inverse = 1.0 / diagonal
                    for f, coupling in enumerate(couplings):
                        a[f, gz, l, rows, :] = jnp.where(here > 0.0, coupling * inverse, 0.0)
                    weight = 6.0 * here * q[gz, l, rows, :] * inverse
                    q[gz, l, rows, :] = jnp.where(here > 0.0, weight, 0.0)

    each_step(0, ROWS, coefficients)
    chunk_out(sums, planck, CHUNK)
    solve(0, a, q, t4, sp, begin, now, old)
    absorb(kap, now, t4)
    chunk_out(sums, t4)
    send_chunks(sums, outs)


def next_kernel(a, q, kap, start, *refs):
    parts = refs[:RING]
    now, *outs = refs[RING : 2 * RING + 1]
    sp, t4, old, sums = refs[2 * RING + 1 :]
    gather_chunks(sums, parts)
    chunk_in(t4, sums, fourth)
    solve(1, a, q, t4, sp, start, now, old)
    absorb(kap, now, t4)
    chunk_out(sums, t4)
    send_chunks(sums, outs)


def last_kernel(a, q, kap, start, *refs):
    parts = refs[:RING]
    radiation, *outs = refs[RING : 2 * RING + 1]
    sp, t4, old, now, sums = refs[2 * RING + 1 :]
    gather_chunks(sums, parts)
    chunk_in(t4, sums, fourth)
    solve(2, a, q, t4, sp, start, now, old)
    rows = pl.ds(PAD + HALO, TILE)
    for gz in range(4):
        radiation[gz // 2, 0, gz % 2, :, :] = now[gz, 0, rows, :]
    for c in range(RING):
        z = c // 2
        part = pl.ds(PAD + HALO + MAIN * (c % 2), MAIN)
        sums[c, pl.ds(0, MAIN), :] = (
            kap[z, 0, part, :] * now[z, 0, part, :] + kap[2 + z, 0, part, :] * now[2 + z, 0, part, :]
        )
    for k, out in enumerate(outs):
        out[...] = sums[turn(k), pl.ds(0, MAIN), :]


def final_kernel(*refs):
    parts, out = refs[:RING], refs[RING]
    gather_chunks(out, parts)


def corrected(current, earlier, inertia, source, emitted, taken):
    mismatch = inertia * (current - earlier) + 4.0 * emitted * fourth(current) - taken - source
    slope = inertia + 16.0 * emitted * (current * current * current)
    return jnp.where(inertia > 0.0, current - mismatch / slope, 0.0)


def call(kernel, outs, scratch=(), space=pltpu.VMEM):
    def run(*args):
        return pl.pallas_call(
            kernel,
            out_shape=[jax.ShapeDtypeStruct(dims, F32) for dims in outs],
            in_specs=[pl.BlockSpec(memory_space=space)] * len(args),
            out_specs=[pl.BlockSpec(memory_space=pltpu.VMEM)] * len(outs),
            scratch_shapes=[pltpu.VMEM(s, F32) if isinstance(s, tuple) else s for s in scratch],
            compiler_params=pltpu.CompilerParams(vmem_limit_bytes=VMEM_LIMIT),
        )(*args)

    return run


FIELD = (4, 2, ROWS, TILE)
PADDED = (4, 2, ROWS + 2 * PAD, TILE)
SHARED = (2, 2, ROWS, TILE)
OUT_TURNS = (2, 1, 3)
BACK_TURNS = (1, 3, 2)


def along_y(array, by):
    pairs = [(4 * z + y, 4 * z + (y + by) % 4) for z in range(4) for y in range(4)]
    return lax.ppermute(array, "gas", pairs)


def along_z(array, by):
    pairs = [(4 * z + y, 4 * ((z + by) % 4) + y) for z in range(4) for y in range(4)]
    return lax.ppermute(array, "gas", pairs)


def sum_over_gas(parts):
    total = parts[0]
    for k in OUT_TURNS:
        total = total + along_y(parts[k], k)
    parts = [along_z(total, k) for k in (2, 1, 3)]
    return total + parts[0] + parts[1] + parts[2]


def spread(chunk):
    parts = {k: along_y(chunk, k) for k in BACK_TURNS}
    return [chunk] + [parts[k] for k in range(1, RING)]


def on_device(*inputs):
    kelvin, inertia, source, extinction, fractions, irradiance = inputs
    own = (extinction, fractions, irradiance, kelvin, inertia, source)
    own = [pltpu.with_memory_space_constraint(array, pltpu.HBM) for array in own]
    devices = lax.axis_size("space")
    planes, up, down = call(
        load_kernel,
        [(PLANES, TILE, TILE)] + [(PLANES, HALO, TILE)] * 2,
        [pltpu.SemaphoreType.DMA((27,))],
        space=pltpu.HBM,
    )(*own)
    ring = [(i, (i + ACROSS) % devices) for i in range(devices)]
    top = lax.ppermute(up, "space", ring)
    bottom = lax.ppermute(down, "space", [(j, i) for i, j in ring])
    first, second = call(pack_y_kernel, [(PACKS, ROWS, TILE)] * 2)(planes, top, bottom)
    first = lax.ppermute(first, "space", [(i, i ^ 1) for i in range(devices)])
    swaps = (0, 2, 1, 3)
    second = lax.ppermute(second, "space", [(i, i - i % ACROSS + swaps[i % ACROSS]) for i in range(devices)])
    two = (2 * CHUNK, TILE)
    a, q, kap, now, held, *parts = call(
        first_kernel,
        [(5,) + FIELD, FIELD, PADDED, PADDED, (3, CHUNK, TILE)] + [two] * RING,
        [(4, 2, ROWS, TILE), FIELD, SHARED, PADDED, PADDED, (RING,) + two],
    )(planes, top, bottom, first, second)
    total = sum_over_gas(parts)
    taken, emitted = total[:CHUNK], total[CHUNK:]
    earlier, inertia, source = held[0], held[1], held[2]
    current = corrected(earlier, earlier, inertia, source, emitted, taken)
    one = (CHUNK, TILE)
    now, *parts = call(
        next_kernel, [PADDED] + [one] * RING, [FIELD, SHARED, PADDED, (RING,) + one]
    )(a, q, kap, now, *spread(current))
    current = corrected(current, earlier, inertia, source, emitted, sum_over_gas(parts))
    radiation, *parts = call(
        last_kernel,
        [(2, 1, 2, TILE, TILE)] + [(MAIN, TILE)] * RING,
        [FIELD, SHARED, PADDED, PADDED, (RING,) + one],
    )(a, q, kap, now, *spread(current))
    rest = (value[:MAIN] for value in (current, earlier, inertia, source, emitted))
    current = corrected(*rest, sum_over_gas(parts))
    (final,) = call(final_kernel, [(RING, MAIN, TILE)])(*spread(current))
    return final.reshape(1, 2, TILE, TILE), radiation


def solution(mesh):
    placed = (
        P("space", None, None, None),
        P("space", None, None, None),
        P("space", None, None, None),
        P("gas", "space", None, None, None),
        P("gas", "space", None, None, None),
        P("gas", "space", None, None, None),
    )
    return jax.shard_map(
        on_device,
        mesh=mesh,
        in_specs=placed,
        out_specs=(P("space", None, None, None), P("gas", "space", None, None, None)),
        check_vma=False,
    )
```

time: 133 us -> 127 us (0.955); the launches traced: 131 us -> 127 us
  waiting for transfers between devices: 52.8 us -> 48 us
  Pallas kernels: 18.2 us -> 19.6 us
    ppermute x10 -> x13, starting transfers between devices: 38.4 us -> 28.4 us  [the longest x9 23.1 us: along_z(): return lax.ppermute(array, 'gas', pairs)]
    ppermute x18, starting transfers between devices: 20.3 us -> 30 us  [along_y(): return lax.ppermute(array, 'gas', pairs)]
    ppermute x18, waiting for transfers between devices: 28.6 us -> 21.5 us  [along_y(): return lax.ppermute(array, 'gas', pairs)]
    ppermute x10 -> x13, waiting for transfers between devices: 24.2 us -> 26.5 us  [the longest x9 15.9 us: along_z(): return lax.ppermute(array, 'gas', pairs)]
    pallas_call x6, Pallas kernels: 18.2 us -> 19.6 us  [run(): pl.pallas_call(kernel, out_shape=[jax.ShapeDtypeStruct(dims, F32) for dim...]
  transfers between devices with their start and end apart: 28 -> 31, of which waited for: 26 -> 20; matrix products, arithmetic and copies ran while one was open for 0% -> 0% of each run, Pallas kernels for 0% -> 0%
where the time goes in v3:
time: 127 us
  starting transfers between devices  58.4 us (46%)
  waiting for transfers between devices  48 us (38%)
  Pallas kernels  19.6 us (15%)
    ppermute x18, starting transfers between devices, along_y(): return lax.ppermute(array, 'gas', pairs)  30 us
    ppermute x9, starting transfers between devices, along_z(): return lax.ppermute(array, 'gas', pairs)  23.1 us
    ppermute x18, waiting for transfers between devices, along_y(): return lax.ppermute(array, 'gas', pairs)  21.5 us
    pallas_call x6, Pallas kernels, run(): pl.pallas_call(kernel, out_shape=[jax.ShapeDtypeStruct(dims, F32) for dim...  19.6 us
    ppermute x9, waiting for transfers between devices, along_z(): return lax.ppermute(array, 'gas', pairs)  15.9 us
    ppermute x1, waiting for transfers between devices, on_device(): top = lax.ppermute(up, 'space', ring)  4.61 us
    ppermute x1, waiting for transfers between devices, on_device(): lax.ppermute(second, 'space', [(i, i - i % ACROSS + swaps[i % ACROSS]) fo...  4.61 us
    ppermute x1, starting transfers between devices, on_device(): lax.ppermute(second, 'space', [(i, i - i % ACROSS + swaps[i % ACROSS]) fo...  3.15 us
  transfers between devices with their start and end apart: 31, of which 20 were waited for; matrix products, arithmetic and copies ran while one was open for 0% of the time, Pallas kernels for 0%

profile of v3, /device:TPU:38, one launch (start us, length us, event | category | flops | bytes accessed | tf_op | source)
XLA Modules:
  0.0 127.0 jit_solution(11130258238484481808)
XLA Ops:
  0.6 1.6 %shard_map.77 = (f32[16,128,128]{2,1,0:T(8,128)S(1)}, f32[16,24,128]{2,1,0:T(8,128)S(1)}, f32[16,24,128]{2,1,0:T(8,128)S(1)}) custom-call(f32[2,1,2,128,128]{4,3,2,1,0:T(8,128)} %refs_0_.1, f32[2,1,2,128,128]{4,3,2,1,0:T(8,128)} %refs_1_.1, f32[2,1,2,128,128]{4,3,2,1,0:T(8,128)} %refs_2_.1, f32[1,2,128,128]{3,2,1,0:T(8,128)} %refs_3_.1, ...), custom_call_target="tpu_custom_call" | custom-call | tf_op jit(solution)/shard_map/pallas_call | solution.py:365
  2.3 0.6 collective-permute-start
  2.8 1.5 %collective-permute-start.1 = (f32[16,24,128]{2,1,0:T(8,128)S(1)}, f32[16,24,128]{2,1,0:T(8,128)S(1)}, u32[]{:S(2)}, u32[]{:S(2)}) collective-permute-start(f32[16,24,128]{2,1,0:T(8,128)S(1)} %get-tuple-element.28), channel_id=1, source_target_pairs={{4,0},{5,1},{6,2},{7,3},{8,4},{9,5},{10,6},{11,7},{12,8},{13,9},{1... | collective-permute-start | bytes 589832 | tf_op jit(solution)/shard_map/ppermute | solution.py:420
  4.4 4.6 %collective-permute-done.top = f32[16,24,128]{2,1,0:T(8,128)S(1)} collective-permute-done((f32[16,24,128]{2,1,0:T(8,128)S(1)}, f32[16,24,128]{2,1,0:T(8,128)S(1)}, u32[]{:S(2)}, u32[]{:S(2)}) %collective-permute-start) | collective-permute-done | bytes 196640 | tf_op jit(solution)/shard_map/ppermute | solution.py:419
  9.0 1.4 %collective-permute-done.1.bottom = f32[16,24,128]{2,1,0:T(8,128)S(1)} collective-permute-done((f32[16,24,128]{2,1,0:T(8,128)S(1)}, f32[16,24,128]{2,1,0:T(8,128)S(1)}, u32[]{:S(2)}, u32[]{:S(2)}) %collective-permute-start.1) | collective-permute-done | bytes 196640 | tf_op jit(solution)/shard_map/ppermute | solution.py:420
  10.4 0.8 shard_map.78
  11.3 3.2 %collective-permute-start.3 = (f32[3,176,128]{2,1,0:T(8,128)S(1)}, f32[3,176,128]{2,1,0:T(8,128)S(1)}, u32[]{:S(2)}, u32[]{:S(2)}) collective-permute-start(f32[3,176,128]{2,1,0:T(8,128)S(1)} %get-tuple-element.30), channel_id=1, source_target_pairs={{0,0},{1,2},{2,1},{3,3},{4,4},{5,6},{6,5},{7,7},{8,8},{9,10},{10,9... | collective-permute-start | bytes 811016 | tf_op jit(solution)/shard_map/ppermute | solution.py:424
  14.4 4.6 %collective-permute-done.3.second = f32[3,176,128]{2,1,0:T(8,128)S(1)} collective-permute-done((f32[3,176,128]{2,1,0:T(8,128)S(1)}, f32[3,176,128]{2,1,0:T(8,128)S(1)}, u32[]{:S(2)}, u32[]{:S(2)}) %collective-permute-start.3) | collective-permute-done | bytes 270368 | tf_op jit(solution)/shard_map/ppermute | solution.py:424
  19.0 6.6 %shard_map.79 = (f32[5,4,2,176,128]{4,3,2,1,0:T(8,128)S(1)}, f32[4,2,176,128]{3,2,1,0:T(8,128)S(1)}, f32[4,2,192,128]{3,2,1,0:T(8,128)S(1)}, f32[4,2,192,128]{3,...) custom-call(f32[16,128,128]{2,1,0:T(8,128)S(1)} %get-tuple-element.2, ...), custom_call_target="tpu_custom_call" | custom-call | tf_op jit(solution)/shard_map/pallas_call | solution.py:365
  25.7 3.3 %collective-permute-start.4 = (f32[208,128]{1,0:T(8,128)S(1)}, f32[208,128]{1,0:T(8,128)S(1)}, u32[]{:S(2)}, u32[]{:S(2)}) collective-permute-start(f32[208,128]{1,0:T(8,128)S(1)} %get-tuple-element.33), channel_id=1, source_target_pairs={{0,32},{16,48},{32,0},{48,16},{64,96},{80,112},{96,64},{112,80},{1... | collective-permute-start | bytes 319496 | tf_op jit(solution)/shard_map/ppermute | solution.py:386
  29.0 0.7 collective-permute-start.5
  29.6 2.5 %collective-permute-start.6 = (f32[208,128]{1,0:T(8,128)S(1)}, f32[208,128]{1,0:T(8,128)S(1)}, u32[]{:S(2)}, u32[]{:S(2)}) collective-permute-start(f32[208,128]{1,0:T(8,128)S(1)} %get-tuple-element.35), channel_id=1, source_target_pairs={{0,48},{16,0},{32,16},{48,32},{64,112},{80,64},{96,80},{112,96},{1... | collective-permute-start | bytes 319496 | tf_op jit(solution)/shard_map/ppermute | solution.py:386
  32.2 2.7 %collective-permute-done.5 = f32[208,128]{1,0:T(8,128)S(1)} collective-permute-done((f32[208,128]{1,0:T(8,128)S(1)}, f32[208,128]{1,0:T(8,128)S(1)}, u32[]{:S(2)}, u32[]{:S(2)}) %collective-permute-start.5) | collective-permute-done | bytes 106528 | tf_op jit(solution)/shard_map/ppermute | solution.py:386
  34.9 5.5 %collective-permute-start.9 = (f32[208,128]{1,0:T(8,128)S(1)}, f32[208,128]{1,0:T(8,128)S(1)}, u32[]{:S(2)}, u32[]{:S(2)}) collective-permute-start(f32[208,128]{1,0:T(8,128)S(1)} %add_add_fusion.1), channel_id=1, source_target_pairs={{0,192},{16,208},{32,224},{48,240},{64,0},{80,16},{96,32},{112,48}... | collective-permute-start | bytes 319496 | tf_op jit(solution)/shard_map/ppermute | solution.py:391
  40.4 3.8 %collective-permute-start.7 = (f32[208,128]{1,0:T(8,128)S(1)}, f32[208,128]{1,0:T(8,128)S(1)}, u32[]{:S(2)}, u32[]{:S(2)}) collective-permute-start(f32[208,128]{1,0:T(8,128)S(1)} %add_add_fusion.1), channel_id=1, source_target_pairs={{0,128},{16,144},{32,160},{48,176},{64,192},{80,208},{96,224},{112... | collective-permute-start | bytes 319496 | tf_op jit(solution)/shard_map/ppermute | solution.py:391
  44.2 4.9 %collective-permute-done.8 = f32[208,128]{1,0:T(8,128)S(1)} collective-permute-done((f32[208,128]{1,0:T(8,128)S(1)}, f32[208,128]{1,0:T(8,128)S(1)}, u32[]{:S(2)}, u32[]{:S(2)}) %collective-permute-start.8) | collective-permute-done | bytes 106528 | tf_op jit(solution)/shard_map/ppermute | solution.py:391
  49.2 3.3 %collective-permute-start.12 = (f32[104,128]{1,0:T(8,128)S(1)}, f32[104,128]{1,0:T(8,128)S(1)}, u32[]{:S(2)}, u32[]{:S(2)}) collective-permute-start(f32[104,128]{1,0:T(8,128)S(1)} %fusion.6.refs_0_), channel_id=1, source_target_pairs={{0,48},{16,0},{32,16},{48,32},{64,112},{80,64},{96,80},{112,96},{1... | collective-permute-start | bytes 159752 | tf_op jit(solution)/shard_map/ppermute | solution.py:386
  52.5 1.0 collective-permute-start.10
  53.4 0.8 collective-permute-done.12.refs_3_
  54.2 4.0 %collective-permute-done.11.refs_2_ = f32[104,128]{1,0:T(8,128)S(1)} collective-permute-done((f32[104,128]{1,0:T(8,128)S(1)}, f32[104,128]{1,0:T(8,128)S(1)}, u32[]{:S(2)}, u32[]{:S(2)}) %collective-permute-start.11) | collective-permute-done | bytes 53280 | tf_op jit(solution)/shard_map/ppermute | solution.py:386
  58.3 0.5 collective-permute-done.10.refs_1_
  58.7 4.6 %shard_map.80 = (f32[4,2,192,128]{3,2,1,0:T(8,128)S(1)}, f32[104,128]{1,0:T(8,128)S(1)}, f32[104,128]{1,0:T(8,128)S(1)}, f32[104,128]{1,0:T(8,128)S(1)}, f32[104,128]{1,0:T(8,128)S(1)}) custom-call(f32[5,4,2,176,128]{4,3,2,1,0:T(8,128)S(1)} %get-tuple-element.36.a, f32[4,2,176,128]{3,2,1,0:T(8,128)S(1)} %get-tuple-element.37.q, ...), custom_call_target="tpu_custom_call" | custom-call | tf_op jit(solution)/shard_map/pallas_call | solution.py:365
  63.3 2.5 %collective-permute-start.13 = (f32[104,128]{1,0:T(8,128)S(1)}, f32[104,128]{1,0:T(8,128)S(1)}, u32[]{:S(2)}, u32[]{:S(2)}) collective-permute-start(f32[104,128]{1,0:T(8,128)S(1)} %get-tuple-element.41), channel_id=1, source_target_pairs={{0,32},{16,48},{32,0},{48,16},{64,96},{80,112},{96,64},{112,80},{1... | collective-permute-start | bytes 159752 | tf_op jit(solution)/shard_map/ppermute | solution.py:386
  65.8 3.2 %collective-permute-start.15 = (f32[104,128]{1,0:T(8,128)S(1)}, f32[104,128]{1,0:T(8,128)S(1)}, u32[]{:S(2)}, u32[]{:S(2)}) collective-permute-start(f32[104,128]{1,0:T(8,128)S(1)} %get-tuple-element.43), channel_id=1, source_target_pairs={{0,48},{16,0},{32,16},{48,32},{64,112},{80,64},{96,80},{112,96},{1... | collective-permute-start | bytes 159752 | tf_op jit(solution)/shard_map/ppermute | solution.py:386
  69.0 2.1 %collective-permute-done.14 = f32[104,128]{1,0:T(8,128)S(1)} collective-permute-done((f32[104,128]{1,0:T(8,128)S(1)}, f32[104,128]{1,0:T(8,128)S(1)}, u32[]{:S(2)}, u32[]{:S(2)}) %collective-permute-start.14) | collective-permute-done | bytes 53280 | tf_op jit(solution)/shard_map/ppermute | solution.py:386
  71.2 4.7 %collective-permute-start.18 = (f32[104,128]{1,0:T(8,128)S(1)}, f32[104,128]{1,0:T(8,128)S(1)}, u32[]{:S(2)}, u32[]{:S(2)}) collective-permute-start(f32[104,128]{1,0:T(8,128)S(1)} %add_add_fusion.2), channel_id=1, source_target_pairs={{0,192},{16,208},{32,224},{48,240},{64,0},{80,16},{96,32},{112,48}... | collective-permute-start | bytes 159752 | tf_op jit(solution)/shard_map/ppermute | solution.py:391
  75.8 2.4 %collective-permute-start.16 = (f32[104,128]{1,0:T(8,128)S(1)}, f32[104,128]{1,0:T(8,128)S(1)}, u32[]{:S(2)}, u32[]{:S(2)}) collective-permute-start(f32[104,128]{1,0:T(8,128)S(1)} %add_add_fusion.2), channel_id=1, source_target_pairs={{0,128},{16,144},{32,160},{48,176},{64,192},{80,208},{96,224},{112... | collective-permute-start | bytes 159752 | tf_op jit(solution)/shard_map/ppermute | solution.py:391
  78.3 3.8 %collective-permute-done.17 = f32[104,128]{1,0:T(8,128)S(1)} collective-permute-done((f32[104,128]{1,0:T(8,128)S(1)}, f32[104,128]{1,0:T(8,128)S(1)}, u32[]{:S(2)}, u32[]{:S(2)}) %collective-permute-start.17) | collective-permute-done | bytes 53280 | tf_op jit(solution)/shard_map/ppermute | solution.py:391
  82.1 1.8 %collective-permute-done.16 = f32[104,128]{1,0:T(8,128)S(1)} collective-permute-done((f32[104,128]{1,0:T(8,128)S(1)}, f32[104,128]{1,0:T(8,128)S(1)}, u32[]{:S(2)}, u32[]{:S(2)}) %collective-permute-start.16) | collective-permute-done | bytes 53280 | tf_op jit(solution)/shard_map/ppermute | solution.py:391
  83.9 3.3 %collective-permute-start.21 = (f32[104,128]{1,0:T(8,128)S(1)}, f32[104,128]{1,0:T(8,128)S(1)}, u32[]{:S(2)}, u32[]{:S(2)}) collective-permute-start(f32[104,128]{1,0:T(8,128)S(1)} %fusion.15.refs_0_), channel_id=1, source_target_pairs={{0,48},{16,0},{32,16},{48,32},{64,112},{80,64},{96,80},{112,96},{1... | collective-permute-start | bytes 159752 | tf_op jit(solution)/shard_map/ppermute | solution.py:386
  87.2 1.0 collective-permute-start.19
  88.2 1.6 %collective-permute-done.21.refs_3_ = f32[104,128]{1,0:T(8,128)S(1)} collective-permute-done((f32[104,128]{1,0:T(8,128)S(1)}, f32[104,128]{1,0:T(8,128)S(1)}, u32[]{:S(2)}, u32[]{:S(2)}) %collective-permute-start.21) | collective-permute-done | bytes 53280 | tf_op jit(solution)/shard_map/ppermute | solution.py:386
  89.8 3.1 %collective-permute-done.20.refs_2_ = f32[104,128]{1,0:T(8,128)S(1)} collective-permute-done((f32[104,128]{1,0:T(8,128)S(1)}, f32[104,128]{1,0:T(8,128)S(1)}, u32[]{:S(2)}, u32[]{:S(2)}) %collective-permute-start.20) | collective-permute-done | bytes 53280 | tf_op jit(solution)/shard_map/ppermute | solution.py:386
  93.0 0.2 collective-permute-done.19.refs_1_
  93.1 5.4 %shard_map.81 = (f32[2,1,2,128,128]{4,3,2,1,0:T(8,128)}, f32[64,128]{1,0:T(8,128)S(1)}, f32[64,128]{1,0:T(8,128)S(1)}, f32[64,128]{1,0:T(8,128)S(1)}, f32[64,128]{1,0:T(8,128)S(1)}) custom-call(f32[5,4,2,176,128]{4,3,2,1,0:T(8,128)S(1)} %get-tuple-element.36.a, f32[4,2,176,128]{3,2,1,0:T(8,128)S(1)} %get-tuple-element.37.q, ...), custom_call_target="tpu_custom_call" | custom-call | tf_op jit(solution)/shard_map/pallas_call | solution.py:365
  98.5 1.7 %collective-permute-start.22 = (f32[64,128]{1,0:T(8,128)S(1)}, f32[64,128]{1,0:T(8,128)S(1)}, u32[]{:S(2)}, u32[]{:S(2)}) collective-permute-start(f32[64,128]{1,0:T(8,128)S(1)} %get-tuple-element.46), channel_id=1, source_target_pairs={{0,32},{16,48},{32,0},{48,16},{64,96},{80,112},{96,64},{112,80},{1... | collective-permute-start | bytes 98312 | tf_op jit(solution)/shard_map/ppermute | solution.py:386
  100.3 3.2 %collective-permute-start.24 = (f32[64,128]{1,0:T(8,128)S(1)}, f32[64,128]{1,0:T(8,128)S(1)}, u32[]{:S(2)}, u32[]{:S(2)}) collective-permute-start(f32[64,128]{1,0:T(8,128)S(1)} %get-tuple-element.48), channel_id=1, source_target_pairs={{0,48},{16,0},{32,16},{48,32},{64,112},{80,64},{96,80},{112,96},{1... | collective-permute-start | bytes 98312 | tf_op jit(solution)/shard_map/ppermute | solution.py:386
  103.5 0.4 collective-permute-done.22
  103.9 1.5 %collective-permute-done.23 = f32[64,128]{1,0:T(8,128)S(1)} collective-permute-done((f32[64,128]{1,0:T(8,128)S(1)}, f32[64,128]{1,0:T(8,128)S(1)}, u32[]{:S(2)}, u32[]{:S(2)}) %collective-permute-start.23) | collective-permute-done | bytes 32800 | tf_op jit(solution)/shard_map/ppermute | solution.py:386
  105.4 4.2 %collective-permute-start.27 = (f32[64,128]{1,0:T(8,128)S(1)}, f32[64,128]{1,0:T(8,128)S(1)}, u32[]{:S(2)}, u32[]{:S(2)}) collective-permute-start(f32[64,128]{1,0:T(8,128)S(1)} %add_add_fusion.3), channel_id=1, source_target_pairs={{0,192},{16,208},{32,224},{48,240},{64,0},{80,16},{96,32},{112,48}... | collective-permute-start | bytes 98312 | tf_op jit(solution)/shard_map/ppermute | solution.py:391
  109.6 2.4 %collective-permute-start.25 = (f32[64,128]{1,0:T(8,128)S(1)}, f32[64,128]{1,0:T(8,128)S(1)}, u32[]{:S(2)}, u32[]{:S(2)}) collective-permute-start(f32[64,128]{1,0:T(8,128)S(1)} %add_add_fusion.3), channel_id=1, source_target_pairs={{0,128},{16,144},{32,160},{48,176},{64,192},{80,208},{96,224},{112... | collective-permute-start | bytes 98312 | tf_op jit(solution)/shard_map/ppermute | solution.py:391
  112.1 3.6 %collective-permute-done.26 = f32[64,128]{1,0:T(8,128)S(1)} collective-permute-done((f32[64,128]{1,0:T(8,128)S(1)}, f32[64,128]{1,0:T(8,128)S(1)}, u32[]{:S(2)}, u32[]{:S(2)}) %collective-permute-start.26) | collective-permute-done | bytes 32800 | tf_op jit(solution)/shard_map/ppermute | solution.py:391
  115.7 1.8 %collective-permute-done.25 = f32[64,128]{1,0:T(8,128)S(1)} collective-permute-done((f32[64,128]{1,0:T(8,128)S(1)}, f32[64,128]{1,0:T(8,128)S(1)}, u32[]{:S(2)}, u32[]{:S(2)}) %collective-permute-start.25) | collective-permute-done | bytes 32800 | tf_op jit(solution)/shard_map/ppermute | solution.py:391
  117.5 3.3 %collective-permute-start.30 = (f32[64,128]{1,0:T(8,128)S(1)}, f32[64,128]{1,0:T(8,128)S(1)}, u32[]{:S(2)}, u32[]{:S(2)}) collective-permute-start(f32[64,128]{1,0:T(8,128)S(1)} %fusion.26.refs_0_), channel_id=1, source_target_pairs={{0,48},{16,0},{32,16},{48,32},{64,112},{80,64},{96,80},{112,96},{1... | collective-permute-start | bytes 98312 | tf_op jit(solution)/shard_map/ppermute | solution.py:386
  120.8 1.0 collective-permute-start.28
  121.8 0.6 collective-permute-done.30.refs_3_
  122.4 3.9 %collective-permute-done.29.refs_2_ = f32[64,128]{1,0:T(8,128)S(1)} collective-permute-done((f32[64,128]{1,0:T(8,128)S(1)}, f32[64,128]{1,0:T(8,128)S(1)}, u32[]{:S(2)}, u32[]{:S(2)}) %collective-permute-start.29) | collective-permute-done | bytes 32800 | tf_op jit(solution)/shard_map/ppermute | solution.py:386
  126.3 0.7 shard_map.82
  (27 shorter events, 0.4 us)
Async XLA Ops:
  2.3 6.7 %collective-permute-start = (f32[16,24,128]{2,1,0:T(8,128)S(1)}, f32[16,24,128]{2,1,0:T(8,128)S(1)}, u32[]{:S(2)}, u32[]{:S(2)}) collective-permute-start(f32[16,24,128]{2,1,0:T(8,128)S(1)} %get-tuple-element.27), channel_id=1, source_target_pairs={{0,4},{1,5},{2,6},{3,7},{4,8},{5,9},{6,10},{7,11},{8,12},{9,13},{1... | collective-permute-start | bytes 589832 | tf_op jit(solution)/shard_map/ppermute | solution.py:419
  2.8 7.6 %collective-permute-start.1 = (f32[16,24,128]{2,1,0:T(8,128)S(1)}, f32[16,24,128]{2,1,0:T(8,128)S(1)}, u32[]{:S(2)}, u32[]{:S(2)}) collective-permute-start(f32[16,24,128]{2,1,0:T(8,128)S(1)} %get-tuple-element.28), channel_id=1, source_target_pairs={{4,0},{5,1},{6,2},{7,3},{8,4},{9,5},{10,6},{11,7},{12,8},{13,9},{1... | collective-permute-start | bytes 589832 | tf_op jit(solution)/shard_map/ppermute | solution.py:420
  11.2 3.3 %collective-permute-start.2 = (f32[3,176,128]{2,1,0:T(8,128)S(1)}, f32[3,176,128]{2,1,0:T(8,128)S(1)}, u32[]{:S(2)}, u32[]{:S(2)}) collective-permute-start(f32[3,176,128]{2,1,0:T(8,128)S(1)} %get-tuple-element.29), channel_id=1, source_target_pairs={{0,1},{1,0},{2,3},{3,2},{4,5},{5,4},{6,7},{7,6},{8,9},{9,8},{10,11... | collective-permute-start | bytes 811016 | tf_op jit(solution)/shard_map/ppermute | solution.py:422
  11.3 7.8 %collective-permute-start.3 = (f32[3,176,128]{2,1,0:T(8,128)S(1)}, f32[3,176,128]{2,1,0:T(8,128)S(1)}, u32[]{:S(2)}, u32[]{:S(2)}) collective-permute-start(f32[3,176,128]{2,1,0:T(8,128)S(1)} %get-tuple-element.30), channel_id=1, source_target_pairs={{0,0},{1,2},{2,1},{3,3},{4,4},{5,6},{6,5},{7,7},{8,8},{9,10},{10,9... | collective-permute-start | bytes 811016 | tf_op jit(solution)/shard_map/ppermute | solution.py:424
  25.7 6.5 %collective-permute-start.4 = (f32[208,128]{1,0:T(8,128)S(1)}, f32[208,128]{1,0:T(8,128)S(1)}, u32[]{:S(2)}, u32[]{:S(2)}) collective-permute-start(f32[208,128]{1,0:T(8,128)S(1)} %get-tuple-element.33), channel_id=1, source_target_pairs={{0,32},{16,48},{32,0},{48,16},{64,96},{80,112},{96,64},{112,80},{1... | collective-permute-start | bytes 319496 | tf_op jit(solution)/shard_map/ppermute | solution.py:386
  29.0 5.9 %collective-permute-start.5 = (f32[208,128]{1,0:T(8,128)S(1)}, f32[208,128]{1,0:T(8,128)S(1)}, u32[]{:S(2)}, u32[]{:S(2)}) collective-permute-start(f32[208,128]{1,0:T(8,128)S(1)} %get-tuple-element.34), channel_id=1, source_target_pairs={{0,16},{16,32},{32,48},{48,0},{64,80},{80,96},{96,112},{112,64},{1... | collective-permute-start | bytes 319496 | tf_op jit(solution)/shard_map/ppermute | solution.py:386
  29.6 5.2 %collective-permute-start.6 = (f32[208,128]{1,0:T(8,128)S(1)}, f32[208,128]{1,0:T(8,128)S(1)}, u32[]{:S(2)}, u32[]{:S(2)}) collective-permute-start(f32[208,128]{1,0:T(8,128)S(1)} %get-tuple-element.35), channel_id=1, source_target_pairs={{0,48},{16,0},{32,16},{48,32},{64,112},{80,64},{96,80},{112,96},{1... | collective-permute-start | bytes 319496 | tf_op jit(solution)/shard_map/ppermute | solution.py:386
  34.9 9.3 %collective-permute-start.9 = (f32[208,128]{1,0:T(8,128)S(1)}, f32[208,128]{1,0:T(8,128)S(1)}, u32[]{:S(2)}, u32[]{:S(2)}) collective-permute-start(f32[208,128]{1,0:T(8,128)S(1)} %add_add_fusion.1), channel_id=1, source_target_pairs={{0,192},{16,208},{32,224},{48,240},{64,0},{80,16},{96,32},{112,48}... | collective-permute-start | bytes 319496 | tf_op jit(solution)/shard_map/ppermute | solution.py:391
  40.4 8.7 %collective-permute-start.8 = (f32[208,128]{1,0:T(8,128)S(1)}, f32[208,128]{1,0:T(8,128)S(1)}, u32[]{:S(2)}, u32[]{:S(2)}) collective-permute-start(f32[208,128]{1,0:T(8,128)S(1)} %add_add_fusion.1), channel_id=1, source_target_pairs={{0,64},{16,80},{32,96},{48,112},{64,128},{80,144},{96,160},{112,17... | collective-permute-start | bytes 319496 | tf_op jit(solution)/shard_map/ppermute | solution.py:391
  40.4 8.7 %collective-permute-start.7 = (f32[208,128]{1,0:T(8,128)S(1)}, f32[208,128]{1,0:T(8,128)S(1)}, u32[]{:S(2)}, u32[]{:S(2)}) collective-permute-start(f32[208,128]{1,0:T(8,128)S(1)} %add_add_fusion.1), channel_id=1, source_target_pairs={{0,128},{16,144},{32,160},{48,176},{64,192},{80,208},{96,224},{112... | collective-permute-start | bytes 319496 | tf_op jit(solution)/shard_map/ppermute | solution.py:391
  49.2 5.1 %collective-permute-start.12 = (f32[104,128]{1,0:T(8,128)S(1)}, f32[104,128]{1,0:T(8,128)S(1)}, u32[]{:S(2)}, u32[]{:S(2)}) collective-permute-start(f32[104,128]{1,0:T(8,128)S(1)} %fusion.6.refs_0_), channel_id=1, source_target_pairs={{0,48},{16,0},{32,16},{48,32},{64,112},{80,64},{96,80},{112,96},{1... | collective-permute-start | bytes 159752 | tf_op jit(solution)/shard_map/ppermute | solution.py:386
  52.4 5.8 %collective-permute-start.11 = (f32[104,128]{1,0:T(8,128)S(1)}, f32[104,128]{1,0:T(8,128)S(1)}, u32[]{:S(2)}, u32[]{:S(2)}) collective-permute-start(f32[104,128]{1,0:T(8,128)S(1)} %fusion.6.refs_0_), channel_id=1, source_target_pairs={{0,32},{16,48},{32,0},{48,16},{64,96},{80,112},{96,64},{112,80},{1... | collective-permute-start | bytes 159752 | tf_op jit(solution)/shard_map/ppermute | solution.py:386
  52.5 6.3 %collective-permute-start.10 = (f32[104,128]{1,0:T(8,128)S(1)}, f32[104,128]{1,0:T(8,128)S(1)}, u32[]{:S(2)}, u32[]{:S(2)}) collective-permute-start(f32[104,128]{1,0:T(8,128)S(1)} %fusion.6.refs_0_), channel_id=1, source_target_pairs={{0,16},{16,32},{32,48},{48,0},{64,80},{80,96},{96,112},{112,64},{1... | collective-permute-start | bytes 159752 | tf_op jit(solution)/shard_map/ppermute | solution.py:386
  63.3 5.7 %collective-permute-start.13 = (f32[104,128]{1,0:T(8,128)S(1)}, f32[104,128]{1,0:T(8,128)S(1)}, u32[]{:S(2)}, u32[]{:S(2)}) collective-permute-start(f32[104,128]{1,0:T(8,128)S(1)} %get-tuple-element.41), channel_id=1, source_target_pairs={{0,32},{16,48},{32,0},{48,16},{64,96},{80,112},{96,64},{112,80},{1... | collective-permute-start | bytes 159752 | tf_op jit(solution)/shard_map/ppermute | solution.py:386
  65.8 5.3 %collective-permute-start.14 = (f32[104,128]{1,0:T(8,128)S(1)}, f32[104,128]{1,0:T(8,128)S(1)}, u32[]{:S(2)}, u32[]{:S(2)}) collective-permute-start(f32[104,128]{1,0:T(8,128)S(1)} %get-tuple-element.42), channel_id=1, source_target_pairs={{0,16},{16,32},{32,48},{48,0},{64,80},{80,96},{96,112},{112,64},{1... | collective-permute-start | bytes 159752 | tf_op jit(solution)/shard_map/ppermute | solution.py:386
  65.8 5.3 %collective-permute-start.15 = (f32[104,128]{1,0:T(8,128)S(1)}, f32[104,128]{1,0:T(8,128)S(1)}, u32[]{:S(2)}, u32[]{:S(2)}) collective-permute-start(f32[104,128]{1,0:T(8,128)S(1)} %get-tuple-element.43), channel_id=1, source_target_pairs={{0,48},{16,0},{32,16},{48,32},{64,112},{80,64},{96,80},{112,96},{1... | collective-permute-start | bytes 159752 | tf_op jit(solution)/shard_map/ppermute | solution.py:386
  71.2 7.1 %collective-permute-start.18 = (f32[104,128]{1,0:T(8,128)S(1)}, f32[104,128]{1,0:T(8,128)S(1)}, u32[]{:S(2)}, u32[]{:S(2)}) collective-permute-start(f32[104,128]{1,0:T(8,128)S(1)} %add_add_fusion.2), channel_id=1, source_target_pairs={{0,192},{16,208},{32,224},{48,240},{64,0},{80,16},{96,32},{112,48}... | collective-permute-start | bytes 159752 | tf_op jit(solution)/shard_map/ppermute | solution.py:391
  75.8 6.2 %collective-permute-start.17 = (f32[104,128]{1,0:T(8,128)S(1)}, f32[104,128]{1,0:T(8,128)S(1)}, u32[]{:S(2)}, u32[]{:S(2)}) collective-permute-start(f32[104,128]{1,0:T(8,128)S(1)} %add_add_fusion.2), channel_id=1, source_target_pairs={{0,64},{16,80},{32,96},{48,112},{64,128},{80,144},{96,160},{112,17... | collective-permute-start | bytes 159752 | tf_op jit(solution)/shard_map/ppermute | solution.py:391
  75.8 8.0 %collective-permute-start.16 = (f32[104,128]{1,0:T(8,128)S(1)}, f32[104,128]{1,0:T(8,128)S(1)}, u32[]{:S(2)}, u32[]{:S(2)}) collective-permute-start(f32[104,128]{1,0:T(8,128)S(1)} %add_add_fusion.2), channel_id=1, source_target_pairs={{0,128},{16,144},{32,160},{48,176},{64,192},{80,208},{96,224},{112... | collective-permute-start | bytes 159752 | tf_op jit(solution)/shard_map/ppermute | solution.py:391
  83.9 5.9 %collective-permute-start.21 = (f32[104,128]{1,0:T(8,128)S(1)}, f32[104,128]{1,0:T(8,128)S(1)}, u32[]{:S(2)}, u32[]{:S(2)}) collective-permute-start(f32[104,128]{1,0:T(8,128)S(1)} %fusion.15.refs_0_), channel_id=1, source_target_pairs={{0,48},{16,0},{32,16},{48,32},{64,112},{80,64},{96,80},{112,96},{1... | collective-permute-start | bytes 159752 | tf_op jit(solution)/shard_map/ppermute | solution.py:386
  87.2 5.7 %collective-permute-start.20 = (f32[104,128]{1,0:T(8,128)S(1)}, f32[104,128]{1,0:T(8,128)S(1)}, u32[]{:S(2)}, u32[]{:S(2)}) collective-permute-start(f32[104,128]{1,0:T(8,128)S(1)} %fusion.15.refs_0_), channel_id=1, source_target_pairs={{0,32},{16,48},{32,0},{48,16},{64,96},{80,112},{96,64},{112,80},{1... | collective-permute-start | bytes 159752 | tf_op jit(solution)/shard_map/ppermute | solution.py:386
  87.2 5.9 %collective-permute-start.19 = (f32[104,128]{1,0:T(8,128)S(1)}, f32[104,128]{1,0:T(8,128)S(1)}, u32[]{:S(2)}, u32[]{:S(2)}) collective-permute-start(f32[104,128]{1,0:T(8,128)S(1)} %fusion.15.refs_0_), channel_id=1, source_target_pairs={{0,16},{16,32},{32,48},{48,0},{64,80},{80,96},{96,112},{112,64},{1... | collective-permute-start | bytes 159752 | tf_op jit(solution)/shard_map/ppermute | solution.py:386
  98.5 5.4 %collective-permute-start.22 = (f32[64,128]{1,0:T(8,128)S(1)}, f32[64,128]{1,0:T(8,128)S(1)}, u32[]{:S(2)}, u32[]{:S(2)}) collective-permute-start(f32[64,128]{1,0:T(8,128)S(1)} %get-tuple-element.46), channel_id=1, source_target_pairs={{0,32},{16,48},{32,0},{48,16},{64,96},{80,112},{96,64},{112,80},{1... | collective-permute-start | bytes 98312 | tf_op jit(solution)/shard_map/ppermute | solution.py:386
  100.3 5.1 %collective-permute-start.23 = (f32[64,128]{1,0:T(8,128)S(1)}, f32[64,128]{1,0:T(8,128)S(1)}, u32[]{:S(2)}, u32[]{:S(2)}) collective-permute-start(f32[64,128]{1,0:T(8,128)S(1)} %get-tuple-element.47), channel_id=1, source_target_pairs={{0,16},{16,32},{32,48},{48,0},{64,80},{80,96},{96,112},{112,64},{1... | collective-permute-start | bytes 98312 | tf_op jit(solution)/shard_map/ppermute | solution.py:386
  100.3 5.1 %collective-permute-start.24 = (f32[64,128]{1,0:T(8,128)S(1)}, f32[64,128]{1,0:T(8,128)S(1)}, u32[]{:S(2)}, u32[]{:S(2)}) collective-permute-start(f32[64,128]{1,0:T(8,128)S(1)} %get-tuple-element.48), channel_id=1, source_target_pairs={{0,48},{16,0},{32,16},{48,32},{64,112},{80,64},{96,80},{112,96},{1... | collective-permute-start | bytes 98312 | tf_op jit(solution)/shard_map/ppermute | solution.py:386
  105.4 6.7 %collective-permute-start.27 = (f32[64,128]{1,0:T(8,128)S(1)}, f32[64,128]{1,0:T(8,128)S(1)}, u32[]{:S(2)}, u32[]{:S(2)}) collective-permute-start(f32[64,128]{1,0:T(8,128)S(1)} %add_add_fusion.3), channel_id=1, source_target_pairs={{0,192},{16,208},{32,224},{48,240},{64,0},{80,16},{96,32},{112,48}... | collective-permute-start | bytes 98312 | tf_op jit(solution)/shard_map/ppermute | solution.py:391
  109.6 6.0 %collective-permute-start.26 = (f32[64,128]{1,0:T(8,128)S(1)}, f32[64,128]{1,0:T(8,128)S(1)}, u32[]{:S(2)}, u32[]{:S(2)}) collective-permute-start(f32[64,128]{1,0:T(8,128)S(1)} %add_add_fusion.3), channel_id=1, source_target_pairs={{0,64},{16,80},{32,96},{48,112},{64,128},{80,144},{96,160},{112,17... | collective-permute-start | bytes 98312 | tf_op jit(solution)/shard_map/ppermute | solution.py:391
  109.6 7.8 %collective-permute-start.25 = (f32[64,128]{1,0:T(8,128)S(1)}, f32[64,128]{1,0:T(8,128)S(1)}, u32[]{:S(2)}, u32[]{:S(2)}) collective-permute-start(f32[64,128]{1,0:T(8,128)S(1)} %add_add_fusion.3), channel_id=1, source_target_pairs={{0,128},{16,144},{32,160},{48,176},{64,192},{80,208},{96,224},{112... | collective-permute-start | bytes 98312 | tf_op jit(solution)/shard_map/ppermute | solution.py:391
  117.5 4.9 %collective-permute-start.30 = (f32[64,128]{1,0:T(8,128)S(1)}, f32[64,128]{1,0:T(8,128)S(1)}, u32[]{:S(2)}, u32[]{:S(2)}) collective-permute-start(f32[64,128]{1,0:T(8,128)S(1)} %fusion.26.refs_0_), channel_id=1, source_target_pairs={{0,48},{16,0},{32,16},{48,32},{64,112},{80,64},{96,80},{112,96},{1... | collective-permute-start | bytes 98312 | tf_op jit(solution)/shard_map/ppermute | solution.py:386
  120.8 5.5 %collective-permute-start.29 = (f32[64,128]{1,0:T(8,128)S(1)}, f32[64,128]{1,0:T(8,128)S(1)}, u32[]{:S(2)}, u32[]{:S(2)}) collective-permute-start(f32[64,128]{1,0:T(8,128)S(1)} %fusion.26.refs_0_), channel_id=1, source_target_pairs={{0,32},{16,48},{32,0},{48,16},{64,96},{80,112},{96,64},{112,80},{1... | collective-permute-start | bytes 98312 | tf_op jit(solution)/shard_map/ppermute | solution.py:386
  120.8 5.5 %collective-permute-start.28 = (f32[64,128]{1,0:T(8,128)S(1)}, f32[64,128]{1,0:T(8,128)S(1)}, u32[]{:S(2)}, u32[]{:S(2)}) collective-permute-start(f32[64,128]{1,0:T(8,128)S(1)} %fusion.26.refs_0_), channel_id=1, source_target_pairs={{0,16},{16,32},{32,48},{48,0},{64,80},{80,96},{96,112},{112,64},{1... | collective-permute-start | bytes 98312 | tf_op jit(solution)/shard_map/ppermute | solution.py:386

commit v4 on v3

--- a/solution.py
+++ b/solution.py
@@ -42,21 +42,12 @@
     return weights
 
 
-def place_in_space():
-    place = lax.axis_index("space")
-    return place >> 2, place & 3
-
-
-def owner():
-    return lax.axis_index("gas") & 3
-
-
 def load_kernel(*refs):
-    planes, up, down, sems = refs[6:]
+    me, planes, up, down, sems = refs[6:]
     copies = []
     sources = [(refs[f].at[gas, 0], 4 * f + 2 * gas, 2) for f in range(3) for gas in range(2)]
     sources.append((refs[3].at[0], 12, 2))
-    layer = owner() >> 1
+    layer = me[0] >> 1
     sources += [(refs[4 + f].at[0, pl.ds(layer, 1)], 14 + f, 1) for f in range(2)]
     for source, first, layers in sources:
         for row, count, out in ((TILE - HALO, HALO, up), (0, HALO, down), (0, TILE, planes)):
@@ -76,8 +67,8 @@
     return pack, lane, [pack] if lane + HALO <= TILE else [pack, pack + 1]
 
 
-def pack_y_kernel(planes, top, bottom, first, second):
-    tile_row, column = place_in_space()
+def pack_y_kernel(planes, top, bottom, tile_row_ref, column_ref, first, second):
+    tile_row, column = tile_row_ref[0], column_ref[0]
     odd = (column & 1) == 1
     for row in range(0, ROWS, 8):
         lane = lax.broadcasted_iota(jnp.int32, (8, TILE), 1)
@@ -130,9 +121,9 @@
             field[z, 1, pl.ds(row, 8), :] = pltpu.roll(packed, (TILE - SIDE - 32 * (k // 3)) % TILE, 1)
 
 
-def own_chunk(out, layer):
+def own_chunk(me, out, layer):
     lane = lax.broadcasted_iota(jnp.int32, (8, TILE), 1)
-    half = owner() & 1
+    half = me[0] & 1
     low, high = chunk_rows(0), chunk_rows(1)
     rows = [pl.multiple_of(a + (b - a) * half, 8) for a, b in zip(low, high)]
     for k, row in enumerate(rows):
@@ -145,18 +136,18 @@
         out[pl.ds(FULL + 8 * slot_of, 8), :] = packed
 
 
-def turn(k):
-    return (owner() + k) & 3
-
-
-def send_chunks(chunks, outs):
+def turn(me, k):
+    return (me[0] + k) & 3
+
+
+def send_chunks(me, chunks, outs):
     for k, out in enumerate(outs):
-        out[...] = chunks[turn(k)]
-
-
-def gather_chunks(chunks, parts):
-    for k, part in enumerate(parts):
-        chunks[turn(RING - k)] = part[...]
+        out[...] = chunks[turn(me, k)]
+
+
+def gather_chunks(me, chunks, parts):
+    for k, part in zip(BACK, parts):
+        chunks[turn(me, RING - k)] = part[...]
 
 
 def fourth(value):
@@ -225,11 +216,11 @@
     each_step(8, ROWS - 8, body)
 
 
-def first_kernel(planes, top, bottom, first, second, *refs):
+def first_kernel(planes, top, bottom, first, second, me, tile_row_ref, column_ref, *refs):
     a, q, kap, now, held, *outs = refs[: 5 + RING]
     tis, sp, t4, old, begin, sums = refs[5 + RING :]
     planck = now
-    tile_row, column = place_in_space()
+    tile_row, column = tile_row_ref[0], column_ref[0]
     odd = (column & 1) == 1
 
     def place(p):
@@ -265,9 +256,9 @@
             dst[at, 1, pl.ds(r + pad, STEP), :] = value
 
     each_step(0, ROWS, sides)
-    own_chunk(held.at[0], tis.at[owner() >> 1])
-    own_chunk(held.at[1], tis.at[2])
-    own_chunk(held.at[2], tis.at[3])
+    own_chunk(me, held.at[0], tis.at[me[0] >> 1])
+    own_chunk(me, held.at[1], tis.at[2])
+    own_chunk(me, held.at[2], tis.at[3])
 
     def halves(r):
         lane = lax.broadcasted_iota(jnp.int32, (STEP, TILE), 1)
@@ -314,26 +305,26 @@
     solve(0, a, q, t4, sp, begin, now, old)
     absorb(kap, now, t4)
     chunk_out(sums, t4)
-    send_chunks(sums, outs)
+    send_chunks(me, sums, outs)
 
 
 def next_kernel(a, q, kap, start, *refs):
-    parts = refs[:RING]
-    now, *outs = refs[RING : 2 * RING + 1]
-    sp, t4, old, sums = refs[2 * RING + 1 :]
-    gather_chunks(sums, parts)
+    parts, me = refs[:RING], refs[RING]
+    now, *outs = refs[RING + 1 : 2 * RING + 2]
+    sp, t4, old, sums = refs[2 * RING + 2 :]
+    gather_chunks(me, sums, parts)
     chunk_in(t4, sums, fourth)
     solve(1, a, q, t4, sp, start, now, old)
     absorb(kap, now, t4)
     chunk_out(sums, t4)
-    send_chunks(sums, outs)
+    send_chunks(me, sums, outs)
 
 
 def last_kernel(a, q, kap, start, *refs):
-    parts = refs[:RING]
-    radiation, *outs = refs[RING : 2 * RING + 1]
-    sp, t4, old, now, sums = refs[2 * RING + 1 :]
-    gather_chunks(sums, parts)
+    parts, me = refs[:RING], refs[RING]
+    radiation, *outs = refs[RING + 1 : 2 * RING + 2]
+    sp, t4, old, now, sums = refs[2 * RING + 2 :]
+    gather_chunks(me, sums, parts)
     chunk_in(t4, sums, fourth)
     solve(2, a, q, t4, sp, start, now, old)
     rows = pl.ds(PAD + HALO, TILE)
@@ -346,12 +337,12 @@
             kap[z, 0, part, :] * now[z, 0, part, :] + kap[2 + z, 0, part, :] * now[2 + z, 0, part, :]
         )
     for k, out in enumerate(outs):
-        out[...] = sums[turn(k), pl.ds(0, MAIN), :]
+        out[...] = sums[turn(me, k), pl.ds(0, MAIN), :]
 
 
 def final_kernel(*refs):
-    parts, out = refs[:RING], refs[RING]
-    gather_chunks(out, parts)
+    parts, me, out = refs[:RING], refs[RING], refs[RING + 1]
+    gather_chunks(me, out, parts)
 
 
 def corrected(current, earlier, inertia, source, emitted, taken):
@@ -365,7 +356,9 @@
         return pl.pallas_call(
             kernel,
             out_shape=[jax.ShapeDtypeStruct(dims, F32) for dims in outs],
-            in_specs=[pl.BlockSpec(memory_space=space)] * len(args),
+            in_specs=[
+                pl.BlockSpec(memory_space=pltpu.SMEM if array.dtype == jnp.int32 else space) for array in args
+            ],
             out_specs=[pl.BlockSpec(memory_space=pltpu.VMEM)] * len(outs),
             scratch_shapes=[pltpu.VMEM(s, F32) if isinstance(s, tuple) else s for s in scratch],
             compiler_params=pltpu.CompilerParams(vmem_limit_bytes=VMEM_LIMIT),
@@ -378,7 +371,7 @@
 PADDED = (4, 2, ROWS + 2 * PAD, TILE)
 SHARED = (2, 2, ROWS, TILE)
 OUT_TURNS = (2, 1, 3)
-BACK_TURNS = (1, 3, 2)
+BACK = (0, 1, 3, 2)
 
 
 def along_y(array, by):
@@ -395,13 +388,12 @@
     total = parts[0]
     for k in OUT_TURNS:
         total = total + along_y(parts[k], k)
-    parts = [along_z(total, k) for k in (2, 1, 3)]
+    parts = [along_z(total, k) for k in (3, 1, 2)]
     return total + parts[0] + parts[1] + parts[2]
 
 
 def spread(chunk):
-    parts = {k: along_y(chunk, k) for k in BACK_TURNS}
-    return [chunk] + [parts[k] for k in range(1, RING)]
+    return [along_y(chunk, k) if k else chunk for k in BACK]
 
 
 def on_device(*inputs):
@@ -409,16 +401,19 @@
     own = (extinction, fractions, irradiance, kelvin, inertia, source)
     own = [pltpu.with_memory_space_constraint(array, pltpu.HBM) for array in own]
     devices = lax.axis_size("space")
+    me = (lax.axis_index("gas") & 3).reshape(1)
+    place = lax.axis_index("space")
+    at = ((place >> 2).reshape(1), (place & 3).reshape(1))
     planes, up, down = call(
         load_kernel,
         [(PLANES, TILE, TILE)] + [(PLANES, HALO, TILE)] * 2,
         [pltpu.SemaphoreType.DMA((27,))],
         space=pltpu.HBM,
-    )(*own)
+    )(*own, me)
     ring = [(i, (i + ACROSS) % devices) for i in range(devices)]
     top = lax.ppermute(up, "space", ring)
     bottom = lax.ppermute(down, "space", [(j, i) for i, j in ring])
-    first, second = call(pack_y_kernel, [(PACKS, ROWS, TILE)] * 2)(planes, top, bottom)
+    first, second = call(pack_y_kernel, [(PACKS, ROWS, TILE)] * 2)(planes, top, bottom, *at)
     first = lax.ppermute(first, "space", [(i, i ^ 1) for i in range(devices)])
     swaps = (0, 2, 1, 3)
     second = lax.ppermute(second, "space", [(i, i - i % ACROSS + swaps[i % ACROSS]) for i in range(devices)])
@@ -427,7 +422,7 @@
         first_kernel,
         [(5,) + FIELD, FIELD, PADDED, PADDED, (3, CHUNK, TILE)] + [two] * RING,
         [(4, 2, ROWS, TILE), FIELD, SHARED, PADDED, PADDED, (RING,) + two],
-    )(planes, top, bottom, first, second)
+    )(planes, top, bottom, first, second, me, *at)
     total = sum_over_gas(parts)
     taken, emitted = total[:CHUNK], total[CHUNK:]
     earlier, inertia, source = held[0], held[1], held[2]
@@ -435,16 +430,16 @@
     one = (CHUNK, TILE)
     now, *parts = call(
         next_kernel, [PADDED] + [one] * RING, [FIELD, SHARED, PADDED, (RING,) + one]
-    )(a, q, kap, now, *spread(current))
+    )(a, q, kap, now, *spread(current), me)
     current = corrected(current, earlier, inertia, source, emitted, sum_over_gas(parts))
     radiation, *parts = call(
         last_kernel,
         [(2, 1, 2, TILE, TILE)] + [(MAIN, TILE)] * RING,
         [FIELD, SHARED, PADDED, PADDED, (RING,) + one],
-    )(a, q, kap, now, *spread(current))
+    )(a, q, kap, now, *spread(current), me)
     rest = (value[:MAIN] for value in (current, earlier, inertia, source, emitted))
     current = corrected(*rest, sum_over_gas(parts))
-    (final,) = call(final_kernel, [(RING, MAIN, TILE)])(*spread(current))
+    (final,) = call(final_kernel, [(RING, MAIN, TILE)])(*spread(current), me)
     return final.reshape(1, 2, TILE, TILE), radiation
 
 

time: 127 us -> 122 us (0.961)
  waiting for transfers between devices: 48 us -> 41.7 us
    ppermute x9, waiting for transfers between devices: 15.9 us -> 10.9 us  [along_z(): return lax.ppermute(array, 'gas', pairs)]
    ppermute x18, waiting for transfers between devices: 21.5 us -> 20.2 us  [along_y(): return lax.ppermute(array, 'gas', pairs)]
  transfers between devices with their start and end apart: 31 -> 31, of which waited for: 20 -> 24; matrix products, arithmetic and copies ran while one was open for 0% -> 0% of each run, Pallas kernels for 0% -> 0%
where the time goes in v4:
time: 122 us
  starting transfers between devices  58.3 us (48%)
  waiting for transfers between devices  41.7 us (34%)
  Pallas kernels  20.8 us (17%)
    ppermute x18, starting transfers between devices, along_y(): return lax.ppermute(array, 'gas', pairs)  29.5 us
    ppermute x9, starting transfers between devices, along_z(): return lax.ppermute(array, 'gas', pairs)  23.5 us
    pallas_call x6, Pallas kernels, run(): pl.pallas_call(kernel, out_shape=[jax.ShapeDtypeStruct(dims, F32) for dim...  20.8 us
    ppermute x18, waiting for transfers between devices, along_y(): return lax.ppermute(array, 'gas', pairs)  20.2 us
    ppermute x9, waiting for transfers between devices, along_z(): return lax.ppermute(array, 'gas', pairs)  10.9 us
    ppermute x1, waiting for transfers between devices, on_device(): top = lax.ppermute(up, 'space', ring)  4.61 us
    ppermute x1, waiting for transfers between devices, on_device(): lax.ppermute(second, 'space', [(i, i - i % ACROSS + swaps[i % ACROSS]) fo...  4.61 us
    ppermute x1, starting transfers between devices, on_device(): lax.ppermute(second, 'space', [(i, i - i % ACROSS + swaps[i % ACROSS]) fo...  3.15 us
  transfers between devices with their start and end apart: 31, of which 24 were waited for; matrix products, arithmetic and copies ran while one was open for 0% of the time, Pallas kernels for 0%

profile of v4, /device:TPU:38, one launch (start us, length us, event | category | flops | bytes accessed | tf_op | source)
XLA Modules:
  0.0 121.8 jit_solution(5508635156880453788)
XLA Ops:
  0.6 1.6 %shard_map.77 = (f32[16,128,128]{2,1,0:T(8,128)S(1)}, f32[16,24,128]{2,1,0:T(8,128)S(1)}, f32[16,24,128]{2,1,0:T(8,128)S(1)}) custom-call(f32[2,1,2,128,128]{4,3,2,1,0:T(8,128)} %refs_0_.1, f32[2,1,2,128,128]{4,3,2,1,0:T(8,128)} %refs_1_.1, f32[2,1,2,128,128]{4,3,2,1,0:T(8,128)} %refs_2_.1, f32[1,2,128,128]{3,2,1,0:T(8,128)} %refs_3_.1, ...), custom_call_target="tpu_custom_call" | custom-call | tf_op jit(solution)/shard_map/pallas_call | solution.py:356
  2.8 1.5 %collective-permute-start.1 = (f32[16,24,128]{2,1,0:T(8,128)S(1)}, f32[16,24,128]{2,1,0:T(8,128)S(1)}, u32[]{:S(2)}, u32[]{:S(2)}) collective-permute-start(f32[16,24,128]{2,1,0:T(8,128)S(1)} %get-tuple-element.28), channel_id=1, source_target_pairs={{4,0},{5,1},{6,2},{7,3},{8,4},{9,5},{10,6},{11,7},{12,8},{13,9},{1... | collective-permute-start | bytes 589832 | tf_op jit(solution)/shard_map/ppermute | solution.py:415
  4.4 4.6 %collective-permute-done.top = f32[16,24,128]{2,1,0:T(8,128)S(1)} collective-permute-done((f32[16,24,128]{2,1,0:T(8,128)S(1)}, f32[16,24,128]{2,1,0:T(8,128)S(1)}, u32[]{:S(2)}, u32[]{:S(2)}) %collective-permute-start) | collective-permute-done | bytes 196640 | tf_op jit(solution)/shard_map/ppermute | solution.py:414
  9.0 1.4 %collective-permute-done.1.bottom = f32[16,24,128]{2,1,0:T(8,128)S(1)} collective-permute-done((f32[16,24,128]{2,1,0:T(8,128)S(1)}, f32[16,24,128]{2,1,0:T(8,128)S(1)}, u32[]{:S(2)}, u32[]{:S(2)}) %collective-permute-start.1) | collective-permute-done | bytes 196640 | tf_op jit(solution)/shard_map/ppermute | solution.py:415
  11.3 3.2 %collective-permute-start.3 = (f32[3,176,128]{2,1,0:T(8,128)S(1)}, f32[3,176,128]{2,1,0:T(8,128)S(1)}, u32[]{:S(2)}, u32[]{:S(2)}) collective-permute-start(f32[3,176,128]{2,1,0:T(8,128)S(1)} %get-tuple-element.30), channel_id=1, source_target_pairs={{0,0},{1,2},{2,1},{3,3},{4,4},{5,6},{6,5},{7,7},{8,8},{9,10},{10,9... | collective-permute-start | bytes 811016 | tf_op jit(solution)/shard_map/ppermute | solution.py:419
  14.4 4.6 %collective-permute-done.3.second = f32[3,176,128]{2,1,0:T(8,128)S(1)} collective-permute-done((f32[3,176,128]{2,1,0:T(8,128)S(1)}, f32[3,176,128]{2,1,0:T(8,128)S(1)}, u32[]{:S(2)}, u32[]{:S(2)}) %collective-permute-start.3) | collective-permute-done | bytes 270368 | tf_op jit(solution)/shard_map/ppermute | solution.py:419
  19.0 7.2 %shard_map.79 = (f32[5,4,2,176,128]{4,3,2,1,0:T(8,128)S(1)}, f32[4,2,176,128]{3,2,1,0:T(8,128)S(1)}, f32[4,2,192,128]{3,2,1,0:T(8,128)S(1)}, f32[4,2,192,128]{3,...) custom-call(f32[16,128,128]{2,1,0:T(8,128)S(1)} %get-tuple-element.2, ...), custom_call_target="tpu_custom_call" | custom-call | tf_op jit(solution)/shard_map/pallas_call | solution.py:356
  26.2 3.3 %collective-permute-start.4 = (f32[208,128]{1,0:T(8,128)S(1)}, f32[208,128]{1,0:T(8,128)S(1)}, u32[]{:S(2)}, u32[]{:S(2)}) collective-permute-start(f32[208,128]{1,0:T(8,128)S(1)} %get-tuple-element.33), channel_id=1, source_target_pairs={{0,32},{16,48},{32,0},{48,16},{64,96},{80,112},{96,64},{112,80},{1... | collective-permute-start | bytes 319496 | tf_op jit(solution)/shard_map/ppermute | solution.py:379
  30.2 2.6 %collective-permute-start.6 = (f32[208,128]{1,0:T(8,128)S(1)}, f32[208,128]{1,0:T(8,128)S(1)}, u32[]{:S(2)}, u32[]{:S(2)}) collective-permute-start(f32[208,128]{1,0:T(8,128)S(1)} %get-tuple-element.35), channel_id=1, source_target_pairs={{0,48},{16,0},{32,16},{48,32},{64,112},{80,64},{96,80},{112,96},{1... | collective-permute-start | bytes 319496 | tf_op jit(solution)/shard_map/ppermute | solution.py:379
  32.7 2.7 %collective-permute-done.5 = f32[208,128]{1,0:T(8,128)S(1)} collective-permute-done((f32[208,128]{1,0:T(8,128)S(1)}, f32[208,128]{1,0:T(8,128)S(1)}, u32[]{:S(2)}, u32[]{:S(2)}) %collective-permute-start.5) | collective-permute-done | bytes 106528 | tf_op jit(solution)/shard_map/ppermute | solution.py:379
  35.5 6.4 %collective-permute-start.9 = (f32[208,128]{1,0:T(8,128)S(1)}, f32[208,128]{1,0:T(8,128)S(1)}, u32[]{:S(2)}, u32[]{:S(2)}) collective-permute-start(f32[208,128]{1,0:T(8,128)S(1)} %add_add_fusion.1), channel_id=1, source_target_pairs={{0,128},{16,144},{32,160},{48,176},{64,192},{80,208},{96,224},{112... | collective-permute-start | bytes 319496 | tf_op jit(solution)/shard_map/ppermute | solution.py:384
  41.8 1.5 %collective-permute-start.8 = (f32[208,128]{1,0:T(8,128)S(1)}, f32[208,128]{1,0:T(8,128)S(1)}, u32[]{:S(2)}, u32[]{:S(2)}) collective-permute-start(f32[208,128]{1,0:T(8,128)S(1)} %add_add_fusion.1), channel_id=1, source_target_pairs={{0,64},{16,80},{32,96},{48,112},{64,128},{80,144},{96,160},{112,17... | collective-permute-start | bytes 319496 | tf_op jit(solution)/shard_map/ppermute | solution.py:384
  43.3 2.7 %collective-permute-start.7 = (f32[208,128]{1,0:T(8,128)S(1)}, f32[208,128]{1,0:T(8,128)S(1)}, u32[]{:S(2)}, u32[]{:S(2)}) collective-permute-start(f32[208,128]{1,0:T(8,128)S(1)} %add_add_fusion.1), channel_id=1, source_target_pairs={{0,192},{16,208},{32,224},{48,240},{64,0},{80,16},{96,32},{112,48}... | collective-permute-start | bytes 319496 | tf_op jit(solution)/shard_map/ppermute | solution.py:384
  46.0 2.7 %collective-permute-done.8 = f32[208,128]{1,0:T(8,128)S(1)} collective-permute-done((f32[208,128]{1,0:T(8,128)S(1)}, f32[208,128]{1,0:T(8,128)S(1)}, u32[]{:S(2)}, u32[]{:S(2)}) %collective-permute-start.8) | collective-permute-done | bytes 106528 | tf_op jit(solution)/shard_map/ppermute | solution.py:384
  49.0 1.5 %collective-permute-start.12 = (f32[104,128]{1,0:T(8,128)S(1)}, f32[104,128]{1,0:T(8,128)S(1)}, u32[]{:S(2)}, u32[]{:S(2)}) collective-permute-start(f32[104,128]{1,0:T(8,128)S(1)} %fusion.6.refs_0_), channel_id=1, source_target_pairs={{0,32},{16,48},{32,0},{48,16},{64,96},{80,112},{96,64},{112,80},{1... | collective-permute-start | bytes 159752 | tf_op jit(solution)/shard_map/ppermute | solution.py:379
  50.5 1.9 %collective-permute-start.11 = (f32[104,128]{1,0:T(8,128)S(1)}, f32[104,128]{1,0:T(8,128)S(1)}, u32[]{:S(2)}, u32[]{:S(2)}) collective-permute-start(f32[104,128]{1,0:T(8,128)S(1)} %fusion.6.refs_0_), channel_id=1, source_target_pairs={{0,48},{16,0},{32,16},{48,32},{64,112},{80,64},{96,80},{112,96},{1... | collective-permute-start | bytes 159752 | tf_op jit(solution)/shard_map/ppermute | solution.py:379
  53.2 1.5 %collective-permute-done.12.refs_3_ = f32[104,128]{1,0:T(8,128)S(1)} collective-permute-done((f32[104,128]{1,0:T(8,128)S(1)}, f32[104,128]{1,0:T(8,128)S(1)}, u32[]{:S(2)}, u32[]{:S(2)}) %collective-permute-start.12) | collective-permute-done | bytes 53280 | tf_op jit(solution)/shard_map/ppermute | solution.py:379
  54.7 1.2 collective-permute-done.11.refs_2_
  55.9 1.9 %collective-permute-done.10.refs_1_ = f32[104,128]{1,0:T(8,128)S(1)} collective-permute-done((f32[104,128]{1,0:T(8,128)S(1)}, f32[104,128]{1,0:T(8,128)S(1)}, u32[]{:S(2)}, u32[]{:S(2)}) %collective-permute-start.10) | collective-permute-done | bytes 53280 | tf_op jit(solution)/shard_map/ppermute | solution.py:379
  57.8 5.0 %shard_map.80 = (f32[4,2,192,128]{3,2,1,0:T(8,128)S(1)}, f32[104,128]{1,0:T(8,128)S(1)}, f32[104,128]{1,0:T(8,128)S(1)}, f32[104,128]{1,0:T(8,128)S(1)}, f32[104,128]{1,0:T(8,128)S(1)}) custom-call(f32[5,4,2,176,128]{4,3,2,1,0:T(8,128)S(1)} %get-tuple-element.36.a, f32[4,2,176,128]{3,2,1,0:T(8,128)S(1)} %get-tuple-element.37.q, ...), custom_call_target="tpu_custom_call" | custom-call | tf_op jit(solution)/shard_map/pallas_call | solution.py:356
  62.8 1.7 %collective-permute-start.13 = (f32[104,128]{1,0:T(8,128)S(1)}, f32[104,128]{1,0:T(8,128)S(1)}, u32[]{:S(2)}, u32[]{:S(2)}) collective-permute-start(f32[104,128]{1,0:T(8,128)S(1)} %get-tuple-element.41), channel_id=1, source_target_pairs={{0,32},{16,48},{32,0},{48,16},{64,96},{80,112},{96,64},{112,80},{1... | collective-permute-start | bytes 159752 | tf_op jit(solution)/shard_map/ppermute | solution.py:379
  64.5 3.2 %collective-permute-start.15 = (f32[104,128]{1,0:T(8,128)S(1)}, f32[104,128]{1,0:T(8,128)S(1)}, u32[]{:S(2)}, u32[]{:S(2)}) collective-permute-start(f32[104,128]{1,0:T(8,128)S(1)} %get-tuple-element.43), channel_id=1, source_target_pairs={{0,48},{16,0},{32,16},{48,32},{64,112},{80,64},{96,80},{112,96},{1... | collective-permute-start | bytes 159752 | tf_op jit(solution)/shard_map/ppermute | solution.py:379
  68.5 1.3 %collective-permute-done.14 = f32[104,128]{1,0:T(8,128)S(1)} collective-permute-done((f32[104,128]{1,0:T(8,128)S(1)}, f32[104,128]{1,0:T(8,128)S(1)}, u32[]{:S(2)}, u32[]{:S(2)}) %collective-permute-start.14) | collective-permute-done | bytes 53280 | tf_op jit(solution)/shard_map/ppermute | solution.py:379
  69.8 3.9 %collective-permute-start.18 = (f32[104,128]{1,0:T(8,128)S(1)}, f32[104,128]{1,0:T(8,128)S(1)}, u32[]{:S(2)}, u32[]{:S(2)}) collective-permute-start(f32[104,128]{1,0:T(8,128)S(1)} %add_add_fusion.2), channel_id=1, source_target_pairs={{0,128},{16,144},{32,160},{48,176},{64,192},{80,208},{96,224},{112... | collective-permute-start | bytes 159752 | tf_op jit(solution)/shard_map/ppermute | solution.py:384
  73.7 2.7 %collective-permute-start.17 = (f32[104,128]{1,0:T(8,128)S(1)}, f32[104,128]{1,0:T(8,128)S(1)}, u32[]{:S(2)}, u32[]{:S(2)}) collective-permute-start(f32[104,128]{1,0:T(8,128)S(1)} %add_add_fusion.2), channel_id=1, source_target_pairs={{0,64},{16,80},{32,96},{48,112},{64,128},{80,144},{96,160},{112,17... | collective-permute-start | bytes 159752 | tf_op jit(solution)/shard_map/ppermute | solution.py:384
  76.4 1.5 %collective-permute-start.16 = (f32[104,128]{1,0:T(8,128)S(1)}, f32[104,128]{1,0:T(8,128)S(1)}, u32[]{:S(2)}, u32[]{:S(2)}) collective-permute-start(f32[104,128]{1,0:T(8,128)S(1)} %add_add_fusion.2), channel_id=1, source_target_pairs={{0,192},{16,208},{32,224},{48,240},{64,0},{80,16},{96,32},{112,48}... | collective-permute-start | bytes 159752 | tf_op jit(solution)/shard_map/ppermute | solution.py:384
  77.9 1.2 %collective-permute-done.18 = f32[104,128]{1,0:T(8,128)S(1)} collective-permute-done((f32[104,128]{1,0:T(8,128)S(1)}, f32[104,128]{1,0:T(8,128)S(1)}, u32[]{:S(2)}, u32[]{:S(2)}) %collective-permute-start.18) | collective-permute-done | bytes 53280 | tf_op jit(solution)/shard_map/ppermute | solution.py:384
  79.1 0.9 collective-permute-done.17
  80.0 1.4 %collective-permute-done.16 = f32[104,128]{1,0:T(8,128)S(1)} collective-permute-done((f32[104,128]{1,0:T(8,128)S(1)}, f32[104,128]{1,0:T(8,128)S(1)}, u32[]{:S(2)}, u32[]{:S(2)}) %collective-permute-start.16) | collective-permute-done | bytes 53280 | tf_op jit(solution)/shard_map/ppermute | solution.py:384
  81.5 1.3 %collective-permute-start.21 = (f32[104,128]{1,0:T(8,128)S(1)}, f32[104,128]{1,0:T(8,128)S(1)}, u32[]{:S(2)}, u32[]{:S(2)}) collective-permute-start(f32[104,128]{1,0:T(8,128)S(1)} %fusion.15.refs_0_), channel_id=1, source_target_pairs={{0,32},{16,48},{32,0},{48,16},{64,96},{80,112},{96,64},{112,80},{1... | collective-permute-start | bytes 159752 | tf_op jit(solution)/shard_map/ppermute | solution.py:379
  82.8 2.7 %collective-permute-start.20 = (f32[104,128]{1,0:T(8,128)S(1)}, f32[104,128]{1,0:T(8,128)S(1)}, u32[]{:S(2)}, u32[]{:S(2)}) collective-permute-start(f32[104,128]{1,0:T(8,128)S(1)} %fusion.15.refs_0_), channel_id=1, source_target_pairs={{0,48},{16,0},{32,16},{48,32},{64,112},{80,64},{96,80},{112,96},{1... | collective-permute-start | bytes 159752 | tf_op jit(solution)/shard_map/ppermute | solution.py:379
  85.5 0.8 collective-permute-start.19
  86.3 0.9 collective-permute-done.21.refs_3_
  87.2 1.7 %collective-permute-done.20.refs_2_ = f32[104,128]{1,0:T(8,128)S(1)} collective-permute-done((f32[104,128]{1,0:T(8,128)S(1)}, f32[104,128]{1,0:T(8,128)S(1)}, u32[]{:S(2)}, u32[]{:S(2)}) %collective-permute-start.20) | collective-permute-done | bytes 53280 | tf_op jit(solution)/shard_map/ppermute | solution.py:379
  89.0 1.9 %collective-permute-done.19.refs_1_ = f32[104,128]{1,0:T(8,128)S(1)} collective-permute-done((f32[104,128]{1,0:T(8,128)S(1)}, f32[104,128]{1,0:T(8,128)S(1)}, u32[]{:S(2)}, u32[]{:S(2)}) %collective-permute-start.19) | collective-permute-done | bytes 53280 | tf_op jit(solution)/shard_map/ppermute | solution.py:379
  90.9 5.6 %shard_map.81 = (f32[2,1,2,128,128]{4,3,2,1,0:T(8,128)}, f32[64,128]{1,0:T(8,128)S(1)}, f32[64,128]{1,0:T(8,128)S(1)}, f32[64,128]{1,0:T(8,128)S(1)}, f32[64,128]{1,0:T(8,128)S(1)}) custom-call(f32[5,4,2,176,128]{4,3,2,1,0:T(8,128)S(1)} %get-tuple-element.36.a, f32[4,2,176,128]{3,2,1,0:T(8,128)S(1)} %get-tuple-element.37.q, ...), custom_call_target="tpu_custom_call" | custom-call | tf_op jit(solution)/shard_map/pallas_call | solution.py:356
  96.4 1.6 %collective-permute-start.22 = (f32[64,128]{1,0:T(8,128)S(1)}, f32[64,128]{1,0:T(8,128)S(1)}, u32[]{:S(2)}, u32[]{:S(2)}) collective-permute-start(f32[64,128]{1,0:T(8,128)S(1)} %get-tuple-element.46), channel_id=1, source_target_pairs={{0,32},{16,48},{32,0},{48,16},{64,96},{80,112},{96,64},{112,80},{1... | collective-permute-start | bytes 98312 | tf_op jit(solution)/shard_map/ppermute | solution.py:379
  98.1 3.2 %collective-permute-start.24 = (f32[64,128]{1,0:T(8,128)S(1)}, f32[64,128]{1,0:T(8,128)S(1)}, u32[]{:S(2)}, u32[]{:S(2)}) collective-permute-start(f32[64,128]{1,0:T(8,128)S(1)} %get-tuple-element.48), channel_id=1, source_target_pairs={{0,48},{16,0},{32,16},{48,32},{64,112},{80,64},{96,80},{112,96},{1... | collective-permute-start | bytes 98312 | tf_op jit(solution)/shard_map/ppermute | solution.py:379
  101.9 1.3 %collective-permute-done.23 = f32[64,128]{1,0:T(8,128)S(1)} collective-permute-done((f32[64,128]{1,0:T(8,128)S(1)}, f32[64,128]{1,0:T(8,128)S(1)}, u32[]{:S(2)}, u32[]{:S(2)}) %collective-permute-start.23) | collective-permute-done | bytes 32800 | tf_op jit(solution)/shard_map/ppermute | solution.py:379
  103.2 0.8 collective-permute-start.27
  104.0 3.8 %collective-permute-start.26 = (f32[64,128]{1,0:T(8,128)S(1)}, f32[64,128]{1,0:T(8,128)S(1)}, u32[]{:S(2)}, u32[]{:S(2)}) collective-permute-start(f32[64,128]{1,0:T(8,128)S(1)} %add_add_fusion.3), channel_id=1, source_target_pairs={{0,64},{16,80},{32,96},{48,112},{64,128},{80,144},{96,160},{112,17... | collective-permute-start | bytes 98312 | tf_op jit(solution)/shard_map/ppermute | solution.py:384
  108.1 3.0 %collective-permute-done.27 = f32[64,128]{1,0:T(8,128)S(1)} collective-permute-done((f32[64,128]{1,0:T(8,128)S(1)}, f32[64,128]{1,0:T(8,128)S(1)}, u32[]{:S(2)}, u32[]{:S(2)}) %collective-permute-start.27) | collective-permute-done | bytes 32800 | tf_op jit(solution)/shard_map/ppermute | solution.py:384
  111.1 1.4 %collective-permute-done.25 = f32[64,128]{1,0:T(8,128)S(1)} collective-permute-done((f32[64,128]{1,0:T(8,128)S(1)}, f32[64,128]{1,0:T(8,128)S(1)}, u32[]{:S(2)}, u32[]{:S(2)}) %collective-permute-start.25) | collective-permute-done | bytes 32800 | tf_op jit(solution)/shard_map/ppermute | solution.py:384
  112.6 1.5 %collective-permute-start.30 = (f32[64,128]{1,0:T(8,128)S(1)}, f32[64,128]{1,0:T(8,128)S(1)}, u32[]{:S(2)}, u32[]{:S(2)}) collective-permute-start(f32[64,128]{1,0:T(8,128)S(1)} %fusion.26.refs_0_), channel_id=1, source_target_pairs={{0,32},{16,48},{32,0},{48,16},{64,96},{80,112},{96,64},{112,80},{1... | collective-permute-start | bytes 98312 | tf_op jit(solution)/shard_map/ppermute | solution.py:379
  114.1 1.9 %collective-permute-start.29 = (f32[64,128]{1,0:T(8,128)S(1)}, f32[64,128]{1,0:T(8,128)S(1)}, u32[]{:S(2)}, u32[]{:S(2)}) collective-permute-start(f32[64,128]{1,0:T(8,128)S(1)} %fusion.26.refs_0_), channel_id=1, source_target_pairs={{0,48},{16,0},{32,16},{48,32},{64,112},{80,64},{96,80},{112,96},{1... | collective-permute-start | bytes 98312 | tf_op jit(solution)/shard_map/ppermute | solution.py:379
  116.8 1.3 %collective-permute-done.30.refs_3_ = f32[64,128]{1,0:T(8,128)S(1)} collective-permute-done((f32[64,128]{1,0:T(8,128)S(1)}, f32[64,128]{1,0:T(8,128)S(1)}, u32[]{:S(2)}, u32[]{:S(2)}) %collective-permute-start.30) | collective-permute-done | bytes 32800 | tf_op jit(solution)/shard_map/ppermute | solution.py:379
  118.1 0.9 collective-permute-done.29.refs_2_
  119.0 2.1 %collective-permute-done.28.refs_1_ = f32[64,128]{1,0:T(8,128)S(1)} collective-permute-done((f32[64,128]{1,0:T(8,128)S(1)}, f32[64,128]{1,0:T(8,128)S(1)}, u32[]{:S(2)}, u32[]{:S(2)}) %collective-permute-start.28) | collective-permute-done | bytes 32800 | tf_op jit(solution)/shard_map/ppermute | solution.py:379
  (27 shorter events, 6.5 us)
Async XLA Ops:
  2.3 6.7 %collective-permute-start = (f32[16,24,128]{2,1,0:T(8,128)S(1)}, f32[16,24,128]{2,1,0:T(8,128)S(1)}, u32[]{:S(2)}, u32[]{:S(2)}) collective-permute-start(f32[16,24,128]{2,1,0:T(8,128)S(1)} %get-tuple-element.27), channel_id=1, source_target_pairs={{0,4},{1,5},{2,6},{3,7},{4,8},{5,9},{6,10},{7,11},{8,12},{9,13},{1... | collective-permute-start | bytes 589832 | tf_op jit(solution)/shard_map/ppermute | solution.py:414
  2.8 7.6 %collective-permute-start.1 = (f32[16,24,128]{2,1,0:T(8,128)S(1)}, f32[16,24,128]{2,1,0:T(8,128)S(1)}, u32[]{:S(2)}, u32[]{:S(2)}) collective-permute-start(f32[16,24,128]{2,1,0:T(8,128)S(1)} %get-tuple-element.28), channel_id=1, source_target_pairs={{4,0},{5,1},{6,2},{7,3},{8,4},{9,5},{10,6},{11,7},{12,8},{13,9},{1... | collective-permute-start | bytes 589832 | tf_op jit(solution)/shard_map/ppermute | solution.py:415
  11.2 3.3 %collective-permute-start.2 = (f32[3,176,128]{2,1,0:T(8,128)S(1)}, f32[3,176,128]{2,1,0:T(8,128)S(1)}, u32[]{:S(2)}, u32[]{:S(2)}) collective-permute-start(f32[3,176,128]{2,1,0:T(8,128)S(1)} %get-tuple-element.29), channel_id=1, source_target_pairs={{0,1},{1,0},{2,3},{3,2},{4,5},{5,4},{6,7},{7,6},{8,9},{9,8},{10,11... | collective-permute-start | bytes 811016 | tf_op jit(solution)/shard_map/ppermute | solution.py:417
  11.3 7.8 %collective-permute-start.3 = (f32[3,176,128]{2,1,0:T(8,128)S(1)}, f32[3,176,128]{2,1,0:T(8,128)S(1)}, u32[]{:S(2)}, u32[]{:S(2)}) collective-permute-start(f32[3,176,128]{2,1,0:T(8,128)S(1)} %get-tuple-element.30), channel_id=1, source_target_pairs={{0,0},{1,2},{2,1},{3,3},{4,4},{5,6},{6,5},{7,7},{8,8},{9,10},{10,9... | collective-permute-start | bytes 811016 | tf_op jit(solution)/shard_map/ppermute | solution.py:419
  26.2 6.5 %collective-permute-start.4 = (f32[208,128]{1,0:T(8,128)S(1)}, f32[208,128]{1,0:T(8,128)S(1)}, u32[]{:S(2)}, u32[]{:S(2)}) collective-permute-start(f32[208,128]{1,0:T(8,128)S(1)} %get-tuple-element.33), channel_id=1, source_target_pairs={{0,32},{16,48},{32,0},{48,16},{64,96},{80,112},{96,64},{112,80},{1... | collective-permute-start | bytes 319496 | tf_op jit(solution)/shard_map/ppermute | solution.py:379
  29.5 5.9 %collective-permute-start.5 = (f32[208,128]{1,0:T(8,128)S(1)}, f32[208,128]{1,0:T(8,128)S(1)}, u32[]{:S(2)}, u32[]{:S(2)}) collective-permute-start(f32[208,128]{1,0:T(8,128)S(1)} %get-tuple-element.34), channel_id=1, source_target_pairs={{0,16},{16,32},{32,48},{48,0},{64,80},{80,96},{96,112},{112,64},{1... | collective-permute-start | bytes 319496 | tf_op jit(solution)/shard_map/ppermute | solution.py:379
  30.2 5.2 %collective-permute-start.6 = (f32[208,128]{1,0:T(8,128)S(1)}, f32[208,128]{1,0:T(8,128)S(1)}, u32[]{:S(2)}, u32[]{:S(2)}) collective-permute-start(f32[208,128]{1,0:T(8,128)S(1)} %get-tuple-element.35), channel_id=1, source_target_pairs={{0,48},{16,0},{32,16},{48,32},{64,112},{80,64},{96,80},{112,96},{1... | collective-permute-start | bytes 319496 | tf_op jit(solution)/shard_map/ppermute | solution.py:379
  35.5 10.5 %collective-permute-start.9 = (f32[208,128]{1,0:T(8,128)S(1)}, f32[208,128]{1,0:T(8,128)S(1)}, u32[]{:S(2)}, u32[]{:S(2)}) collective-permute-start(f32[208,128]{1,0:T(8,128)S(1)} %add_add_fusion.1), channel_id=1, source_target_pairs={{0,128},{16,144},{32,160},{48,176},{64,192},{80,208},{96,224},{112... | collective-permute-start | bytes 319496 | tf_op jit(solution)/shard_map/ppermute | solution.py:384
  41.8 6.8 %collective-permute-start.8 = (f32[208,128]{1,0:T(8,128)S(1)}, f32[208,128]{1,0:T(8,128)S(1)}, u32[]{:S(2)}, u32[]{:S(2)}) collective-permute-start(f32[208,128]{1,0:T(8,128)S(1)} %add_add_fusion.1), channel_id=1, source_target_pairs={{0,64},{16,80},{32,96},{48,112},{64,128},{80,144},{96,160},{112,17... | collective-permute-start | bytes 319496 | tf_op jit(solution)/shard_map/ppermute | solution.py:384
  43.3 5.6 %collective-permute-start.7 = (f32[208,128]{1,0:T(8,128)S(1)}, f32[208,128]{1,0:T(8,128)S(1)}, u32[]{:S(2)}, u32[]{:S(2)}) collective-permute-start(f32[208,128]{1,0:T(8,128)S(1)} %add_add_fusion.1), channel_id=1, source_target_pairs={{0,192},{16,208},{32,224},{48,240},{64,0},{80,16},{96,32},{112,48}... | collective-permute-start | bytes 319496 | tf_op jit(solution)/shard_map/ppermute | solution.py:384
  49.0 5.7 %collective-permute-start.12 = (f32[104,128]{1,0:T(8,128)S(1)}, f32[104,128]{1,0:T(8,128)S(1)}, u32[]{:S(2)}, u32[]{:S(2)}) collective-permute-start(f32[104,128]{1,0:T(8,128)S(1)} %fusion.6.refs_0_), channel_id=1, source_target_pairs={{0,32},{16,48},{32,0},{48,16},{64,96},{80,112},{96,64},{112,80},{1... | collective-permute-start | bytes 159752 | tf_op jit(solution)/shard_map/ppermute | solution.py:379
  50.5 5.3 %collective-permute-start.11 = (f32[104,128]{1,0:T(8,128)S(1)}, f32[104,128]{1,0:T(8,128)S(1)}, u32[]{:S(2)}, u32[]{:S(2)}) collective-permute-start(f32[104,128]{1,0:T(8,128)S(1)} %fusion.6.refs_0_), channel_id=1, source_target_pairs={{0,48},{16,0},{32,16},{48,32},{64,112},{80,64},{96,80},{112,96},{1... | collective-permute-start | bytes 159752 | tf_op jit(solution)/shard_map/ppermute | solution.py:379
  52.4 5.3 %collective-permute-start.10 = (f32[104,128]{1,0:T(8,128)S(1)}, f32[104,128]{1,0:T(8,128)S(1)}, u32[]{:S(2)}, u32[]{:S(2)}) collective-permute-start(f32[104,128]{1,0:T(8,128)S(1)} %fusion.6.refs_0_), channel_id=1, source_target_pairs={{0,16},{16,32},{32,48},{48,0},{64,80},{80,96},{96,112},{112,64},{1... | collective-permute-start | bytes 159752 | tf_op jit(solution)/shard_map/ppermute | solution.py:379
  62.8 5.7 %collective-permute-start.13 = (f32[104,128]{1,0:T(8,128)S(1)}, f32[104,128]{1,0:T(8,128)S(1)}, u32[]{:S(2)}, u32[]{:S(2)}) collective-permute-start(f32[104,128]{1,0:T(8,128)S(1)} %get-tuple-element.41), channel_id=1, source_target_pairs={{0,32},{16,48},{32,0},{48,16},{64,96},{80,112},{96,64},{112,80},{1... | collective-permute-start | bytes 159752 | tf_op jit(solution)/shard_map/ppermute | solution.py:379
  64.5 5.3 %collective-permute-start.14 = (f32[104,128]{1,0:T(8,128)S(1)}, f32[104,128]{1,0:T(8,128)S(1)}, u32[]{:S(2)}, u32[]{:S(2)}) collective-permute-start(f32[104,128]{1,0:T(8,128)S(1)} %get-tuple-element.42), channel_id=1, source_target_pairs={{0,16},{16,32},{32,48},{48,0},{64,80},{80,96},{96,112},{112,64},{1... | collective-permute-start | bytes 159752 | tf_op jit(solution)/shard_map/ppermute | solution.py:379
  64.5 5.3 %collective-permute-start.15 = (f32[104,128]{1,0:T(8,128)S(1)}, f32[104,128]{1,0:T(8,128)S(1)}, u32[]{:S(2)}, u32[]{:S(2)}) collective-permute-start(f32[104,128]{1,0:T(8,128)S(1)} %get-tuple-element.43), channel_id=1, source_target_pairs={{0,48},{16,0},{32,16},{48,32},{64,112},{80,64},{96,80},{112,96},{1... | collective-permute-start | bytes 159752 | tf_op jit(solution)/shard_map/ppermute | solution.py:379
  69.8 9.3 %collective-permute-start.18 = (f32[104,128]{1,0:T(8,128)S(1)}, f32[104,128]{1,0:T(8,128)S(1)}, u32[]{:S(2)}, u32[]{:S(2)}) collective-permute-start(f32[104,128]{1,0:T(8,128)S(1)} %add_add_fusion.2), channel_id=1, source_target_pairs={{0,128},{16,144},{32,160},{48,176},{64,192},{80,208},{96,224},{112... | collective-permute-start | bytes 159752 | tf_op jit(solution)/shard_map/ppermute | solution.py:384
  73.7 6.2 %collective-permute-start.17 = (f32[104,128]{1,0:T(8,128)S(1)}, f32[104,128]{1,0:T(8,128)S(1)}, u32[]{:S(2)}, u32[]{:S(2)}) collective-permute-start(f32[104,128]{1,0:T(8,128)S(1)} %add_add_fusion.2), channel_id=1, source_target_pairs={{0,64},{16,80},{32,96},{48,112},{64,128},{80,144},{96,160},{112,17... | collective-permute-start | bytes 159752 | tf_op jit(solution)/shard_map/ppermute | solution.py:384
  76.4 5.0 %collective-permute-start.16 = (f32[104,128]{1,0:T(8,128)S(1)}, f32[104,128]{1,0:T(8,128)S(1)}, u32[]{:S(2)}, u32[]{:S(2)}) collective-permute-start(f32[104,128]{1,0:T(8,128)S(1)} %add_add_fusion.2), channel_id=1, source_target_pairs={{0,192},{16,208},{32,224},{48,240},{64,0},{80,16},{96,32},{112,48}... | collective-permute-start | bytes 159752 | tf_op jit(solution)/shard_map/ppermute | solution.py:384
  81.5 5.7 %collective-permute-start.21 = (f32[104,128]{1,0:T(8,128)S(1)}, f32[104,128]{1,0:T(8,128)S(1)}, u32[]{:S(2)}, u32[]{:S(2)}) collective-permute-start(f32[104,128]{1,0:T(8,128)S(1)} %fusion.15.refs_0_), channel_id=1, source_target_pairs={{0,32},{16,48},{32,0},{48,16},{64,96},{80,112},{96,64},{112,80},{1... | collective-permute-start | bytes 159752 | tf_op jit(solution)/shard_map/ppermute | solution.py:379
  82.8 6.2 %collective-permute-start.20 = (f32[104,128]{1,0:T(8,128)S(1)}, f32[104,128]{1,0:T(8,128)S(1)}, u32[]{:S(2)}, u32[]{:S(2)}) collective-permute-start(f32[104,128]{1,0:T(8,128)S(1)} %fusion.15.refs_0_), channel_id=1, source_target_pairs={{0,48},{16,0},{32,16},{48,32},{64,112},{80,64},{96,80},{112,96},{1... | collective-permute-start | bytes 159752 | tf_op jit(solution)/shard_map/ppermute | solution.py:379
  85.5 5.3 %collective-permute-start.19 = (f32[104,128]{1,0:T(8,128)S(1)}, f32[104,128]{1,0:T(8,128)S(1)}, u32[]{:S(2)}, u32[]{:S(2)}) collective-permute-start(f32[104,128]{1,0:T(8,128)S(1)} %fusion.15.refs_0_), channel_id=1, source_target_pairs={{0,16},{16,32},{32,48},{48,0},{64,80},{80,96},{96,112},{112,64},{1... | collective-permute-start | bytes 159752 | tf_op jit(solution)/shard_map/ppermute | solution.py:379
  96.4 5.4 %collective-permute-start.22 = (f32[64,128]{1,0:T(8,128)S(1)}, f32[64,128]{1,0:T(8,128)S(1)}, u32[]{:S(2)}, u32[]{:S(2)}) collective-permute-start(f32[64,128]{1,0:T(8,128)S(1)} %get-tuple-element.46), channel_id=1, source_target_pairs={{0,32},{16,48},{32,0},{48,16},{64,96},{80,112},{96,64},{112,80},{1... | collective-permute-start | bytes 98312 | tf_op jit(solution)/shard_map/ppermute | solution.py:379
  98.1 5.1 %collective-permute-start.23 = (f32[64,128]{1,0:T(8,128)S(1)}, f32[64,128]{1,0:T(8,128)S(1)}, u32[]{:S(2)}, u32[]{:S(2)}) collective-permute-start(f32[64,128]{1,0:T(8,128)S(1)} %get-tuple-element.47), channel_id=1, source_target_pairs={{0,16},{16,32},{32,48},{48,0},{64,80},{80,96},{96,112},{112,64},{1... | collective-permute-start | bytes 98312 | tf_op jit(solution)/shard_map/ppermute | solution.py:379
  98.1 5.1 %collective-permute-start.24 = (f32[64,128]{1,0:T(8,128)S(1)}, f32[64,128]{1,0:T(8,128)S(1)}, u32[]{:S(2)}, u32[]{:S(2)}) collective-permute-start(f32[64,128]{1,0:T(8,128)S(1)} %get-tuple-element.48), channel_id=1, source_target_pairs={{0,48},{16,0},{32,16},{48,32},{64,112},{80,64},{96,80},{112,96},{1... | collective-permute-start | bytes 98312 | tf_op jit(solution)/shard_map/ppermute | solution.py:379
  103.2 7.9 %collective-permute-start.27 = (f32[64,128]{1,0:T(8,128)S(1)}, f32[64,128]{1,0:T(8,128)S(1)}, u32[]{:S(2)}, u32[]{:S(2)}) collective-permute-start(f32[64,128]{1,0:T(8,128)S(1)} %add_add_fusion.3), channel_id=1, source_target_pairs={{0,128},{16,144},{32,160},{48,176},{64,192},{80,208},{96,224},{112... | collective-permute-start | bytes 98312 | tf_op jit(solution)/shard_map/ppermute | solution.py:384
  104.0 7.1 %collective-permute-start.26 = (f32[64,128]{1,0:T(8,128)S(1)}, f32[64,128]{1,0:T(8,128)S(1)}, u32[]{:S(2)}, u32[]{:S(2)}) collective-permute-start(f32[64,128]{1,0:T(8,128)S(1)} %add_add_fusion.3), channel_id=1, source_target_pairs={{0,64},{16,80},{32,96},{48,112},{64,128},{80,144},{96,160},{112,17... | collective-permute-start | bytes 98312 | tf_op jit(solution)/shard_map/ppermute | solution.py:384
  107.7 4.8 %collective-permute-start.25 = (f32[64,128]{1,0:T(8,128)S(1)}, f32[64,128]{1,0:T(8,128)S(1)}, u32[]{:S(2)}, u32[]{:S(2)}) collective-permute-start(f32[64,128]{1,0:T(8,128)S(1)} %add_add_fusion.3), channel_id=1, source_target_pairs={{0,192},{16,208},{32,224},{48,240},{64,0},{80,16},{96,32},{112,48}... | collective-permute-start | bytes 98312 | tf_op jit(solution)/shard_map/ppermute | solution.py:384
  112.6 5.5 %collective-permute-start.30 = (f32[64,128]{1,0:T(8,128)S(1)}, f32[64,128]{1,0:T(8,128)S(1)}, u32[]{:S(2)}, u32[]{:S(2)}) collective-permute-start(f32[64,128]{1,0:T(8,128)S(1)} %fusion.26.refs_0_), channel_id=1, source_target_pairs={{0,32},{16,48},{32,0},{48,16},{64,96},{80,112},{96,64},{112,80},{1... | collective-permute-start | bytes 98312 | tf_op jit(solution)/shard_map/ppermute | solution.py:379
  114.1 4.9 %collective-permute-start.29 = (f32[64,128]{1,0:T(8,128)S(1)}, f32[64,128]{1,0:T(8,128)S(1)}, u32[]{:S(2)}, u32[]{:S(2)}) collective-permute-start(f32[64,128]{1,0:T(8,128)S(1)} %fusion.26.refs_0_), channel_id=1, source_target_pairs={{0,48},{16,0},{32,16},{48,32},{64,112},{80,64},{96,80},{112,96},{1... | collective-permute-start | bytes 98312 | tf_op jit(solution)/shard_map/ppermute | solution.py:379
  116.0 5.1 %collective-permute-start.28 = (f32[64,128]{1,0:T(8,128)S(1)}, f32[64,128]{1,0:T(8,128)S(1)}, u32[]{:S(2)}, u32[]{:S(2)}) collective-permute-start(f32[64,128]{1,0:T(8,128)S(1)} %fusion.26.refs_0_), channel_id=1, source_target_pairs={{0,16},{16,32},{32,48},{48,0},{64,80},{80,96},{96,112},{112,64},{1... | collective-permute-start | bytes 98312 | tf_op jit(solution)/shard_map/ppermute | solution.py:379

commit v5 on v4

v5 whole, which is shorter than its diff:
```python
import functools

import jax
import jax.numpy as jnp
from jax import lax
from jax.experimental import pallas as pl
from jax.experimental.pallas import tpu as pltpu
from jax.sharding import PartitionSpec as P

SWEEPS = 8
OUTER = 3
LOW_BOUND = 0.05
HIGH_BOUND = 2.0

TILE = 128
HALO = SWEEPS * OUTER
ROWS = TILE + 2 * HALO
PAD = 8
STEP = 16
PLANES = 16
PACKS = 3
ACROSS = 4
RING = 4
MAIN = 64
FULL = 80
CHUNK = 104
SIDE = 16
VMEM_LIMIT = 16 * 1024 * 1024
F32 = jnp.float32


def sweep_weights():
    theta_mid = (HIGH_BOUND + LOW_BOUND) / 2.0
    delta_half = (HIGH_BOUND - LOW_BOUND) / 2.0
    sigma_ratio = theta_mid / delta_half
    rho_now = 1.0 / sigma_ratio
    weights = [(0.0, 1.0 / theta_mid)]
    for _ in range(SWEEPS - 1):
        rho_next = 1.0 / (2.0 * sigma_ratio - rho_now)
        weights.append((rho_next * rho_now, 2.0 * rho_next / delta_half))
        rho_now = rho_next
    return weights


def field_sources(refs, me):
    sources = [(refs[f].at[gas, 0], 4 * f + 2 * gas, 2) for f in range(3) for gas in range(2)]
    sources.append((refs[3].at[0], 12, 2))
    layer = me[0] >> 1
    return sources + [(refs[4 + f].at[0, pl.ds(layer, 1)], 14 + f, 1) for f in range(2)]


def copy_rows(refs, me, parts, sems):
    copies = []
    for source, first, layers in field_sources(refs, me):
        for row, count, out in parts:
            copies.append(
                pltpu.make_async_copy(
                    source.at[:, pl.ds(row, count), :], out.at[pl.ds(first, layers)], sems.at[len(copies)]
                )
            )
    for copy in copies:
        copy.start()
    for copy in copies:
        copy.wait()


def edge_kernel(*refs):
    me, up, down, sems = refs[6:]
    copy_rows(refs[:6], me, ((TILE - HALO, HALO, up), (0, HALO, down)), sems)


def load_kernel(*refs):
    me, planes, sems = refs[6:]
    copy_rows(refs[:6], me, ((0, TILE, planes),), sems)


def slot(p):
    pack, lane = divmod(HALO * p, TILE)
    return pack, lane, [pack] if lane + HALO <= TILE else [pack, pack + 1]


def pack_y_kernel(planes, top, bottom, tile_row_ref, column_ref, first, second):
    tile_row, column = tile_row_ref[0], column_ref[0]
    odd = (column & 1) == 1
    for row in range(0, ROWS, 8):
        lane = lax.broadcasted_iota(jnp.int32, (8, TILE), 1)
        to_right = [jnp.zeros((8, TILE), F32) for _ in range(PACKS)]
        to_left = [jnp.zeros((8, TILE), F32) for _ in range(PACKS)]
        for p in range(PLANES):
            if row < HALO:
                value = jnp.where(tile_row > 0, top[p, pl.ds(row, 8), :], 0.0)
            elif row < HALO + TILE:
                value = planes[p, pl.ds(row - HALO, 8), :]
            else:
                value = jnp.where(tile_row < ACROSS - 1, bottom[p, pl.ds(row - HALO - TILE, 8), :], 0.0)
            _, start, packs = slot(p)
            left = pltpu.roll(value, start, 1) if start else value
            right = pltpu.roll(value, (start + HALO) % TILE, 1)
            for pack in packs:
                at = lane + TILE * pack
                here = (at >= HALO * p) & (at < HALO * (p + 1))
                to_left[pack] = jnp.where(here, left, to_left[pack])
                to_right[pack] = jnp.where(here, right, to_right[pack])
        for pack in range(PACKS):
            first[pack, pl.ds(row, 8), :] = jnp.where(odd, to_left[pack], to_right[pack])
            second[pack, pl.ds(row, 8), :] = jnp.where(odd, to_right[pack], to_left[pack])


def chunk_rows(half):
    return [HALO + MAIN * half + 8 * k for k in range(8)] + ([8, 16], [ROWS - 24, ROWS - 16])[half]


def chunk_out(out, field, first=0):
    lane = lax.broadcasted_iota(jnp.int32, (8, TILE), 1)
    for c in range(RING):
        z, rows = c // 2, chunk_rows(c % 2)
        for k, row in enumerate(rows):
            out[c, pl.ds(first + 8 * k, 8), :] = field[z, 0, pl.ds(row, 8), :]
        for slot in range(3):
            packed = jnp.zeros((8, TILE), F32)
            for j, k in enumerate(range(slot, 10, 3)):
                value = pltpu.roll(field[z, 1, pl.ds(rows[k], 8), :], (SIDE + 32 * j) % TILE, 1)
                packed = jnp.where((lane >= 32 * j) & (lane < 32 * (j + 1)), value, packed)
            out[c, pl.ds(first + FULL + 8 * slot, 8), :] = packed


def three(own, halo, lane):
    own64, halo64 = pltpu.roll(own, 64, 1), pltpu.roll(halo, 64, 1)
    middle = jnp.where(lane < 32, halo, jnp.where(lane < 64, halo64, own64))
    last = jnp.where(lane < 64, own64, jnp.where(lane < 96, halo64, halo))
    return own, middle, last


def packed_gases(own0, halo0, own1, halo1, lane):
    own64, halo64 = pltpu.roll(own1, 64, 1), pltpu.roll(halo1, 64, 1)
    middle = jnp.where(lane < 32, halo0, jnp.where(lane < 64, halo64, own64))
    last = jnp.where(lane < 64, own64, jnp.where(lane < 96, halo64, halo0))
    return own0, middle, last


def sum_of_gases(tiles, lane):
    low = jnp.where(lane < 64, tiles[1], tiles[2])
    high = jnp.where(lane < 64, tiles[2], tiles[1])
    return tiles[0] + pltpu.roll(high, 64, 1), low + pltpu.roll(low, 64, 1)


def chunk_in(t4, chunks, change):
    lane = lax.broadcasted_iota(jnp.int32, (8, TILE), 1)
    for c in range(RING):
        z, rows = c // 2, chunk_rows(c % 2)
        sides = [change(chunks[c, pl.ds(FULL + 8 * k, 8), :]) for k in range(3)]
        for k, row in enumerate(rows):
            own = change(chunks[c, pl.ds(8 * k, 8), :])
            halo = pltpu.roll(sides[k % 3], (TILE - SIDE - 32 * (k // 3)) % TILE, 1)
            for t, value in enumerate(three(own, halo, lane)):
                t4[z, t, pl.ds(row, 8), :] = value


def own_chunk(me, out, layer):
    lane = lax.broadcasted_iota(jnp.int32, (8, TILE), 1)
    half = me[0] & 1
    low, high = chunk_rows(0), chunk_rows(1)
    rows = [pl.multiple_of(a + (b - a) * half, 8) for a, b in zip(low, high)]
    for k, row in enumerate(rows):
        out[pl.ds(8 * k, 8), :] = layer[0, pl.ds(row, 8), :]
    for slot_of in range(3):
        packed = jnp.zeros((8, TILE), F32)
        for j, k in enumerate(range(slot_of, 10, 3)):
            value = pltpu.roll(layer[1, pl.ds(rows[k], 8), :], (SIDE + 32 * j) % TILE, 1)
            packed = jnp.where((lane >= 32 * j) & (lane < 32 * (j + 1)), value, packed)
        out[pl.ds(FULL + 8 * slot_of, 8), :] = packed


def turn(me, k):
    return (me[0] + k) & 3


def send_chunks(me, chunks, outs):
    for k, out in enumerate(outs):
        out[...] = chunks[turn(me, k)]


def gather_chunks(me, chunks, parts):
    for k, part in zip(BACK, parts):
        chunks[turn(me, RING - k)] = part[...]


def fourth(value):
    square = value * value
    return square * square


def to_left_of(tiles, t, lane):
    return pltpu.roll(jnp.where(lane == TILE - 1, tiles[t - 1], tiles[t]), 1, 1)


def to_right_of(tiles, t, lane):
    return pltpu.roll(jnp.where(lane == 0, tiles[(t + 1) % 3], tiles[t]), TILE - 1, 1)


def each_step(first, last, body):
    for r in range(first, last, STEP):
        body(r)


def solve(step, a, q, t4, sp, start, now, old):
    first, last = 8 * step, ROWS - 8 * step

    def source(r):
        for z in range(2):
            for t in range(3):
                weight = q[z, t, pl.ds(r, STEP), :]
                value = weight * t4[z, t, pl.ds(r, STEP), :]
                sp[z, t, pl.ds(r, STEP), :] = jnp.where(weight > 0.0, value, 0.0)

    each_step(first, last, source)
    before, src = None, start
    for sweep, (keep, push) in enumerate(sweep_weights()):
        dst = old if sweep % 2 == 0 else now

        def body(r, src=src, dst=dst, before=before, keep=keep, push=push):
            lane = lax.broadcasted_iota(jnp.int32, (STEP, TILE), 1)
            rows = pl.ds(r, STEP)
            own = [[src[z, t, pl.ds(r + PAD, STEP), :] for t in range(3)] for z in range(2)]
            for z in range(2):
                for t in range(3):
                    here = own[z][t]
                    total = sp[z, t, rows, :] + a[0, z, t, rows, :] * own[1 - z][t]
                    total += a[1, z, t, rows, :] * src[z, t, pl.ds(r + PAD - 1, STEP), :]
                    total += a[2, z, t, rows, :] * src[z, t, pl.ds(r + PAD + 1, STEP), :]
                    total += a[3, z, t, rows, :] * to_left_of(own[z], t, lane)
                    total += a[4, z, t, rows, :] * to_right_of(own[z], t, lane)
                    value = (1.0 + keep - push) * here + push * total
                    if before is not None:
                        value -= keep * before[z, t, pl.ds(r + PAD, STEP), :]
                    dst[z, t, pl.ds(r + PAD, STEP), :] = value

        each_step(first, last, body)
        before, src = src, dst


def absorb(kap, now, out):
    lane = lax.broadcasted_iota(jnp.int32, (STEP, TILE), 1)

    def body(r):
        for z in range(2):
            rows = pl.ds(r + PAD, STEP)
            tiles = [kap[z, t, rows, :] * now[z, t, rows, :] for t in range(3)]
            for l, value in enumerate(sum_of_gases(tiles, lane)):
                out[z, l, pl.ds(r, STEP), :] = value

    each_step(8, ROWS - 8, body)


def first_kernel(planes, top, bottom, first, second, me, tile_row_ref, column_ref, *refs):
    a, q, kap, now, held, *outs = refs[: 5 + RING]
    tis, sp, t4, old, begin, shared, sums = refs[5 + RING :]
    tile_row, column = tile_row_ref[0], column_ref[0]
    odd = (column & 1) == 1

    def own_rows(p, row):
        if row < HALO:
            return jnp.where(tile_row > 0, top[p, pl.ds(row, 8), :], 0.0)
        if row < HALO + TILE:
            return planes[p, pl.ds(row - HALO, 8), :]
        return jnp.where(tile_row < ACROSS - 1, bottom[p, pl.ds(row - HALO - TILE, 8), :], 0.0)

    for row in range(0, ROWS, 8):
        lane = lax.broadcasted_iota(jnp.int32, (8, TILE), 1)
        got = [(first[pack, pl.ds(row, 8), :], second[pack, pl.ds(row, 8), :]) for pack in range(PACKS)]
        lefts = [jnp.where(column > 0, jnp.where(odd, f, s), 0.0) for f, s in got]
        rights = [jnp.where(column < ACROSS - 1, jnp.where(odd, s, f), 0.0) for f, s in got]
        halos = []
        for p in range(PLANES):
            pack, start, packs = slot(p)
            left, right = lefts[pack], rights[pack]
            if len(packs) > 1:
                left = jnp.where(lane >= start, left, lefts[pack + 1])
                right = jnp.where(lane >= start, right, rights[pack + 1])
            left = pltpu.roll(left, (2 * TILE - HALO - start) % TILE, 1)
            right = pltpu.roll(right, TILE - start, 1) if start else right
            halos.append(jnp.where(lane < HALO, right, jnp.where(lane >= TILE - HALO, left, 0.0)))
        for f, (dst, pad) in enumerate(((kap, PAD), (q, 0), (begin, PAD))):
            for z in range(2):
                p0, p1 = 4 * f + z, 4 * f + 2 + z
                tiles = packed_gases(own_rows(p0, row), halos[p0], own_rows(p1, row), halos[p1], lane)
                for t, value in enumerate(tiles):
                    dst[z, t, pl.ds(row + pad, 8), :] = value
        for p in range(12, PLANES):
            own = own_rows(p, row)
            tis[p - 12, 0, pl.ds(row, 8), :] = own
            tis[p - 12, 1, pl.ds(row, 8), :] = halos[p]
            if p < 14:
                for t, value in enumerate(three(fourth(own), fourth(halos[p]), lane)):
                    t4[p - 12, t, pl.ds(row, 8), :] = value

    own_chunk(me, held.at[0], tis.at[me[0] >> 1])
    own_chunk(me, held.at[1], tis.at[2])
    own_chunk(me, held.at[2], tis.at[3])

    def halves(r):
        lane = lax.broadcasted_iota(jnp.int32, (STEP, TILE), 1)
        rows, padded = pl.ds(r, STEP), pl.ds(r + PAD, STEP)
        for z in range(2):
            own = [kap[z, t, padded, :] for t in range(3)]
            for l, value in enumerate(sum_of_gases([own[t] * q[z, t, rows, :] for t in range(3)], lane)):
                shared[z, l, rows, :] = value
            for t in range(3):
                old[z, t, padded, :] = 1.0 / (own[t] + kap[z, t, pl.ds(r + PAD + 1, STEP), :])
                sp[z, t, rows, :] = 1.0 / (own[t] + to_right_of(own, t, lane))

    each_step(0, ROWS, halves)

    def coefficients(r):
        lane = lax.broadcasted_iota(jnp.int32, (STEP, TILE), 1)
        rows, padded = pl.ds(r, STEP), pl.ds(r + PAD, STEP)
        own = [[kap[z, t, padded, :] for t in range(3)] for z in range(2)]
        between = [1.0 / (own[0][t] + own[1][t]) for t in range(3)]
        for z in range(2):
            to_right = [sp[z, t, rows, :] for t in range(3)]
            for t in range(3):
                here = own[z][t]
                to_left = to_left_of(to_right, t, lane)
                to_up = old[z, t, pl.ds(r + PAD - 1, STEP), :]
                couplings = [between[t], to_up, old[z, t, padded, :], to_left, to_right[t]]
                diagonal = 1.5 * here + 1.0 / here
                for coupling in couplings:
                    diagonal += coupling
                inverse = 1.0 / diagonal
                for f, coupling in enumerate(couplings):
                    a[f, z, t, rows, :] = jnp.where(here > 0.0, coupling * inverse, 0.0)
                weight = 6.0 * here * q[z, t, rows, :] * inverse
                q[z, t, rows, :] = jnp.where(here > 0.0, weight, 0.0)

    each_step(0, ROWS, coefficients)
    chunk_out(sums, shared, CHUNK)
    solve(0, a, q, t4, sp, begin, now, old)
    absorb(kap, now, shared)
    chunk_out(sums, shared)
    send_chunks(me, sums, outs)


def next_kernel(a, q, kap, start, *refs):
    parts, me = refs[:RING], refs[RING]
    now, *outs = refs[RING + 1 : 2 * RING + 2]
    sp, t4, old, shared, sums = refs[2 * RING + 2 :]
    gather_chunks(me, sums, parts)
    chunk_in(t4, sums, fourth)
    solve(1, a, q, t4, sp, start, now, old)
    absorb(kap, now, shared)
    chunk_out(sums, shared)
    send_chunks(me, sums, outs)


def last_kernel(a, q, kap, start, *refs):
    parts, me = refs[:RING], refs[RING]
    now, *outs = refs[RING + 1 : 2 * RING + 2]
    sp, t4, old, sums = refs[2 * RING + 2 :]
    gather_chunks(me, sums, parts)
    chunk_in(t4, sums, fourth)
    solve(2, a, q, t4, sp, start, now, old)
    lane = lax.broadcasted_iota(jnp.int32, (MAIN, TILE), 1)
    for c in range(RING):
        z, half = c // 2, c % 2
        rows = pl.ds(PAD + HALO + MAIN * half, MAIN)
        tiles = [now[z, t, rows, :] for t in range(3)]
        taken = [kap[z, t, rows, :] * tiles[t] for t in range(3)]
        sums[c, pl.ds(0, MAIN), :] = sum_of_gases(taken, lane)[0]
    for k, out in enumerate(outs):
        out[...] = sums[turn(me, k), pl.ds(0, MAIN), :]


def radiation_kernel(now, radiation):
    lane = lax.broadcasted_iota(jnp.int32, (TILE, TILE), 1)
    for z in range(2):
        tiles = [now[z, t, pl.ds(PAD + HALO, TILE), :] for t in range(3)]
        radiation[0, 0, z] = tiles[0]
        radiation[1, 0, z] = pltpu.roll(jnp.where(lane < 64, tiles[2], tiles[1]), 64, 1)


def final_kernel(*refs):
    parts, me, out = refs[:RING], refs[RING], refs[RING + 1]
    gather_chunks(me, out, parts)


def corrected(current, earlier, inertia, source, emitted, taken):
    mismatch = inertia * (current - earlier) + 4.0 * emitted * fourth(current) - taken - source
    slope = inertia + 16.0 * emitted * (current * current * current)
    return jnp.where(inertia > 0.0, current - mismatch / slope, 0.0)


def call(kernel, outs, scratch=(), space=pltpu.VMEM, cost=None):
    def run(*args):
        return pl.pallas_call(
            kernel,
            out_shape=[jax.ShapeDtypeStruct(dims, F32) for dims in outs],
            in_specs=[
                pl.BlockSpec(memory_space=pltpu.SMEM if array.dtype == jnp.int32 else space) for array in args
            ],
            out_specs=[pl.BlockSpec(memory_space=pltpu.VMEM)] * len(outs),
            scratch_shapes=[pltpu.VMEM(s, F32) if isinstance(s, tuple) else s for s in scratch],
            compiler_params=pltpu.CompilerParams(vmem_limit_bytes=VMEM_LIMIT),
            cost_estimate=cost and pl.CostEstimate(flops=0, bytes_accessed=cost, transcendentals=0),
        )(*args)

    return run


FIELD = (2, 3, ROWS, TILE)
PADDED = (2, 3, ROWS + 2 * PAD, TILE)
SHARED = (2, 2, ROWS, TILE)
OUT_TURNS = (2, 3, 1)
BACK = (0, 3, 1, 2)


def along_y(array, by):
    pairs = [(4 * z + y, 4 * z + (y + by) % 4) for z in range(4) for y in range(4)]
    return lax.ppermute(array, "gas", pairs)


def along_z(array, by):
    pairs = [(4 * z + y, 4 * ((z + by) % 4) + y) for z in range(4) for y in range(4)]
    return lax.ppermute(array, "gas", pairs)


def sum_over_gas(parts):
    total = parts[0]
    for k in OUT_TURNS:
        total = total + along_y(parts[k], k)
    parts = [along_z(total, k) for k in (3, 1, 2)]
    return total + parts[0] + parts[1] + parts[2]


def spread(chunk):
    return [along_y(chunk, k) if k else chunk for k in BACK]


def on_device(*inputs):
    kelvin, inertia, source, extinction, fractions, irradiance = inputs
    own = (extinction, fractions, irradiance, kelvin, inertia, source)
    own = [pltpu.with_memory_space_constraint(array, pltpu.HBM) for array in own]
    devices = lax.axis_size("space")
    me = (lax.axis_index("gas") & 3).reshape(1)
    place = lax.axis_index("space")
    at = ((place >> 2).reshape(1), (place & 3).reshape(1))
    sems = pltpu.SemaphoreType.DMA((18,))
    up, down = call(edge_kernel, [(PLANES, HALO, TILE)] * 2, [sems], space=pltpu.HBM)(*own, me)
    (planes,) = call(load_kernel, [(PLANES, TILE, TILE)], [sems], space=pltpu.HBM, cost=4000000)(*own, me)
    ring = [(i, (i + ACROSS) % devices) for i in range(devices)]
    top = lax.ppermute(up, "space", ring)
    bottom = lax.ppermute(down, "space", [(j, i) for i, j in ring])
    first, second = call(pack_y_kernel, [(PACKS, ROWS, TILE)] * 2)(planes, top, bottom, *at)
    first = lax.ppermute(first, "space", [(i, i ^ 1) for i in range(devices)])
    swaps = (0, 2, 1, 3)
    second = lax.ppermute(second, "space", [(i, i - i % ACROSS + swaps[i % ACROSS]) for i in range(devices)])
    two = (2 * CHUNK, TILE)
    a, q, kap, now, held, *parts = call(
        first_kernel,
        [(5,) + FIELD, FIELD, PADDED, PADDED, (3, CHUNK, TILE)] + [two] * RING,
        [(4, 2, ROWS, TILE), FIELD, FIELD, PADDED, PADDED, SHARED, (RING,) + two],
    )(planes, top, bottom, first, second, me, *at)
    total = sum_over_gas(parts)
    taken, emitted = total[:CHUNK], total[CHUNK:]
    earlier, inertia, source = held[0], held[1], held[2]
    current = corrected(earlier, earlier, inertia, source, emitted, taken)
    one = (CHUNK, TILE)
    now, *parts = call(
        next_kernel, [PADDED] + [one] * RING, [FIELD, FIELD, PADDED, SHARED, (RING,) + one]
    )(a, q, kap, now, *spread(current), me)
    current = corrected(current, earlier, inertia, source, emitted, sum_over_gas(parts))
    now, *parts = call(
        last_kernel,
        [PADDED] + [(MAIN, TILE)] * RING,
        [FIELD, FIELD, PADDED, (RING,) + one],
    )(a, q, kap, now, *spread(current), me)
    (radiation,) = call(radiation_kernel, [(2, 1, 2, TILE, TILE)], cost=4000000)(now)
    rest = (value[:MAIN] for value in (current, earlier, inertia, source, emitted))
    current = corrected(*rest, sum_over_gas(parts))
    (final,) = call(final_kernel, [(RING, MAIN, TILE)])(*spread(current), me)
    return final.reshape(1, 2, TILE, TILE), radiation


def solution(mesh):
    placed = (
        P("space", None, None, None),
        P("space", None, None, None),
        P("space", None, None, None),
        P("gas", "space", None, None, None),
        P("gas", "space", None, None, None),
        P("gas", "space", None, None, None),
    )
    return jax.shard_map(
        on_device,
        mesh=mesh,
        in_specs=placed,
        out_specs=(P("space", None, None, None), P("gas", "space", None, None, None)),
        check_vma=False,
    )
```

time: 122 us -> 118 us (0.967)
  starting transfers between devices: 58.3 us -> 53.1 us
    ppermute x18, starting transfers between devices: 29.5 us -> 24.9 us  [along_y(): return lax.ppermute(array, 'gas', pairs)]
    ppermute x18, waiting for transfers between devices: 20.2 us -> 22.4 us  [along_y(): return lax.ppermute(array, 'gas', pairs)]
    ppermute x1, waiting for transfers between devices: 4.61 us -> 3.2 us  [on_device(): top = lax.ppermute(up, 'space', ring)]
    pallas_call x6 -> x8, Pallas kernels: 20.8 us -> 20.7 us  [run(): pl.pallas_call(kernel, out_shape=[jax.ShapeDtypeStruct(dims, F32) for dim...]
  transfers between devices with their start and end apart: 31 -> 31, of which waited for: 24 -> 24; matrix products, arithmetic and copies ran while one was open for 0% -> 0% of each run, Pallas kernels for 0% -> 2%
where the time goes in v5:
time: 118 us
  starting transfers between devices  53.1 us (45%)
  waiting for transfers between devices  42.9 us (36%)
  Pallas kernels  20.7 us (18%)
    ppermute x18, starting transfers between devices, along_y(): return lax.ppermute(array, 'gas', pairs)  24.9 us
    ppermute x9, starting transfers between devices, along_z(): return lax.ppermute(array, 'gas', pairs)  22.9 us
    ppermute x18, waiting for transfers between devices, along_y(): return lax.ppermute(array, 'gas', pairs)  22.4 us
    pallas_call x8, Pallas kernels, run(): pl.pallas_call(kernel, out_shape=[jax.ShapeDtypeStruct(dims, F32) for dim...  20.7 us
    ppermute x9, waiting for transfers between devices, along_z(): return lax.ppermute(array, 'gas', pairs)  11.3 us
    ppermute x1, waiting for transfers between devices, on_device(): lax.ppermute(second, 'space', [(i, i - i % ACROSS + swaps[i % ACROSS]) fo...  4.61 us
    ppermute x1, waiting for transfers between devices, on_device(): top = lax.ppermute(up, 'space', ring)  3.2 us
    ppermute x1, starting transfers between devices, on_device(): lax.ppermute(second, 'space', [(i, i - i % ACROSS + swaps[i % ACROSS]) fo...  3.15 us
  transfers between devices with their start and end apart: 31, of which 24 were waited for; matrix products, arithmetic and copies ran while one was open for 0% of the time, Pallas kernels for 2%

profile of v5, /device:TPU:38, one launch (start us, length us, event | category | flops | bytes accessed | tf_op | source)
XLA Modules:
  0.0 117.7 jit_solution(12816831861912171529)
XLA Ops:
  0.6 1.1 shard_map.78
  2.3 1.5 %collective-permute-start.1 = (f32[16,24,128]{2,1,0:T(8,128)S(1)}, f32[16,24,128]{2,1,0:T(8,128)S(1)}, u32[]{:S(2)}, u32[]{:S(2)}) collective-permute-start(f32[16,24,128]{2,1,0:T(8,128)S(1)} %get-tuple-element.26), channel_id=1, source_target_pairs={{4,0},{5,1},{6,2},{7,3},{8,4},{9,5},{10,6},{11,7},{12,8},{13,9},{1... | collective-permute-start | bytes 589832 | tf_op jit(solution)/shard_map/ppermute | solution.py:451
  3.8 1.4 %shard_map.77.planes = f32[16,128,128]{2,1,0:T(8,128)S(1)} custom-call(f32[2,1,2,128,128]{4,3,2,1,0:T(8,128)} %refs_0_.3, f32[2,1,2,128,128]{4,3,2,1,0:T(8,128)} %refs_1_.3, f32[2,1,2,128,128]{4,3,2,1,0:T(8,128)} %refs_2_.3, f32[1,2,128,128]{3,2,1,0:T(8,128)} %refs_3_.3, f32[1,2,128,128]{3,2,1,0:T(8,128)} %refs_4_.3, f32[1,2,128,128]{3,2,1,0:T(8,128)} %refs_5_.3, ...), custom_call_target="tpu_custom_call" | custom-call | bytes 4000000 | tf_op jit(solution)/shard_map/pallas_call | solution.py:394
  5.3 3.2 %collective-permute-done.top = f32[16,24,128]{2,1,0:T(8,128)S(1)} collective-permute-done((f32[16,24,128]{2,1,0:T(8,128)S(1)}, f32[16,24,128]{2,1,0:T(8,128)S(1)}, u32[]{:S(2)}, u32[]{:S(2)}) %collective-permute-start) | collective-permute-done | bytes 196640 | tf_op jit(solution)/shard_map/ppermute | solution.py:450
  8.5 1.4 %collective-permute-done.1.bottom = f32[16,24,128]{2,1,0:T(8,128)S(1)} collective-permute-done((f32[16,24,128]{2,1,0:T(8,128)S(1)}, f32[16,24,128]{2,1,0:T(8,128)S(1)}, u32[]{:S(2)}, u32[]{:S(2)}) %collective-permute-start.1) | collective-permute-done | bytes 196640 | tf_op jit(solution)/shard_map/ppermute | solution.py:451
  9.9 0.8 shard_map.79
  10.7 3.2 %collective-permute-start.3 = (f32[3,176,128]{2,1,0:T(8,128)S(1)}, f32[3,176,128]{2,1,0:T(8,128)S(1)}, u32[]{:S(2)}, u32[]{:S(2)}) collective-permute-start(f32[3,176,128]{2,1,0:T(8,128)S(1)} %get-tuple-element.28), channel_id=1, source_target_pairs={{0,0},{1,2},{2,1},{3,3},{4,4},{5,6},{6,5},{7,7},{8,8},{9,10},{10,9... | collective-permute-start | bytes 811016 | tf_op jit(solution)/shard_map/ppermute | solution.py:455
  13.9 4.6 %collective-permute-done.3.second = f32[3,176,128]{2,1,0:T(8,128)S(1)} collective-permute-done((f32[3,176,128]{2,1,0:T(8,128)S(1)}, f32[3,176,128]{2,1,0:T(8,128)S(1)}, u32[]{:S(2)}, u32[]{:S(2)}) %collective-permute-start.3) | collective-permute-done | bytes 270368 | tf_op jit(solution)/shard_map/ppermute | solution.py:455
  18.5 7.2 %shard_map.80 = (f32[5,2,3,176,128]{4,3,2,1,0:T(8,128)S(1)}, f32[2,3,176,128]{3,2,1,0:T(8,128)S(1)}, f32[2,3,192,128]{3,2,1,0:T(8,128)S(1)}, f32[2,3,192,128]{3,...) custom-call(f32[16,128,128]{2,1,0:T(8,128)S(1)} %shard_map.77.planes, ...), custom_call_target="tpu_custom_call" | custom-call | tf_op jit(solution)/shard_map/pallas_call | solution.py:394
  25.7 3.3 %collective-permute-start.4 = (f32[208,128]{1,0:T(8,128)S(1)}, f32[208,128]{1,0:T(8,128)S(1)}, u32[]{:S(2)}, u32[]{:S(2)}) collective-permute-start(f32[208,128]{1,0:T(8,128)S(1)} %get-tuple-element.31), channel_id=1, source_target_pairs={{0,32},{16,48},{32,0},{48,16},{64,96},{80,112},{96,64},{112,80},{1... | collective-permute-start | bytes 319496 | tf_op jit(solution)/shard_map/ppermute | solution.py:418
  29.0 1.1 collective-permute-start.5
  30.0 1.0 collective-permute-start.6
  31.0 1.0 collective-permute-done.4
  32.0 1.7 %collective-permute-done.5 = f32[208,128]{1,0:T(8,128)S(1)} collective-permute-done((f32[208,128]{1,0:T(8,128)S(1)}, f32[208,128]{1,0:T(8,128)S(1)}, u32[]{:S(2)}, u32[]{:S(2)}) %collective-permute-start.5) | collective-permute-done | bytes 106528 | tf_op jit(solution)/shard_map/ppermute | solution.py:418
  33.7 2.3 %collective-permute-done.6 = f32[208,128]{1,0:T(8,128)S(1)} collective-permute-done((f32[208,128]{1,0:T(8,128)S(1)}, f32[208,128]{1,0:T(8,128)S(1)}, u32[]{:S(2)}, u32[]{:S(2)}) %collective-permute-start.6) | collective-permute-done | bytes 106528 | tf_op jit(solution)/shard_map/ppermute | solution.py:418
  36.0 6.4 %collective-permute-start.9 = (f32[208,128]{1,0:T(8,128)S(1)}, f32[208,128]{1,0:T(8,128)S(1)}, u32[]{:S(2)}, u32[]{:S(2)}) collective-permute-start(f32[208,128]{1,0:T(8,128)S(1)} %add_add_fusion.1), channel_id=1, source_target_pairs={{0,128},{16,144},{32,160},{48,176},{64,192},{80,208},{96,224},{112... | collective-permute-start | bytes 319496 | tf_op jit(solution)/shard_map/ppermute | solution.py:423
  42.3 1.5 %collective-permute-start.8 = (f32[208,128]{1,0:T(8,128)S(1)}, f32[208,128]{1,0:T(8,128)S(1)}, u32[]{:S(2)}, u32[]{:S(2)}) collective-permute-start(f32[208,128]{1,0:T(8,128)S(1)} %add_add_fusion.1), channel_id=1, source_target_pairs={{0,64},{16,80},{32,96},{48,112},{64,128},{80,144},{96,160},{112,17... | collective-permute-start | bytes 319496 | tf_op jit(solution)/shard_map/ppermute | solution.py:423
  43.8 2.7 %collective-permute-start.7 = (f32[208,128]{1,0:T(8,128)S(1)}, f32[208,128]{1,0:T(8,128)S(1)}, u32[]{:S(2)}, u32[]{:S(2)}) collective-permute-start(f32[208,128]{1,0:T(8,128)S(1)} %add_add_fusion.1), channel_id=1, source_target_pairs={{0,192},{16,208},{32,224},{48,240},{64,0},{80,16},{96,32},{112,48}... | collective-permute-start | bytes 319496 | tf_op jit(solution)/shard_map/ppermute | solution.py:423
  46.5 2.7 %collective-permute-done.8 = f32[208,128]{1,0:T(8,128)S(1)} collective-permute-done((f32[208,128]{1,0:T(8,128)S(1)}, f32[208,128]{1,0:T(8,128)S(1)}, u32[]{:S(2)}, u32[]{:S(2)}) %collective-permute-start.8) | collective-permute-done | bytes 106528 | tf_op jit(solution)/shard_map/ppermute | solution.py:423
  50.7 2.6 %collective-permute-start.10 = (f32[104,128]{1,0:T(8,128)S(1)}, f32[104,128]{1,0:T(8,128)S(1)}, u32[]{:S(2)}, u32[]{:S(2)}) collective-permute-start(f32[104,128]{1,0:T(8,128)S(1)} %fusion.6.refs_0_), channel_id=1, source_target_pairs={{0,48},{16,0},{32,16},{48,32},{64,112},{80,64},{96,80},{112,96},{1... | collective-permute-start | bytes 159752 | tf_op jit(solution)/shard_map/ppermute | solution.py:418
  53.3 2.0 %collective-permute-done.12.refs_3_ = f32[104,128]{1,0:T(8,128)S(1)} collective-permute-done((f32[104,128]{1,0:T(8,128)S(1)}, f32[104,128]{1,0:T(8,128)S(1)}, u32[]{:S(2)}, u32[]{:S(2)}) %collective-permute-start.12) | collective-permute-done | bytes 53280 | tf_op jit(solution)/shard_map/ppermute | solution.py:418
  55.3 0.9 collective-permute-done.11.refs_2_
  56.2 4.7 %shard_map.81 = (f32[2,3,192,128]{3,2,1,0:T(8,128)S(1)}, f32[104,128]{1,0:T(8,128)S(1)}, f32[104,128]{1,0:T(8,128)S(1)}, f32[104,128]{1,0:T(8,128)S(1)}, f32[104,128]{1,0:T(8,128)S(1)}) custom-call(f32[5,2,3,176,128]{4,3,2,1,0:T(8,128)S(1)} %get-tuple-element.34.a, f32[2,3,176,128]{3,2,1,0:T(8,128)S(1)} %get-tuple-element.35.q, ...), custom_call_target="tpu_custom_call" | custom-call | tf_op jit(solution)/shard_map/pallas_call | solution.py:394
  60.9 1.8 %collective-permute-start.13 = (f32[104,128]{1,0:T(8,128)S(1)}, f32[104,128]{1,0:T(8,128)S(1)}, u32[]{:S(2)}, u32[]{:S(2)}) collective-permute-start(f32[104,128]{1,0:T(8,128)S(1)} %get-tuple-element.39), channel_id=1, source_target_pairs={{0,32},{16,48},{32,0},{48,16},{64,96},{80,112},{96,64},{112,80},{1... | collective-permute-start | bytes 159752 | tf_op jit(solution)/shard_map/ppermute | solution.py:418
  62.6 2.8 %collective-permute-start.14 = (f32[104,128]{1,0:T(8,128)S(1)}, f32[104,128]{1,0:T(8,128)S(1)}, u32[]{:S(2)}, u32[]{:S(2)}) collective-permute-start(f32[104,128]{1,0:T(8,128)S(1)} %get-tuple-element.40), channel_id=1, source_target_pairs={{0,48},{16,0},{32,16},{48,32},{64,112},{80,64},{96,80},{112,96},{1... | collective-permute-start | bytes 159752 | tf_op jit(solution)/shard_map/ppermute | solution.py:418
  65.4 1.1 collective-permute-done.13
  66.6 1.3 %collective-permute-done.14 = f32[104,128]{1,0:T(8,128)S(1)} collective-permute-done((f32[104,128]{1,0:T(8,128)S(1)}, f32[104,128]{1,0:T(8,128)S(1)}, u32[]{:S(2)}, u32[]{:S(2)}) %collective-permute-start.14) | collective-permute-done | bytes 53280 | tf_op jit(solution)/shard_map/ppermute | solution.py:418
  67.9 2.9 %collective-permute-done.15 = f32[104,128]{1,0:T(8,128)S(1)} collective-permute-done((f32[104,128]{1,0:T(8,128)S(1)}, f32[104,128]{1,0:T(8,128)S(1)}, u32[]{:S(2)}, u32[]{:S(2)}) %collective-permute-start.15) | collective-permute-done | bytes 53280 | tf_op jit(solution)/shard_map/ppermute | solution.py:418
  70.8 3.1 %collective-permute-start.18 = (f32[104,128]{1,0:T(8,128)S(1)}, f32[104,128]{1,0:T(8,128)S(1)}, u32[]{:S(2)}, u32[]{:S(2)}) collective-permute-start(f32[104,128]{1,0:T(8,128)S(1)} %add_add_fusion.2), channel_id=1, source_target_pairs={{0,128},{16,144},{32,160},{48,176},{64,192},{80,208},{96,224},{112... | collective-permute-start | bytes 159752 | tf_op jit(solution)/shard_map/ppermute | solution.py:423
  73.9 3.2 %collective-permute-start.17 = (f32[104,128]{1,0:T(8,128)S(1)}, f32[104,128]{1,0:T(8,128)S(1)}, u32[]{:S(2)}, u32[]{:S(2)}) collective-permute-start(f32[104,128]{1,0:T(8,128)S(1)} %add_add_fusion.2), channel_id=1, source_target_pairs={{0,64},{16,80},{32,96},{48,112},{64,128},{80,144},{96,160},{112,17... | collective-permute-start | bytes 159752 | tf_op jit(solution)/shard_map/ppermute | solution.py:423
  77.1 0.9 collective-permute-start.16
  78.0 1.5 %collective-permute-done.18 = f32[104,128]{1,0:T(8,128)S(1)} collective-permute-done((f32[104,128]{1,0:T(8,128)S(1)}, f32[104,128]{1,0:T(8,128)S(1)}, u32[]{:S(2)}, u32[]{:S(2)}) %collective-permute-start.18) | collective-permute-done | bytes 53280 | tf_op jit(solution)/shard_map/ppermute | solution.py:423
  80.2 2.0 %collective-permute-done.16 = f32[104,128]{1,0:T(8,128)S(1)} collective-permute-done((f32[104,128]{1,0:T(8,128)S(1)}, f32[104,128]{1,0:T(8,128)S(1)}, u32[]{:S(2)}, u32[]{:S(2)}) %collective-permute-start.16) | collective-permute-done | bytes 53280 | tf_op jit(solution)/shard_map/ppermute | solution.py:423
  82.4 3.2 %collective-permute-start.19 = (f32[104,128]{1,0:T(8,128)S(1)}, f32[104,128]{1,0:T(8,128)S(1)}, u32[]{:S(2)}, u32[]{:S(2)}) collective-permute-start(f32[104,128]{1,0:T(8,128)S(1)} %fusion.15.refs_0_), channel_id=1, source_target_pairs={{0,48},{16,0},{32,16},{48,32},{64,112},{80,64},{96,80},{112,96},{1... | collective-permute-start | bytes 159752 | tf_op jit(solution)/shard_map/ppermute | solution.py:418
  85.6 2.4 %collective-permute-done.21.refs_3_ = f32[104,128]{1,0:T(8,128)S(1)} collective-permute-done((f32[104,128]{1,0:T(8,128)S(1)}, f32[104,128]{1,0:T(8,128)S(1)}, u32[]{:S(2)}, u32[]{:S(2)}) %collective-permute-start.21) | collective-permute-done | bytes 53280 | tf_op jit(solution)/shard_map/ppermute | solution.py:418
  88.3 4.2 %shard_map.82 = (f32[2,3,192,128]{3,2,1,0:T(8,128)S(1)}, f32[64,128]{1,0:T(8,128)S(1)}, f32[64,128]{1,0:T(8,128)S(1)}, f32[64,128]{1,0:T(8,128)S(1)}, f32[64,128]{1,0:T(8,128)S(1)}) custom-call(f32[5,2,3,176,128]{4,3,2,1,0:T(8,128)S(1)} %get-tuple-element.34.a, f32[2,3,176,128]{3,2,1,0:T(8,128)S(1)} %get-tuple-element.35.q, ...), custom_call_target="tpu_custom_call" | custom-call | tf_op jit(solution)/shard_map/pallas_call | solution.py:394
  92.4 1.7 %collective-permute-start.22 = (f32[64,128]{1,0:T(8,128)S(1)}, f32[64,128]{1,0:T(8,128)S(1)}, u32[]{:S(2)}, u32[]{:S(2)}) collective-permute-start(f32[64,128]{1,0:T(8,128)S(1)} %get-tuple-element.44), channel_id=1, source_target_pairs={{0,32},{16,48},{32,0},{48,16},{64,96},{80,112},{96,64},{112,80},{1... | collective-permute-start | bytes 98312 | tf_op jit(solution)/shard_map/ppermute | solution.py:418
  94.2 2.6 %collective-permute-start.23 = (f32[64,128]{1,0:T(8,128)S(1)}, f32[64,128]{1,0:T(8,128)S(1)}, u32[]{:S(2)}, u32[]{:S(2)}) collective-permute-start(f32[64,128]{1,0:T(8,128)S(1)} %get-tuple-element.45), channel_id=1, source_target_pairs={{0,48},{16,0},{32,16},{48,32},{64,112},{80,64},{96,80},{112,96},{1... | collective-permute-start | bytes 98312 | tf_op jit(solution)/shard_map/ppermute | solution.py:418
  96.8 1.1 collective-permute-done.22
  98.4 3.5 %collective-permute-done.24 = f32[64,128]{1,0:T(8,128)S(1)} collective-permute-done((f32[64,128]{1,0:T(8,128)S(1)}, f32[64,128]{1,0:T(8,128)S(1)}, u32[]{:S(2)}, u32[]{:S(2)}) %collective-permute-start.24) | collective-permute-done | bytes 32800 | tf_op jit(solution)/shard_map/ppermute | solution.py:418
  101.9 1.0 collective-permute-start.27
  103.0 3.6 %collective-permute-start.26 = (f32[64,128]{1,0:T(8,128)S(1)}, f32[64,128]{1,0:T(8,128)S(1)}, u32[]{:S(2)}, u32[]{:S(2)}) collective-permute-start(f32[64,128]{1,0:T(8,128)S(1)} %add_add_fusion.3), channel_id=1, source_target_pairs={{0,64},{16,80},{32,96},{48,112},{64,128},{80,144},{96,160},{112,17... | collective-permute-start | bytes 98312 | tf_op jit(solution)/shard_map/ppermute | solution.py:423
  107.1 2.8 %collective-permute-done.27 = f32[64,128]{1,0:T(8,128)S(1)} collective-permute-done((f32[64,128]{1,0:T(8,128)S(1)}, f32[64,128]{1,0:T(8,128)S(1)}, u32[]{:S(2)}, u32[]{:S(2)}) %collective-permute-start.27) | collective-permute-done | bytes 32800 | tf_op jit(solution)/shard_map/ppermute | solution.py:423
  109.9 1.5 %collective-permute-done.25 = f32[64,128]{1,0:T(8,128)S(1)} collective-permute-done((f32[64,128]{1,0:T(8,128)S(1)}, f32[64,128]{1,0:T(8,128)S(1)}, u32[]{:S(2)}, u32[]{:S(2)}) %collective-permute-start.25) | collective-permute-done | bytes 32800 | tf_op jit(solution)/shard_map/ppermute | solution.py:423
  111.6 0.8 collective-permute-start.29
  112.4 2.5 %collective-permute-start.28 = (f32[64,128]{1,0:T(8,128)S(1)}, f32[64,128]{1,0:T(8,128)S(1)}, u32[]{:S(2)}, u32[]{:S(2)}) collective-permute-start(f32[64,128]{1,0:T(8,128)S(1)} %fusion.26.refs_0_), channel_id=1, source_target_pairs={{0,48},{16,0},{32,16},{48,32},{64,112},{80,64},{96,80},{112,96},{1... | collective-permute-start | bytes 98312 | tf_op jit(solution)/shard_map/ppermute | solution.py:418
  114.8 0.8 shard_map.84
  115.6 1.4 %collective-permute-done.30.refs_3_ = f32[64,128]{1,0:T(8,128)S(1)} collective-permute-done((f32[64,128]{1,0:T(8,128)S(1)}, f32[64,128]{1,0:T(8,128)S(1)}, u32[]{:S(2)}, u32[]{:S(2)}) %collective-permute-start.30) | collective-permute-done | bytes 32800 | tf_op jit(solution)/shard_map/ppermute | solution.py:418
  (29 shorter events, 5.3 us)
Async XLA Ops:
  1.7 6.7 %collective-permute-start = (f32[16,24,128]{2,1,0:T(8,128)S(1)}, f32[16,24,128]{2,1,0:T(8,128)S(1)}, u32[]{:S(2)}, u32[]{:S(2)}) collective-permute-start(f32[16,24,128]{2,1,0:T(8,128)S(1)} %get-tuple-element.25), channel_id=1, source_target_pairs={{0,4},{1,5},{2,6},{3,7},{4,8},{5,9},{6,10},{7,11},{8,12},{9,13},{1... | collective-permute-start | bytes 589832 | tf_op jit(solution)/shard_map/ppermute | solution.py:450
  2.3 7.6 %collective-permute-start.1 = (f32[16,24,128]{2,1,0:T(8,128)S(1)}, f32[16,24,128]{2,1,0:T(8,128)S(1)}, u32[]{:S(2)}, u32[]{:S(2)}) collective-permute-start(f32[16,24,128]{2,1,0:T(8,128)S(1)} %get-tuple-element.26), channel_id=1, source_target_pairs={{4,0},{5,1},{6,2},{7,3},{8,4},{9,5},{10,6},{11,7},{12,8},{13,9},{1... | collective-permute-start | bytes 589832 | tf_op jit(solution)/shard_map/ppermute | solution.py:451
  10.6 3.3 %collective-permute-start.2 = (f32[3,176,128]{2,1,0:T(8,128)S(1)}, f32[3,176,128]{2,1,0:T(8,128)S(1)}, u32[]{:S(2)}, u32[]{:S(2)}) collective-permute-start(f32[3,176,128]{2,1,0:T(8,128)S(1)} %get-tuple-element.27), channel_id=1, source_target_pairs={{0,1},{1,0},{2,3},{3,2},{4,5},{5,4},{6,7},{7,6},{8,9},{9,8},{10,11... | collective-permute-start | bytes 811016 | tf_op jit(solution)/shard_map/ppermute | solution.py:453
  10.7 7.8 %collective-permute-start.3 = (f32[3,176,128]{2,1,0:T(8,128)S(1)}, f32[3,176,128]{2,1,0:T(8,128)S(1)}, u32[]{:S(2)}, u32[]{:S(2)}) collective-permute-start(f32[3,176,128]{2,1,0:T(8,128)S(1)} %get-tuple-element.28), channel_id=1, source_target_pairs={{0,0},{1,2},{2,1},{3,3},{4,4},{5,6},{6,5},{7,7},{8,8},{9,10},{10,9... | collective-permute-start | bytes 811016 | tf_op jit(solution)/shard_map/ppermute | solution.py:455
  25.7 6.3 %collective-permute-start.4 = (f32[208,128]{1,0:T(8,128)S(1)}, f32[208,128]{1,0:T(8,128)S(1)}, u32[]{:S(2)}, u32[]{:S(2)}) collective-permute-start(f32[208,128]{1,0:T(8,128)S(1)} %get-tuple-element.31), channel_id=1, source_target_pairs={{0,32},{16,48},{32,0},{48,16},{64,96},{80,112},{96,64},{112,80},{1... | collective-permute-start | bytes 319496 | tf_op jit(solution)/shard_map/ppermute | solution.py:418
  29.0 4.7 %collective-permute-start.5 = (f32[208,128]{1,0:T(8,128)S(1)}, f32[208,128]{1,0:T(8,128)S(1)}, u32[]{:S(2)}, u32[]{:S(2)}) collective-permute-start(f32[208,128]{1,0:T(8,128)S(1)} %get-tuple-element.32), channel_id=1, source_target_pairs={{0,48},{16,0},{32,16},{48,32},{64,112},{80,64},{96,80},{112,96},{1... | collective-permute-start | bytes 319496 | tf_op jit(solution)/shard_map/ppermute | solution.py:418
  30.0 5.9 %collective-permute-start.6 = (f32[208,128]{1,0:T(8,128)S(1)}, f32[208,128]{1,0:T(8,128)S(1)}, u32[]{:S(2)}, u32[]{:S(2)}) collective-permute-start(f32[208,128]{1,0:T(8,128)S(1)} %get-tuple-element.33), channel_id=1, source_target_pairs={{0,16},{16,32},{32,48},{48,0},{64,80},{80,96},{96,112},{112,64},{1... | collective-permute-start | bytes 319496 | tf_op jit(solution)/shard_map/ppermute | solution.py:418
  36.0 10.5 %collective-permute-start.9 = (f32[208,128]{1,0:T(8,128)S(1)}, f32[208,128]{1,0:T(8,128)S(1)}, u32[]{:S(2)}, u32[]{:S(2)}) collective-permute-start(f32[208,128]{1,0:T(8,128)S(1)} %add_add_fusion.1), channel_id=1, source_target_pairs={{0,128},{16,144},{32,160},{48,176},{64,192},{80,208},{96,224},{112... | collective-permute-start | bytes 319496 | tf_op jit(solution)/shard_map/ppermute | solution.py:423
  42.3 6.8 %collective-permute-start.8 = (f32[208,128]{1,0:T(8,128)S(1)}, f32[208,128]{1,0:T(8,128)S(1)}, u32[]{:S(2)}, u32[]{:S(2)}) collective-permute-start(f32[208,128]{1,0:T(8,128)S(1)} %add_add_fusion.1), channel_id=1, source_target_pairs={{0,64},{16,80},{32,96},{48,112},{64,128},{80,144},{96,160},{112,17... | collective-permute-start | bytes 319496 | tf_op jit(solution)/shard_map/ppermute | solution.py:423
  43.8 5.6 %collective-permute-start.7 = (f32[208,128]{1,0:T(8,128)S(1)}, f32[208,128]{1,0:T(8,128)S(1)}, u32[]{:S(2)}, u32[]{:S(2)}) collective-permute-start(f32[208,128]{1,0:T(8,128)S(1)} %add_add_fusion.1), channel_id=1, source_target_pairs={{0,192},{16,208},{32,224},{48,240},{64,0},{80,16},{96,32},{112,48}... | collective-permute-start | bytes 319496 | tf_op jit(solution)/shard_map/ppermute | solution.py:423
  49.5 5.8 %collective-permute-start.12 = (f32[104,128]{1,0:T(8,128)S(1)}, f32[104,128]{1,0:T(8,128)S(1)}, u32[]{:S(2)}, u32[]{:S(2)}) collective-permute-start(f32[104,128]{1,0:T(8,128)S(1)} %fusion.6.refs_0_), channel_id=1, source_target_pairs={{0,32},{16,48},{32,0},{48,16},{64,96},{80,112},{96,64},{112,80},{1... | collective-permute-start | bytes 159752 | tf_op jit(solution)/shard_map/ppermute | solution.py:418
  50.1 6.1 %collective-permute-start.11 = (f32[104,128]{1,0:T(8,128)S(1)}, f32[104,128]{1,0:T(8,128)S(1)}, u32[]{:S(2)}, u32[]{:S(2)}) collective-permute-start(f32[104,128]{1,0:T(8,128)S(1)} %fusion.6.refs_0_), channel_id=1, source_target_pairs={{0,16},{16,32},{32,48},{48,0},{64,80},{80,96},{96,112},{112,64},{1... | collective-permute-start | bytes 159752 | tf_op jit(solution)/shard_map/ppermute | solution.py:418
  50.7 5.5 %collective-permute-start.10 = (f32[104,128]{1,0:T(8,128)S(1)}, f32[104,128]{1,0:T(8,128)S(1)}, u32[]{:S(2)}, u32[]{:S(2)}) collective-permute-start(f32[104,128]{1,0:T(8,128)S(1)} %fusion.6.refs_0_), channel_id=1, source_target_pairs={{0,48},{16,0},{32,16},{48,32},{64,112},{80,64},{96,80},{112,96},{1... | collective-permute-start | bytes 159752 | tf_op jit(solution)/shard_map/ppermute | solution.py:418
  60.9 5.7 %collective-permute-start.13 = (f32[104,128]{1,0:T(8,128)S(1)}, f32[104,128]{1,0:T(8,128)S(1)}, u32[]{:S(2)}, u32[]{:S(2)}) collective-permute-start(f32[104,128]{1,0:T(8,128)S(1)} %get-tuple-element.39), channel_id=1, source_target_pairs={{0,32},{16,48},{32,0},{48,16},{64,96},{80,112},{96,64},{112,80},{1... | collective-permute-start | bytes 159752 | tf_op jit(solution)/shard_map/ppermute | solution.py:418
  62.6 5.2 %collective-permute-start.14 = (f32[104,128]{1,0:T(8,128)S(1)}, f32[104,128]{1,0:T(8,128)S(1)}, u32[]{:S(2)}, u32[]{:S(2)}) collective-permute-start(f32[104,128]{1,0:T(8,128)S(1)} %get-tuple-element.40), channel_id=1, source_target_pairs={{0,48},{16,0},{32,16},{48,32},{64,112},{80,64},{96,80},{112,96},{1... | collective-permute-start | bytes 159752 | tf_op jit(solution)/shard_map/ppermute | solution.py:418
  65.4 5.3 %collective-permute-start.15 = (f32[104,128]{1,0:T(8,128)S(1)}, f32[104,128]{1,0:T(8,128)S(1)}, u32[]{:S(2)}, u32[]{:S(2)}) collective-permute-start(f32[104,128]{1,0:T(8,128)S(1)} %get-tuple-element.41), channel_id=1, source_target_pairs={{0,16},{16,32},{32,48},{48,0},{64,80},{80,96},{96,112},{112,64},{1... | collective-permute-start | bytes 159752 | tf_op jit(solution)/shard_map/ppermute | solution.py:418
  70.8 8.7 %collective-permute-start.18 = (f32[104,128]{1,0:T(8,128)S(1)}, f32[104,128]{1,0:T(8,128)S(1)}, u32[]{:S(2)}, u32[]{:S(2)}) collective-permute-start(f32[104,128]{1,0:T(8,128)S(1)} %add_add_fusion.2), channel_id=1, source_target_pairs={{0,128},{16,144},{32,160},{48,176},{64,192},{80,208},{96,224},{112... | collective-permute-start | bytes 159752 | tf_op jit(solution)/shard_map/ppermute | solution.py:423
  73.9 6.2 %collective-permute-start.17 = (f32[104,128]{1,0:T(8,128)S(1)}, f32[104,128]{1,0:T(8,128)S(1)}, u32[]{:S(2)}, u32[]{:S(2)}) collective-permute-start(f32[104,128]{1,0:T(8,128)S(1)} %add_add_fusion.2), channel_id=1, source_target_pairs={{0,64},{16,80},{32,96},{48,112},{64,128},{80,144},{96,160},{112,17... | collective-permute-start | bytes 159752 | tf_op jit(solution)/shard_map/ppermute | solution.py:423
  77.1 5.0 %collective-permute-start.16 = (f32[104,128]{1,0:T(8,128)S(1)}, f32[104,128]{1,0:T(8,128)S(1)}, u32[]{:S(2)}, u32[]{:S(2)}) collective-permute-start(f32[104,128]{1,0:T(8,128)S(1)} %add_add_fusion.2), channel_id=1, source_target_pairs={{0,192},{16,208},{32,224},{48,240},{64,0},{80,16},{96,32},{112,48}... | collective-permute-start | bytes 159752 | tf_op jit(solution)/shard_map/ppermute | solution.py:423
  82.2 5.8 %collective-permute-start.21 = (f32[104,128]{1,0:T(8,128)S(1)}, f32[104,128]{1,0:T(8,128)S(1)}, u32[]{:S(2)}, u32[]{:S(2)}) collective-permute-start(f32[104,128]{1,0:T(8,128)S(1)} %fusion.15.refs_0_), channel_id=1, source_target_pairs={{0,32},{16,48},{32,0},{48,16},{64,96},{80,112},{96,64},{112,80},{1... | collective-permute-start | bytes 159752 | tf_op jit(solution)/shard_map/ppermute | solution.py:418
  82.3 6.0 %collective-permute-start.20 = (f32[104,128]{1,0:T(8,128)S(1)}, f32[104,128]{1,0:T(8,128)S(1)}, u32[]{:S(2)}, u32[]{:S(2)}) collective-permute-start(f32[104,128]{1,0:T(8,128)S(1)} %fusion.15.refs_0_), channel_id=1, source_target_pairs={{0,16},{16,32},{32,48},{48,0},{64,80},{80,96},{96,112},{112,64},{1... | collective-permute-start | bytes 159752 | tf_op jit(solution)/shard_map/ppermute | solution.py:418
  82.4 5.9 %collective-permute-start.19 = (f32[104,128]{1,0:T(8,128)S(1)}, f32[104,128]{1,0:T(8,128)S(1)}, u32[]{:S(2)}, u32[]{:S(2)}) collective-permute-start(f32[104,128]{1,0:T(8,128)S(1)} %fusion.15.refs_0_), channel_id=1, source_target_pairs={{0,48},{16,0},{32,16},{48,32},{64,112},{80,64},{96,80},{112,96},{1... | collective-permute-start | bytes 159752 | tf_op jit(solution)/shard_map/ppermute | solution.py:418
  92.4 5.5 %collective-permute-start.22 = (f32[64,128]{1,0:T(8,128)S(1)}, f32[64,128]{1,0:T(8,128)S(1)}, u32[]{:S(2)}, u32[]{:S(2)}) collective-permute-start(f32[64,128]{1,0:T(8,128)S(1)} %get-tuple-element.44), channel_id=1, source_target_pairs={{0,32},{16,48},{32,0},{48,16},{64,96},{80,112},{96,64},{112,80},{1... | collective-permute-start | bytes 98312 | tf_op jit(solution)/shard_map/ppermute | solution.py:418
  94.2 4.2 %collective-permute-start.23 = (f32[64,128]{1,0:T(8,128)S(1)}, f32[64,128]{1,0:T(8,128)S(1)}, u32[]{:S(2)}, u32[]{:S(2)}) collective-permute-start(f32[64,128]{1,0:T(8,128)S(1)} %get-tuple-element.45), channel_id=1, source_target_pairs={{0,48},{16,0},{32,16},{48,32},{64,112},{80,64},{96,80},{112,96},{1... | collective-permute-start | bytes 98312 | tf_op jit(solution)/shard_map/ppermute | solution.py:418
  96.8 5.1 %collective-permute-start.24 = (f32[64,128]{1,0:T(8,128)S(1)}, f32[64,128]{1,0:T(8,128)S(1)}, u32[]{:S(2)}, u32[]{:S(2)}) collective-permute-start(f32[64,128]{1,0:T(8,128)S(1)} %get-tuple-element.46), channel_id=1, source_target_pairs={{0,16},{16,32},{32,48},{48,0},{64,80},{80,96},{96,112},{112,64},{1... | collective-permute-start | bytes 98312 | tf_op jit(solution)/shard_map/ppermute | solution.py:418
  101.9 7.9 %collective-permute-start.27 = (f32[64,128]{1,0:T(8,128)S(1)}, f32[64,128]{1,0:T(8,128)S(1)}, u32[]{:S(2)}, u32[]{:S(2)}) collective-permute-start(f32[64,128]{1,0:T(8,128)S(1)} %add_add_fusion.3), channel_id=1, source_target_pairs={{0,128},{16,144},{32,160},{48,176},{64,192},{80,208},{96,224},{112... | collective-permute-start | bytes 98312 | tf_op jit(solution)/shard_map/ppermute | solution.py:423
  103.0 6.9 %collective-permute-start.26 = (f32[64,128]{1,0:T(8,128)S(1)}, f32[64,128]{1,0:T(8,128)S(1)}, u32[]{:S(2)}, u32[]{:S(2)}) collective-permute-start(f32[64,128]{1,0:T(8,128)S(1)} %add_add_fusion.3), channel_id=1, source_target_pairs={{0,64},{16,80},{32,96},{48,112},{64,128},{80,144},{96,160},{112,17... | collective-permute-start | bytes 98312 | tf_op jit(solution)/shard_map/ppermute | solution.py:423
  106.6 4.8 %collective-permute-start.25 = (f32[64,128]{1,0:T(8,128)S(1)}, f32[64,128]{1,0:T(8,128)S(1)}, u32[]{:S(2)}, u32[]{:S(2)}) collective-permute-start(f32[64,128]{1,0:T(8,128)S(1)} %add_add_fusion.3), channel_id=1, source_target_pairs={{0,192},{16,208},{32,224},{48,240},{64,0},{80,16},{96,32},{112,48}... | collective-permute-start | bytes 98312 | tf_op jit(solution)/shard_map/ppermute | solution.py:423
  111.4 5.6 %collective-permute-start.30 = (f32[64,128]{1,0:T(8,128)S(1)}, f32[64,128]{1,0:T(8,128)S(1)}, u32[]{:S(2)}, u32[]{:S(2)}) collective-permute-start(f32[64,128]{1,0:T(8,128)S(1)} %fusion.26.refs_0_), channel_id=1, source_target_pairs={{0,32},{16,48},{32,0},{48,16},{64,96},{80,112},{96,64},{112,80},{1... | collective-permute-start | bytes 98312 | tf_op jit(solution)/shard_map/ppermute | solution.py:418
  111.6 5.5 %collective-permute-start.29 = (f32[64,128]{1,0:T(8,128)S(1)}, f32[64,128]{1,0:T(8,128)S(1)}, u32[]{:S(2)}, u32[]{:S(2)}) collective-permute-start(f32[64,128]{1,0:T(8,128)S(1)} %fusion.26.refs_0_), channel_id=1, source_target_pairs={{0,16},{16,32},{32,48},{48,0},{64,80},{80,96},{96,112},{112,64},{1... | collective-permute-start | bytes 98312 | tf_op jit(solution)/shard_map/ppermute | solution.py:418
  112.4 4.7 %collective-permute-start.28 = (f32[64,128]{1,0:T(8,128)S(1)}, f32[64,128]{1,0:T(8,128)S(1)}, u32[]{:S(2)}, u32[]{:S(2)}) collective-permute-start(f32[64,128]{1,0:T(8,128)S(1)} %fusion.26.refs_0_), channel_id=1, source_target_pairs={{0,48},{16,0},{32,16},{48,32},{64,112},{80,64},{96,80},{112,96},{1... | collective-permute-start | bytes 98312 | tf_op jit(solution)/shard_map/ppermute | solution.py:418

commit v6 on v5

--- a/solution.py
+++ b/solution.py
@@ -16,7 +16,7 @@
 HALO = SWEEPS * OUTER
 ROWS = TILE + 2 * HALO
 PAD = 8
-STEP = 16
+STEP = 8
 PLANES = 16
 PACKS = 3
 ACROSS = 4
@@ -409,7 +409,7 @@
 FIELD = (2, 3, ROWS, TILE)
 PADDED = (2, 3, ROWS + 2 * PAD, TILE)
 SHARED = (2, 2, ROWS, TILE)
-OUT_TURNS = (2, 3, 1)
+OUT_TURNS = (2, 1, 3)
 BACK = (0, 3, 1, 2)
 
 

time: 118 us -> 117 us (level)
  waiting for transfers between devices: 42.9 us -> 37.7 us
  starting transfers between devices: 53.1 us -> 58 us
    ppermute x18, waiting for transfers between devices: 22.4 us -> 17.1 us  [along_y(): return lax.ppermute(array, 'gas', pairs)]
    ppermute x18, starting transfers between devices: 24.9 us -> 29.5 us  [along_y(): return lax.ppermute(array, 'gas', pairs)]
  transfers between devices with their start and end apart: 31 -> 31, of which waited for: 24 -> 26; matrix products, arithmetic and copies ran while one was open for 0% -> 0% of each run, Pallas kernels for 2% -> 2%
where the time goes in v6:
time: 117 us
  starting transfers between devices  58 us (50%)
  waiting for transfers between devices  37.7 us (32%)
  Pallas kernels  20.7 us (18%)
    ppermute x18, starting transfers between devices, along_y(): return lax.ppermute(array, 'gas', pairs)  29.5 us
    ppermute x9, starting transfers between devices, along_z(): return lax.ppermute(array, 'gas', pairs)  23.2 us
    pallas_call x8, Pallas kernels, run(): pl.pallas_call(kernel, out_shape=[jax.ShapeDtypeStruct(dims, F32) for dim...  20.7 us
    ppermute x18, waiting for transfers between devices, along_y(): return lax.ppermute(array, 'gas', pairs)  17.1 us
    ppermute x9, waiting for transfers between devices, along_z(): return lax.ppermute(array, 'gas', pairs)  11.3 us
    ppermute x1, waiting for transfers between devices, on_device(): lax.ppermute(second, 'space', [(i, i - i % ACROSS + swaps[i % ACROSS]) fo...  4.61 us
    ppermute x1, waiting for transfers between devices, on_device(): top = lax.ppermute(up, 'space', ring)  3.2 us
    ppermute x1, starting transfers between devices, on_device(): lax.ppermute(second, 'space', [(i, i - i % ACROSS + swaps[i % ACROSS]) fo...  3.15 us
  transfers between devices with their start and end apart: 31, of which 26 were waited for; matrix products, arithmetic and copies ran while one was open for 0% of the time, Pallas kernels for 2%

profile of v6, /device:TPU:38, one launch (start us, length us, event | category | flops | bytes accessed | tf_op | source)
XLA Modules:
  0.0 117.3 jit_solution(17729588114767193842)
XLA Ops:
  0.6 1.1 shard_map.78
  2.3 1.5 %collective-permute-start.1 = (f32[16,24,128]{2,1,0:T(8,128)S(1)}, f32[16,24,128]{2,1,0:T(8,128)S(1)}, u32[]{:S(2)}, u32[]{:S(2)}) collective-permute-start(f32[16,24,128]{2,1,0:T(8,128)S(1)} %get-tuple-element.26), channel_id=1, source_target_pairs={{4,0},{5,1},{6,2},{7,3},{8,4},{9,5},{10,6},{11,7},{12,8},{13,9},{1... | collective-permute-start | bytes 589832 | tf_op jit(solution)/shard_map/ppermute | solution.py:451
  3.8 1.4 %shard_map.77.planes = f32[16,128,128]{2,1,0:T(8,128)S(1)} custom-call(f32[2,1,2,128,128]{4,3,2,1,0:T(8,128)} %refs_0_.3, f32[2,1,2,128,128]{4,3,2,1,0:T(8,128)} %refs_1_.3, f32[2,1,2,128,128]{4,3,2,1,0:T(8,128)} %refs_2_.3, f32[1,2,128,128]{3,2,1,0:T(8,128)} %refs_3_.3, f32[1,2,128,128]{3,2,1,0:T(8,128)} %refs_4_.3, f32[1,2,128,128]{3,2,1,0:T(8,128)} %refs_5_.3, ...), custom_call_target="tpu_custom_call" | custom-call | bytes 4000000 | tf_op jit(solution)/shard_map/pallas_call | solution.py:394
  5.3 3.2 %collective-permute-done.top = f32[16,24,128]{2,1,0:T(8,128)S(1)} collective-permute-done((f32[16,24,128]{2,1,0:T(8,128)S(1)}, f32[16,24,128]{2,1,0:T(8,128)S(1)}, u32[]{:S(2)}, u32[]{:S(2)}) %collective-permute-start) | collective-permute-done | bytes 196640 | tf_op jit(solution)/shard_map/ppermute | solution.py:450
  8.5 1.4 %collective-permute-done.1.bottom = f32[16,24,128]{2,1,0:T(8,128)S(1)} collective-permute-done((f32[16,24,128]{2,1,0:T(8,128)S(1)}, f32[16,24,128]{2,1,0:T(8,128)S(1)}, u32[]{:S(2)}, u32[]{:S(2)}) %collective-permute-start.1) | collective-permute-done | bytes 196640 | tf_op jit(solution)/shard_map/ppermute | solution.py:451
  10.7 3.2 %collective-permute-start.3 = (f32[3,176,128]{2,1,0:T(8,128)S(1)}, f32[3,176,128]{2,1,0:T(8,128)S(1)}, u32[]{:S(2)}, u32[]{:S(2)}) collective-permute-start(f32[3,176,128]{2,1,0:T(8,128)S(1)} %get-tuple-element.28), channel_id=1, source_target_pairs={{0,0},{1,2},{2,1},{3,3},{4,4},{5,6},{6,5},{7,7},{8,8},{9,10},{10,9... | collective-permute-start | bytes 811016 | tf_op jit(solution)/shard_map/ppermute | solution.py:455
  13.9 4.6 %collective-permute-done.3.second = f32[3,176,128]{2,1,0:T(8,128)S(1)} collective-permute-done((f32[3,176,128]{2,1,0:T(8,128)S(1)}, f32[3,176,128]{2,1,0:T(8,128)S(1)}, u32[]{:S(2)}, u32[]{:S(2)}) %collective-permute-start.3) | collective-permute-done | bytes 270368 | tf_op jit(solution)/shard_map/ppermute | solution.py:455
  18.5 7.1 %shard_map.80 = (f32[5,2,3,176,128]{4,3,2,1,0:T(8,128)S(1)}, f32[2,3,176,128]{3,2,1,0:T(8,128)S(1)}, f32[2,3,192,128]{3,2,1,0:T(8,128)S(1)}, f32[2,3,192,128]{3,...) custom-call(f32[16,128,128]{2,1,0:T(8,128)S(1)} %shard_map.77.planes, ...), custom_call_target="tpu_custom_call" | custom-call | tf_op jit(solution)/shard_map/pallas_call | solution.py:394
  25.6 3.3 %collective-permute-start.4 = (f32[208,128]{1,0:T(8,128)S(1)}, f32[208,128]{1,0:T(8,128)S(1)}, u32[]{:S(2)}, u32[]{:S(2)}) collective-permute-start(f32[208,128]{1,0:T(8,128)S(1)} %get-tuple-element.31), channel_id=1, source_target_pairs={{0,32},{16,48},{32,0},{48,16},{64,96},{80,112},{96,64},{112,80},{1... | collective-permute-start | bytes 319496 | tf_op jit(solution)/shard_map/ppermute | solution.py:418
  29.5 2.6 %collective-permute-start.6 = (f32[208,128]{1,0:T(8,128)S(1)}, f32[208,128]{1,0:T(8,128)S(1)}, u32[]{:S(2)}, u32[]{:S(2)}) collective-permute-start(f32[208,128]{1,0:T(8,128)S(1)} %get-tuple-element.33), channel_id=1, source_target_pairs={{0,48},{16,0},{32,16},{48,32},{64,112},{80,64},{96,80},{112,96},{1... | collective-permute-start | bytes 319496 | tf_op jit(solution)/shard_map/ppermute | solution.py:418
  32.1 2.7 %collective-permute-done.5 = f32[208,128]{1,0:T(8,128)S(1)} collective-permute-done((f32[208,128]{1,0:T(8,128)S(1)}, f32[208,128]{1,0:T(8,128)S(1)}, u32[]{:S(2)}, u32[]{:S(2)}) %collective-permute-start.5) | collective-permute-done | bytes 106528 | tf_op jit(solution)/shard_map/ppermute | solution.py:418
  34.8 6.4 %collective-permute-start.9 = (f32[208,128]{1,0:T(8,128)S(1)}, f32[208,128]{1,0:T(8,128)S(1)}, u32[]{:S(2)}, u32[]{:S(2)}) collective-permute-start(f32[208,128]{1,0:T(8,128)S(1)} %add_add_fusion.1), channel_id=1, source_target_pairs={{0,128},{16,144},{32,160},{48,176},{64,192},{80,208},{96,224},{112... | collective-permute-start | bytes 319496 | tf_op jit(solution)/shard_map/ppermute | solution.py:423
  41.2 1.5 %collective-permute-start.8 = (f32[208,128]{1,0:T(8,128)S(1)}, f32[208,128]{1,0:T(8,128)S(1)}, u32[]{:S(2)}, u32[]{:S(2)}) collective-permute-start(f32[208,128]{1,0:T(8,128)S(1)} %add_add_fusion.1), channel_id=1, source_target_pairs={{0,64},{16,80},{32,96},{48,112},{64,128},{80,144},{96,160},{112,17... | collective-permute-start | bytes 319496 | tf_op jit(solution)/shard_map/ppermute | solution.py:423
  42.7 2.7 %collective-permute-start.7 = (f32[208,128]{1,0:T(8,128)S(1)}, f32[208,128]{1,0:T(8,128)S(1)}, u32[]{:S(2)}, u32[]{:S(2)}) collective-permute-start(f32[208,128]{1,0:T(8,128)S(1)} %add_add_fusion.1), channel_id=1, source_target_pairs={{0,192},{16,208},{32,224},{48,240},{64,0},{80,16},{96,32},{112,48}... | collective-permute-start | bytes 319496 | tf_op jit(solution)/shard_map/ppermute | solution.py:423
  45.3 2.7 %collective-permute-done.8 = f32[208,128]{1,0:T(8,128)S(1)} collective-permute-done((f32[208,128]{1,0:T(8,128)S(1)}, f32[208,128]{1,0:T(8,128)S(1)}, u32[]{:S(2)}, u32[]{:S(2)}) %collective-permute-start.8) | collective-permute-done | bytes 106528 | tf_op jit(solution)/shard_map/ppermute | solution.py:423
  48.3 1.5 %collective-permute-start.12 = (f32[104,128]{1,0:T(8,128)S(1)}, f32[104,128]{1,0:T(8,128)S(1)}, u32[]{:S(2)}, u32[]{:S(2)}) collective-permute-start(f32[104,128]{1,0:T(8,128)S(1)} %fusion.6.refs_0_), channel_id=1, source_target_pairs={{0,32},{16,48},{32,0},{48,16},{64,96},{80,112},{96,64},{112,80},{1... | collective-permute-start | bytes 159752 | tf_op jit(solution)/shard_map/ppermute | solution.py:418
  49.9 2.6 %collective-permute-start.11 = (f32[104,128]{1,0:T(8,128)S(1)}, f32[104,128]{1,0:T(8,128)S(1)}, u32[]{:S(2)}, u32[]{:S(2)}) collective-permute-start(f32[104,128]{1,0:T(8,128)S(1)} %fusion.6.refs_0_), channel_id=1, source_target_pairs={{0,16},{16,32},{32,48},{48,0},{64,80},{80,96},{96,112},{112,64},{1... | collective-permute-start | bytes 159752 | tf_op jit(solution)/shard_map/ppermute | solution.py:418
  53.1 0.9 collective-permute-done.12.refs_3_
  54.1 1.2 collective-permute-done.11.refs_2_
  55.2 1.6 %collective-permute-done.10.refs_1_ = f32[104,128]{1,0:T(8,128)S(1)} collective-permute-done((f32[104,128]{1,0:T(8,128)S(1)}, f32[104,128]{1,0:T(8,128)S(1)}, u32[]{:S(2)}, u32[]{:S(2)}) %collective-permute-start.10) | collective-permute-done | bytes 53280 | tf_op jit(solution)/shard_map/ppermute | solution.py:418
  56.8 4.7 %shard_map.81 = (f32[2,3,192,128]{3,2,1,0:T(8,128)S(1)}, f32[104,128]{1,0:T(8,128)S(1)}, f32[104,128]{1,0:T(8,128)S(1)}, f32[104,128]{1,0:T(8,128)S(1)}, f32[104,128]{1,0:T(8,128)S(1)}) custom-call(f32[5,2,3,176,128]{4,3,2,1,0:T(8,128)S(1)} %get-tuple-element.34.a, f32[2,3,176,128]{3,2,1,0:T(8,128)S(1)} %get-tuple-element.35.q, ...), custom_call_target="tpu_custom_call" | custom-call | tf_op jit(solution)/shard_map/pallas_call | solution.py:394
  61.6 0.9 collective-permute-start.13
  62.4 2.2 %collective-permute-start.14 = (f32[104,128]{1,0:T(8,128)S(1)}, f32[104,128]{1,0:T(8,128)S(1)}, u32[]{:S(2)}, u32[]{:S(2)}) collective-permute-start(f32[104,128]{1,0:T(8,128)S(1)} %get-tuple-element.40), channel_id=1, source_target_pairs={{0,16},{16,32},{32,48},{48,0},{64,80},{80,96},{96,112},{112,64},{1... | collective-permute-start | bytes 159752 | tf_op jit(solution)/shard_map/ppermute | solution.py:418
  64.6 1.1 collective-permute-start.15
  65.7 1.6 %collective-permute-done.13 = f32[104,128]{1,0:T(8,128)S(1)} collective-permute-done((f32[104,128]{1,0:T(8,128)S(1)}, f32[104,128]{1,0:T(8,128)S(1)}, u32[]{:S(2)}, u32[]{:S(2)}) %collective-permute-start.13) | collective-permute-done | bytes 53280 | tf_op jit(solution)/shard_map/ppermute | solution.py:418
  67.9 0.9 collective-permute-done.15
  68.7 3.7 %collective-permute-start.18 = (f32[104,128]{1,0:T(8,128)S(1)}, f32[104,128]{1,0:T(8,128)S(1)}, u32[]{:S(2)}, u32[]{:S(2)}) collective-permute-start(f32[104,128]{1,0:T(8,128)S(1)} %add_add_fusion.2), channel_id=1, source_target_pairs={{0,128},{16,144},{32,160},{48,176},{64,192},{80,208},{96,224},{112... | collective-permute-start | bytes 159752 | tf_op jit(solution)/shard_map/ppermute | solution.py:423
  72.4 3.0 %collective-permute-start.17 = (f32[104,128]{1,0:T(8,128)S(1)}, f32[104,128]{1,0:T(8,128)S(1)}, u32[]{:S(2)}, u32[]{:S(2)}) collective-permute-start(f32[104,128]{1,0:T(8,128)S(1)} %add_add_fusion.2), channel_id=1, source_target_pairs={{0,64},{16,80},{32,96},{48,112},{64,128},{80,144},{96,160},{112,17... | collective-permute-start | bytes 159752 | tf_op jit(solution)/shard_map/ppermute | solution.py:423
  75.4 1.2 %collective-permute-start.16 = (f32[104,128]{1,0:T(8,128)S(1)}, f32[104,128]{1,0:T(8,128)S(1)}, u32[]{:S(2)}, u32[]{:S(2)}) collective-permute-start(f32[104,128]{1,0:T(8,128)S(1)} %add_add_fusion.2), channel_id=1, source_target_pairs={{0,192},{16,208},{32,224},{48,240},{64,0},{80,16},{96,32},{112,48}... | collective-permute-start | bytes 159752 | tf_op jit(solution)/shard_map/ppermute | solution.py:423
  76.5 1.0 collective-permute-done.18
  77.5 1.1 collective-permute-done.17
  78.6 1.7 %collective-permute-done.16 = f32[104,128]{1,0:T(8,128)S(1)} collective-permute-done((f32[104,128]{1,0:T(8,128)S(1)}, f32[104,128]{1,0:T(8,128)S(1)}, u32[]{:S(2)}, u32[]{:S(2)}) %collective-permute-start.16) | collective-permute-done | bytes 53280 | tf_op jit(solution)/shard_map/ppermute | solution.py:423
  80.4 1.7 %collective-permute-start.21 = (f32[104,128]{1,0:T(8,128)S(1)}, f32[104,128]{1,0:T(8,128)S(1)}, u32[]{:S(2)}, u32[]{:S(2)}) collective-permute-start(f32[104,128]{1,0:T(8,128)S(1)} %fusion.15.refs_0_), channel_id=1, source_target_pairs={{0,32},{16,48},{32,0},{48,16},{64,96},{80,112},{96,64},{112,80},{1... | collective-permute-start | bytes 159752 | tf_op jit(solution)/shard_map/ppermute | solution.py:418
  82.1 1.5 %collective-permute-start.20 = (f32[104,128]{1,0:T(8,128)S(1)}, f32[104,128]{1,0:T(8,128)S(1)}, u32[]{:S(2)}, u32[]{:S(2)}) collective-permute-start(f32[104,128]{1,0:T(8,128)S(1)} %fusion.15.refs_0_), channel_id=1, source_target_pairs={{0,16},{16,32},{32,48},{48,0},{64,80},{80,96},{96,112},{112,64},{1... | collective-permute-start | bytes 159752 | tf_op jit(solution)/shard_map/ppermute | solution.py:418
  83.6 1.7 %collective-permute-start.19 = (f32[104,128]{1,0:T(8,128)S(1)}, f32[104,128]{1,0:T(8,128)S(1)}, u32[]{:S(2)}, u32[]{:S(2)}) collective-permute-start(f32[104,128]{1,0:T(8,128)S(1)} %fusion.15.refs_0_), channel_id=1, source_target_pairs={{0,48},{16,0},{32,16},{48,32},{64,112},{80,64},{96,80},{112,96},{1... | collective-permute-start | bytes 159752 | tf_op jit(solution)/shard_map/ppermute | solution.py:418
  86.2 1.3 %collective-permute-done.20.refs_2_ = f32[104,128]{1,0:T(8,128)S(1)} collective-permute-done((f32[104,128]{1,0:T(8,128)S(1)}, f32[104,128]{1,0:T(8,128)S(1)}, u32[]{:S(2)}, u32[]{:S(2)}) %collective-permute-start.20) | collective-permute-done | bytes 53280 | tf_op jit(solution)/shard_map/ppermute | solution.py:418
  87.8 4.2 %shard_map.82 = (f32[2,3,192,128]{3,2,1,0:T(8,128)S(1)}, f32[64,128]{1,0:T(8,128)S(1)}, f32[64,128]{1,0:T(8,128)S(1)}, f32[64,128]{1,0:T(8,128)S(1)}, f32[64,128]{1,0:T(8,128)S(1)}) custom-call(f32[5,2,3,176,128]{4,3,2,1,0:T(8,128)S(1)} %get-tuple-element.34.a, f32[2,3,176,128]{3,2,1,0:T(8,128)S(1)} %get-tuple-element.35.q, ...), custom_call_target="tpu_custom_call" | custom-call | tf_op jit(solution)/shard_map/pallas_call | solution.py:394
  91.9 1.6 %collective-permute-start.22 = (f32[64,128]{1,0:T(8,128)S(1)}, f32[64,128]{1,0:T(8,128)S(1)}, u32[]{:S(2)}, u32[]{:S(2)}) collective-permute-start(f32[64,128]{1,0:T(8,128)S(1)} %get-tuple-element.44), channel_id=1, source_target_pairs={{0,32},{16,48},{32,0},{48,16},{64,96},{80,112},{96,64},{112,80},{1... | collective-permute-start | bytes 98312 | tf_op jit(solution)/shard_map/ppermute | solution.py:418
  93.5 2.3 %collective-permute-start.23 = (f32[64,128]{1,0:T(8,128)S(1)}, f32[64,128]{1,0:T(8,128)S(1)}, u32[]{:S(2)}, u32[]{:S(2)}) collective-permute-start(f32[64,128]{1,0:T(8,128)S(1)} %get-tuple-element.45), channel_id=1, source_target_pairs={{0,16},{16,32},{32,48},{48,0},{64,80},{80,96},{96,112},{112,64},{1... | collective-permute-start | bytes 98312 | tf_op jit(solution)/shard_map/ppermute | solution.py:418
  95.8 0.9 collective-permute-start.24
  97.4 1.2 %collective-permute-done.23 = f32[64,128]{1,0:T(8,128)S(1)} collective-permute-done((f32[64,128]{1,0:T(8,128)S(1)}, f32[64,128]{1,0:T(8,128)S(1)}, u32[]{:S(2)}, u32[]{:S(2)}) %collective-permute-start.23) | collective-permute-done | bytes 32800 | tf_op jit(solution)/shard_map/ppermute | solution.py:418
  98.6 1.1 collective-permute-done.24
  100.5 3.8 %collective-permute-start.26 = (f32[64,128]{1,0:T(8,128)S(1)}, f32[64,128]{1,0:T(8,128)S(1)}, u32[]{:S(2)}, u32[]{:S(2)}) collective-permute-start(f32[64,128]{1,0:T(8,128)S(1)} %add_add_fusion.3), channel_id=1, source_target_pairs={{0,64},{16,80},{32,96},{48,112},{64,128},{80,144},{96,160},{112,17... | collective-permute-start | bytes 98312 | tf_op jit(solution)/shard_map/ppermute | solution.py:423
  104.6 3.0 %collective-permute-done.27 = f32[64,128]{1,0:T(8,128)S(1)} collective-permute-done((f32[64,128]{1,0:T(8,128)S(1)}, f32[64,128]{1,0:T(8,128)S(1)}, u32[]{:S(2)}, u32[]{:S(2)}) %collective-permute-start.27) | collective-permute-done | bytes 32800 | tf_op jit(solution)/shard_map/ppermute | solution.py:423
  107.6 1.5 %collective-permute-done.25 = f32[64,128]{1,0:T(8,128)S(1)} collective-permute-done((f32[64,128]{1,0:T(8,128)S(1)}, f32[64,128]{1,0:T(8,128)S(1)}, u32[]{:S(2)}, u32[]{:S(2)}) %collective-permute-start.25) | collective-permute-done | bytes 32800 | tf_op jit(solution)/shard_map/ppermute | solution.py:423
  109.1 1.1 collective-permute-start.30
  110.3 2.4 %collective-permute-start.29 = (f32[64,128]{1,0:T(8,128)S(1)}, f32[64,128]{1,0:T(8,128)S(1)}, u32[]{:S(2)}, u32[]{:S(2)}) collective-permute-start(f32[64,128]{1,0:T(8,128)S(1)} %fusion.26.refs_0_), channel_id=1, source_target_pairs={{0,16},{16,32},{32,48},{48,0},{64,80},{80,96},{96,112},{112,64},{1... | collective-permute-start | bytes 98312 | tf_op jit(solution)/shard_map/ppermute | solution.py:418
  115.4 1.2 %collective-permute-done.28.refs_1_ = f32[64,128]{1,0:T(8,128)S(1)} collective-permute-done((f32[64,128]{1,0:T(8,128)S(1)}, f32[64,128]{1,0:T(8,128)S(1)}, u32[]{:S(2)}, u32[]{:S(2)}) %collective-permute-start.28) | collective-permute-done | bytes 32800 | tf_op jit(solution)/shard_map/ppermute | solution.py:418
  (29 shorter events, 10.0 us)
Async XLA Ops:
  1.7 6.7 %collective-permute-start = (f32[16,24,128]{2,1,0:T(8,128)S(1)}, f32[16,24,128]{2,1,0:T(8,128)S(1)}, u32[]{:S(2)}, u32[]{:S(2)}) collective-permute-start(f32[16,24,128]{2,1,0:T(8,128)S(1)} %get-tuple-element.25), channel_id=1, source_target_pairs={{0,4},{1,5},{2,6},{3,7},{4,8},{5,9},{6,10},{7,11},{8,12},{9,13},{1... | collective-permute-start | bytes 589832 | tf_op jit(solution)/shard_map/ppermute | solution.py:450
  2.3 7.6 %collective-permute-start.1 = (f32[16,24,128]{2,1,0:T(8,128)S(1)}, f32[16,24,128]{2,1,0:T(8,128)S(1)}, u32[]{:S(2)}, u32[]{:S(2)}) collective-permute-start(f32[16,24,128]{2,1,0:T(8,128)S(1)} %get-tuple-element.26), channel_id=1, source_target_pairs={{4,0},{5,1},{6,2},{7,3},{8,4},{9,5},{10,6},{11,7},{12,8},{13,9},{1... | collective-permute-start | bytes 589832 | tf_op jit(solution)/shard_map/ppermute | solution.py:451
  10.6 3.3 %collective-permute-start.2 = (f32[3,176,128]{2,1,0:T(8,128)S(1)}, f32[3,176,128]{2,1,0:T(8,128)S(1)}, u32[]{:S(2)}, u32[]{:S(2)}) collective-permute-start(f32[3,176,128]{2,1,0:T(8,128)S(1)} %get-tuple-element.27), channel_id=1, source_target_pairs={{0,1},{1,0},{2,3},{3,2},{4,5},{5,4},{6,7},{7,6},{8,9},{9,8},{10,11... | collective-permute-start | bytes 811016 | tf_op jit(solution)/shard_map/ppermute | solution.py:453
  10.7 7.8 %collective-permute-start.3 = (f32[3,176,128]{2,1,0:T(8,128)S(1)}, f32[3,176,128]{2,1,0:T(8,128)S(1)}, u32[]{:S(2)}, u32[]{:S(2)}) collective-permute-start(f32[3,176,128]{2,1,0:T(8,128)S(1)} %get-tuple-element.28), channel_id=1, source_target_pairs={{0,0},{1,2},{2,1},{3,3},{4,4},{5,6},{6,5},{7,7},{8,8},{9,10},{10,9... | collective-permute-start | bytes 811016 | tf_op jit(solution)/shard_map/ppermute | solution.py:455
  25.6 6.5 %collective-permute-start.4 = (f32[208,128]{1,0:T(8,128)S(1)}, f32[208,128]{1,0:T(8,128)S(1)}, u32[]{:S(2)}, u32[]{:S(2)}) collective-permute-start(f32[208,128]{1,0:T(8,128)S(1)} %get-tuple-element.31), channel_id=1, source_target_pairs={{0,32},{16,48},{32,0},{48,16},{64,96},{80,112},{96,64},{112,80},{1... | collective-permute-start | bytes 319496 | tf_op jit(solution)/shard_map/ppermute | solution.py:418
  28.9 5.9 %collective-permute-start.5 = (f32[208,128]{1,0:T(8,128)S(1)}, f32[208,128]{1,0:T(8,128)S(1)}, u32[]{:S(2)}, u32[]{:S(2)}) collective-permute-start(f32[208,128]{1,0:T(8,128)S(1)} %get-tuple-element.32), channel_id=1, source_target_pairs={{0,16},{16,32},{32,48},{48,0},{64,80},{80,96},{96,112},{112,64},{1... | collective-permute-start | bytes 319496 | tf_op jit(solution)/shard_map/ppermute | solution.py:418
  29.5 5.2 %collective-permute-start.6 = (f32[208,128]{1,0:T(8,128)S(1)}, f32[208,128]{1,0:T(8,128)S(1)}, u32[]{:S(2)}, u32[]{:S(2)}) collective-permute-start(f32[208,128]{1,0:T(8,128)S(1)} %get-tuple-element.33), channel_id=1, source_target_pairs={{0,48},{16,0},{32,16},{48,32},{64,112},{80,64},{96,80},{112,96},{1... | collective-permute-start | bytes 319496 | tf_op jit(solution)/shard_map/ppermute | solution.py:418
  34.8 10.5 %collective-permute-start.9 = (f32[208,128]{1,0:T(8,128)S(1)}, f32[208,128]{1,0:T(8,128)S(1)}, u32[]{:S(2)}, u32[]{:S(2)}) collective-permute-start(f32[208,128]{1,0:T(8,128)S(1)} %add_add_fusion.1), channel_id=1, source_target_pairs={{0,128},{16,144},{32,160},{48,176},{64,192},{80,208},{96,224},{112... | collective-permute-start | bytes 319496 | tf_op jit(solution)/shard_map/ppermute | solution.py:423
  41.2 6.8 %collective-permute-start.8 = (f32[208,128]{1,0:T(8,128)S(1)}, f32[208,128]{1,0:T(8,128)S(1)}, u32[]{:S(2)}, u32[]{:S(2)}) collective-permute-start(f32[208,128]{1,0:T(8,128)S(1)} %add_add_fusion.1), channel_id=1, source_target_pairs={{0,64},{16,80},{32,96},{48,112},{64,128},{80,144},{96,160},{112,17... | collective-permute-start | bytes 319496 | tf_op jit(solution)/shard_map/ppermute | solution.py:423
  42.7 5.6 %collective-permute-start.7 = (f32[208,128]{1,0:T(8,128)S(1)}, f32[208,128]{1,0:T(8,128)S(1)}, u32[]{:S(2)}, u32[]{:S(2)}) collective-permute-start(f32[208,128]{1,0:T(8,128)S(1)} %add_add_fusion.1), channel_id=1, source_target_pairs={{0,192},{16,208},{32,224},{48,240},{64,0},{80,16},{96,32},{112,48}... | collective-permute-start | bytes 319496 | tf_op jit(solution)/shard_map/ppermute | solution.py:423
  48.3 5.7 %collective-permute-start.12 = (f32[104,128]{1,0:T(8,128)S(1)}, f32[104,128]{1,0:T(8,128)S(1)}, u32[]{:S(2)}, u32[]{:S(2)}) collective-permute-start(f32[104,128]{1,0:T(8,128)S(1)} %fusion.6.refs_0_), channel_id=1, source_target_pairs={{0,32},{16,48},{32,0},{48,16},{64,96},{80,112},{96,64},{112,80},{1... | collective-permute-start | bytes 159752 | tf_op jit(solution)/shard_map/ppermute | solution.py:418
  49.9 5.3 %collective-permute-start.11 = (f32[104,128]{1,0:T(8,128)S(1)}, f32[104,128]{1,0:T(8,128)S(1)}, u32[]{:S(2)}, u32[]{:S(2)}) collective-permute-start(f32[104,128]{1,0:T(8,128)S(1)} %fusion.6.refs_0_), channel_id=1, source_target_pairs={{0,16},{16,32},{32,48},{48,0},{64,80},{80,96},{96,112},{112,64},{1... | collective-permute-start | bytes 159752 | tf_op jit(solution)/shard_map/ppermute | solution.py:418
  52.5 4.3 %collective-permute-start.10 = (f32[104,128]{1,0:T(8,128)S(1)}, f32[104,128]{1,0:T(8,128)S(1)}, u32[]{:S(2)}, u32[]{:S(2)}) collective-permute-start(f32[104,128]{1,0:T(8,128)S(1)} %fusion.6.refs_0_), channel_id=1, source_target_pairs={{0,48},{16,0},{32,16},{48,32},{64,112},{80,64},{96,80},{112,96},{1... | collective-permute-start | bytes 159752 | tf_op jit(solution)/shard_map/ppermute | solution.py:418
  61.6 5.7 %collective-permute-start.13 = (f32[104,128]{1,0:T(8,128)S(1)}, f32[104,128]{1,0:T(8,128)S(1)}, u32[]{:S(2)}, u32[]{:S(2)}) collective-permute-start(f32[104,128]{1,0:T(8,128)S(1)} %get-tuple-element.39), channel_id=1, source_target_pairs={{0,32},{16,48},{32,0},{48,16},{64,96},{80,112},{96,64},{112,80},{1... | collective-permute-start | bytes 159752 | tf_op jit(solution)/shard_map/ppermute | solution.py:418
  62.4 5.4 %collective-permute-start.14 = (f32[104,128]{1,0:T(8,128)S(1)}, f32[104,128]{1,0:T(8,128)S(1)}, u32[]{:S(2)}, u32[]{:S(2)}) collective-permute-start(f32[104,128]{1,0:T(8,128)S(1)} %get-tuple-element.40), channel_id=1, source_target_pairs={{0,16},{16,32},{32,48},{48,0},{64,80},{80,96},{96,112},{112,64},{1... | collective-permute-start | bytes 159752 | tf_op jit(solution)/shard_map/ppermute | solution.py:418
  64.6 4.1 %collective-permute-start.15 = (f32[104,128]{1,0:T(8,128)S(1)}, f32[104,128]{1,0:T(8,128)S(1)}, u32[]{:S(2)}, u32[]{:S(2)}) collective-permute-start(f32[104,128]{1,0:T(8,128)S(1)} %get-tuple-element.41), channel_id=1, source_target_pairs={{0,48},{16,0},{32,16},{48,32},{64,112},{80,64},{96,80},{112,96},{1... | collective-permute-start | bytes 159752 | tf_op jit(solution)/shard_map/ppermute | solution.py:418
  68.7 8.8 %collective-permute-start.18 = (f32[104,128]{1,0:T(8,128)S(1)}, f32[104,128]{1,0:T(8,128)S(1)}, u32[]{:S(2)}, u32[]{:S(2)}) collective-permute-start(f32[104,128]{1,0:T(8,128)S(1)} %add_add_fusion.2), channel_id=1, source_target_pairs={{0,128},{16,144},{32,160},{48,176},{64,192},{80,208},{96,224},{112... | collective-permute-start | bytes 159752 | tf_op jit(solution)/shard_map/ppermute | solution.py:423
  72.4 6.2 %collective-permute-start.17 = (f32[104,128]{1,0:T(8,128)S(1)}, f32[104,128]{1,0:T(8,128)S(1)}, u32[]{:S(2)}, u32[]{:S(2)}) collective-permute-start(f32[104,128]{1,0:T(8,128)S(1)} %add_add_fusion.2), channel_id=1, source_target_pairs={{0,64},{16,80},{32,96},{48,112},{64,128},{80,144},{96,160},{112,17... | collective-permute-start | bytes 159752 | tf_op jit(solution)/shard_map/ppermute | solution.py:423
  75.4 5.0 %collective-permute-start.16 = (f32[104,128]{1,0:T(8,128)S(1)}, f32[104,128]{1,0:T(8,128)S(1)}, u32[]{:S(2)}, u32[]{:S(2)}) collective-permute-start(f32[104,128]{1,0:T(8,128)S(1)} %add_add_fusion.2), channel_id=1, source_target_pairs={{0,192},{16,208},{32,224},{48,240},{64,0},{80,16},{96,32},{112,48}... | collective-permute-start | bytes 159752 | tf_op jit(solution)/shard_map/ppermute | solution.py:423
  80.4 5.7 %collective-permute-start.21 = (f32[104,128]{1,0:T(8,128)S(1)}, f32[104,128]{1,0:T(8,128)S(1)}, u32[]{:S(2)}, u32[]{:S(2)}) collective-permute-start(f32[104,128]{1,0:T(8,128)S(1)} %fusion.15.refs_0_), channel_id=1, source_target_pairs={{0,32},{16,48},{32,0},{48,16},{64,96},{80,112},{96,64},{112,80},{1... | collective-permute-start | bytes 159752 | tf_op jit(solution)/shard_map/ppermute | solution.py:418
  82.1 5.3 %collective-permute-start.20 = (f32[104,128]{1,0:T(8,128)S(1)}, f32[104,128]{1,0:T(8,128)S(1)}, u32[]{:S(2)}, u32[]{:S(2)}) collective-permute-start(f32[104,128]{1,0:T(8,128)S(1)} %fusion.15.refs_0_), channel_id=1, source_target_pairs={{0,16},{16,32},{32,48},{48,0},{64,80},{80,96},{96,112},{112,64},{1... | collective-permute-start | bytes 159752 | tf_op jit(solution)/shard_map/ppermute | solution.py:418
  83.6 4.1 %collective-permute-start.19 = (f32[104,128]{1,0:T(8,128)S(1)}, f32[104,128]{1,0:T(8,128)S(1)}, u32[]{:S(2)}, u32[]{:S(2)}) collective-permute-start(f32[104,128]{1,0:T(8,128)S(1)} %fusion.15.refs_0_), channel_id=1, source_target_pairs={{0,48},{16,0},{32,16},{48,32},{64,112},{80,64},{96,80},{112,96},{1... | collective-permute-start | bytes 159752 | tf_op jit(solution)/shard_map/ppermute | solution.py:418
  91.9 5.5 %collective-permute-start.22 = (f32[64,128]{1,0:T(8,128)S(1)}, f32[64,128]{1,0:T(8,128)S(1)}, u32[]{:S(2)}, u32[]{:S(2)}) collective-permute-start(f32[64,128]{1,0:T(8,128)S(1)} %get-tuple-element.44), channel_id=1, source_target_pairs={{0,32},{16,48},{32,0},{48,16},{64,96},{80,112},{96,64},{112,80},{1... | collective-permute-start | bytes 98312 | tf_op jit(solution)/shard_map/ppermute | solution.py:418
  93.5 5.1 %collective-permute-start.23 = (f32[64,128]{1,0:T(8,128)S(1)}, f32[64,128]{1,0:T(8,128)S(1)}, u32[]{:S(2)}, u32[]{:S(2)}) collective-permute-start(f32[64,128]{1,0:T(8,128)S(1)} %get-tuple-element.45), channel_id=1, source_target_pairs={{0,16},{16,32},{32,48},{48,0},{64,80},{80,96},{96,112},{112,64},{1... | collective-permute-start | bytes 98312 | tf_op jit(solution)/shard_map/ppermute | solution.py:418
  95.8 3.9 %collective-permute-start.24 = (f32[64,128]{1,0:T(8,128)S(1)}, f32[64,128]{1,0:T(8,128)S(1)}, u32[]{:S(2)}, u32[]{:S(2)}) collective-permute-start(f32[64,128]{1,0:T(8,128)S(1)} %get-tuple-element.46), channel_id=1, source_target_pairs={{0,48},{16,0},{32,16},{48,32},{64,112},{80,64},{96,80},{112,96},{1... | collective-permute-start | bytes 98312 | tf_op jit(solution)/shard_map/ppermute | solution.py:418
  99.7 7.9 %collective-permute-start.27 = (f32[64,128]{1,0:T(8,128)S(1)}, f32[64,128]{1,0:T(8,128)S(1)}, u32[]{:S(2)}, u32[]{:S(2)}) collective-permute-start(f32[64,128]{1,0:T(8,128)S(1)} %add_add_fusion.3), channel_id=1, source_target_pairs={{0,128},{16,144},{32,160},{48,176},{64,192},{80,208},{96,224},{112... | collective-permute-start | bytes 98312 | tf_op jit(solution)/shard_map/ppermute | solution.py:423
  100.5 7.2 %collective-permute-start.26 = (f32[64,128]{1,0:T(8,128)S(1)}, f32[64,128]{1,0:T(8,128)S(1)}, u32[]{:S(2)}, u32[]{:S(2)}) collective-permute-start(f32[64,128]{1,0:T(8,128)S(1)} %add_add_fusion.3), channel_id=1, source_target_pairs={{0,64},{16,80},{32,96},{48,112},{64,128},{80,144},{96,160},{112,17... | collective-permute-start | bytes 98312 | tf_op jit(solution)/shard_map/ppermute | solution.py:423
  104.3 4.8 %collective-permute-start.25 = (f32[64,128]{1,0:T(8,128)S(1)}, f32[64,128]{1,0:T(8,128)S(1)}, u32[]{:S(2)}, u32[]{:S(2)}) collective-permute-start(f32[64,128]{1,0:T(8,128)S(1)} %add_add_fusion.3), channel_id=1, source_target_pairs={{0,192},{16,208},{32,224},{48,240},{64,0},{80,16},{96,32},{112,48}... | collective-permute-start | bytes 98312 | tf_op jit(solution)/shard_map/ppermute | solution.py:423
  109.1 5.5 %collective-permute-start.30 = (f32[64,128]{1,0:T(8,128)S(1)}, f32[64,128]{1,0:T(8,128)S(1)}, u32[]{:S(2)}, u32[]{:S(2)}) collective-permute-start(f32[64,128]{1,0:T(8,128)S(1)} %fusion.26.refs_0_), channel_id=1, source_target_pairs={{0,32},{16,48},{32,0},{48,16},{64,96},{80,112},{96,64},{112,80},{1... | collective-permute-start | bytes 98312 | tf_op jit(solution)/shard_map/ppermute | solution.py:418
  110.3 5.1 %collective-permute-start.29 = (f32[64,128]{1,0:T(8,128)S(1)}, f32[64,128]{1,0:T(8,128)S(1)}, u32[]{:S(2)}, u32[]{:S(2)}) collective-permute-start(f32[64,128]{1,0:T(8,128)S(1)} %fusion.26.refs_0_), channel_id=1, source_target_pairs={{0,16},{16,32},{32,48},{48,0},{64,80},{80,96},{96,112},{112,64},{1... | collective-permute-start | bytes 98312 | tf_op jit(solution)/shard_map/ppermute | solution.py:418
  112.7 3.9 %collective-permute-start.28 = (f32[64,128]{1,0:T(8,128)S(1)}, f32[64,128]{1,0:T(8,128)S(1)}, u32[]{:S(2)}, u32[]{:S(2)}) collective-permute-start(f32[64,128]{1,0:T(8,128)S(1)} %fusion.26.refs_0_), channel_id=1, source_target_pairs={{0,48},{16,0},{32,16},{48,32},{64,112},{80,64},{96,80},{112,96},{1... | collective-permute-start | bytes 98312 | tf_op jit(solution)/shard_map/ppermute | solution.py:418
